TPU v7x, 256 devices: a whole 4x4x8 slice. The times are simulated.
256 devices in a mesh: gx: 64 (over z, x, core), gy: 4 (over y).
Axes of the slice: x: 4, y: 4, z: 8, core: 2. Of those that a mesh axis runs over, the one named last changes fastest.
Arguments:
- velocity: float32 [3, 256, 64, 256], P(None, 'gx', 'gy')
- cell_swimmer: int32 [256, 64, 256], P('gx', 'gy'), may hold values from 0 to 15, as said below
- swimmer_speed: float32 [8, 3], replicated, may hold values from -1 to 1
- recentre_cols: int32 [2], replicated, may hold values from 0 to 2, as said below
Outputs:
- velocity_out: float32 [3, 256, 64, 256], P(None, 'gx', 'gy')
- pressure: float32 [256, 64, 256], P('gx', 'gy')
Inputs may be any that keep to these rules, and one draw needn't show every extreme that they name: `cell_swimmer`: values of 8 or more mark fluid cells, smaller ones name the swimmer; the cells of each swimmer lie inside one box of 8 by 8 by 32 cells, periodic along the first and third dimensions. `recentre_cols`: some step recentres by exactly 2 columns.
All inputs are finite; a program needn't handle non-finite values.
Results may differ from a plain program's by a relative error of at most 0.0003.
Values sent between devices are 32-bit elements; how exact they have to be, the bound alone decides.
No kernel may reach another device: no remote copies, remote signals or barrier semaphores. Data moves between devices by JAX's collectives and lax.ppermute only.
A program may use at most 64 MiB of HBM per device.

v0:
```python
import jax
import jax.numpy as jnp
from jax import lax
from jax.sharding import PartitionSpec as P

SWIMMERS = 8
STEPS = 2
PASSES = 8
SMAX = 2


TIME_STEP = 0.1
VISCOSITY = 0.5
PENALTY = 4.0
SCREEN = 0.05


def shifted(value, axis, steps):
    count = lax.axis_size(axis)
    pairs = [(source, (source + steps) % count) for source in range(count)]
    return lax.ppermute(value, axis, pairs)


def padded_2(cells, sides, width, closed):
    for axis, dim in sides:
        count = lax.axis_size(axis)
        ends = count if closed else count - 1
        head = lax.slice_in_dim(cells, 0, width, axis=dim)
        tail = lax.slice_in_dim(cells, cells.shape[dim] - width, cells.shape[dim], axis=dim)
        cells = jnp.concatenate(
            [
                lax.ppermute(tail, axis, [(i, (i + 1) % count) for i in range(ends)]),
                cells,
                lax.ppermute(head, axis, [((i + 1) % count, i) for i in range(ends)]),
            ],
            axis=dim,
        )
    return cells


def pad_walls(padded, width):
    row_count = padded.shape[-2]
    inner_rows = row_count - 2 * width
    global_rows = lax.axis_index("gy") * inner_rows + jnp.arange(row_count, dtype=jnp.int32) - width
    total_rows = inner_rows * lax.axis_size("gy")
    inside = ((global_rows >= 0) & (global_rows < total_rows)).astype(padded.dtype)
    return padded * inside[:, None]


def neighbours(padded):
    centre = padded[..., 1:-1, 1:-1, :]
    x_plus = padded[..., 2:, 1:-1, :]
    x_minus = padded[..., :-2, 1:-1, :]
    y_plus = padded[..., 1:-1, 2:, :]
    y_minus = padded[..., 1:-1, :-2, :]
    z_plus = jnp.roll(centre, -1, axis=-1)
    z_minus = jnp.roll(centre, 1, axis=-1)
    return (centre, x_plus, x_minus, y_plus, y_minus, z_plus, z_minus)


def operate(padded):
    centre, x_plus, x_minus, y_plus, y_minus, z_plus, z_minus = neighbours(padded)
    return (6.0 + SCREEN) * centre - (x_plus + x_minus + y_plus + y_minus + z_plus + z_minus)


def advect(padded):
    centre, x_plus, x_minus, y_plus, y_minus, z_plus, z_minus = neighbours(padded)
    laplace = x_plus + x_minus + y_plus + y_minus + z_plus + z_minus - 6.0 * centre
    transport = (
        centre[0:1] * (x_plus - x_minus) * 0.5
        + centre[1:2] * (y_plus - y_minus) * 0.5
        + centre[2:3] * (z_plus - z_minus) * 0.5
    )
    return centre + TIME_STEP * (VISCOSITY * laplace - transport)


def penalize(velocity, cell_swimmer, swimmer_speed):
    target = jnp.zeros_like(velocity)
    for swimmer in range(SWIMMERS):
        target = (
            target
            + (cell_swimmer == swimmer).astype(jnp.float32)[None]
            * swimmer_speed[swimmer][:, None, None, None]
        )
    solid = (cell_swimmer < SWIMMERS).astype(jnp.float32)[None]
    return (velocity + PENALTY * solid * target) / (1.0 + PENALTY * solid)


def divergence(flux_x, flux_y, flux_z):
    return (
        (flux_x[2:] - flux_x[:-2]) * 0.5
        + (flux_y[:, 2:] - flux_y[:, :-2]) * 0.5
        + (jnp.roll(flux_z, -1, axis=2) - jnp.roll(flux_z, 1, axis=2)) * 0.5
    )


def gradient(padded):
    centre, x_plus, x_minus, y_plus, y_minus, z_plus, z_minus = neighbours(padded)
    return jnp.stack([(x_plus - x_minus) * 0.5, (y_plus - y_minus) * 0.5, (z_plus - z_minus) * 0.5])


def dot_pair(residual, image):
    return lax.psum((jnp.sum(residual * residual), jnp.sum(residual * image)), ("gx", "gy"))


def body(velocity, cell_swimmer, swimmer_speed, recentre_cols):
    width_x = velocity.shape[1]
    pressure = jnp.zeros(velocity.shape[1:], jnp.float32)
    for step_index in range(STEPS):
        offset = recentre_cols[step_index]
        tail_cols = velocity[:, width_x - SMAX :]
        received = shifted(tail_cols, "gx", 1)
        joined = jnp.concatenate([received, velocity], axis=1)
        velocity = lax.dynamic_slice_in_dim(joined, SMAX - offset, width_x, 1)
        padded = pad_walls(padded_2(velocity, (("gx", 1), ("gy", 2)), 1, True), 1)
        velocity = advect(padded)
        velocity = penalize(velocity, cell_swimmer, swimmer_speed)
        flux_x = padded_2(velocity[0], (("gx", 0),), 1, True)
        flux_y = padded_2(velocity[1], (("gy", 1),), 1, False)
        source = -divergence(flux_x, flux_y, velocity[2])
        pressure = jnp.zeros_like(source)
        residual = source
        for pass_index in range(PASSES):
            extended = pad_walls(padded_2(residual, (("gx", 0), ("gy", 1)), 1, True), 1)
            image = operate(extended)
            norm_sq, curvature = dot_pair(residual, image)
            alpha = norm_sq / curvature
            pressure = pressure + alpha * residual
            residual = residual - alpha * image
        padded = pad_walls(padded_2(pressure, (("gx", 0), ("gy", 1)), 1, True), 1)
        velocity = velocity - gradient(padded)
    return (velocity, pressure)


def solution(mesh):
    placed = (P(None, "gx", "gy", None), P("gx", "gy", None), P(), P())
    return jax.shard_map(
        body,
        mesh=mesh,
        in_specs=placed,
        out_specs=(P(None, "gx", "gy", None), P("gx", "gy", None)),
        check_vma=False,
    )
```

profile of v0, /device:TPU:1, one launch (start us, length us, event | category | flops | bytes accessed | tf_op | source)
XLA Modules:
  0.0 1550.9 jit_solution(7095435491239360751)
XLA Ops:
  8.4 4.7 collective-permute-start.2
  19.1 7.1 collective-permute-start.5
  27.5 4.0 collective-permute-start.8
  32.4 4.8 collective-permute-start.10
  44.0 83.9 %all-reduce.15 = (f32[]{:T(128)}, f32[]{:T(128)}) all-reduce(f32[]{:T(128)} %get-tuple-element.33, f32[]{:T(128)} %get-tuple-element.32), channel_id=1, replica_groups=mesh['gx'=64,'gy'=4] {'gx','gy'}, use_global_device_ids=true, to_apply=%region_1.2 | all-reduce | flops 2 | bytes 16 | tf_op jit(solution)/shard_map/psum | solution.py:103
  137.7 81.7 %all-reduce.14 = (f32[]{:T(128)}, f32[]{:T(128)}) all-reduce(f32[]{:T(128)} %get-tuple-element.31, f32[]{:T(128)} %get-tuple-element.30), channel_id=1, replica_groups=mesh['gx'=64,'gy'=4] {'gx','gy'}, use_global_device_ids=true, to_apply=%region_5.6 | all-reduce | flops 2 | bytes 16 | tf_op jit(solution)/shard_map/psum | solution.py:103
  228.9 81.6 %all-reduce.13 = (f32[]{:T(128)}, f32[]{:T(128)}) all-reduce(f32[]{:T(128)} %get-tuple-element.29, f32[]{:T(128)} %get-tuple-element.28), channel_id=1, replica_groups=mesh['gx'=64,'gy'=4] {'gx','gy'}, use_global_device_ids=true, to_apply=%region_9.10 | all-reduce | flops 2 | bytes 16 | tf_op jit(solution)/shard_map/psum | solution.py:103
  320.0 81.6 %all-reduce.12 = (f32[]{:T(128)}, f32[]{:T(128)}) all-reduce(f32[]{:T(128)} %get-tuple-element.27, f32[]{:T(128)} %get-tuple-element.26), channel_id=1, replica_groups=mesh['gx'=64,'gy'=4] {'gx','gy'}, use_global_device_ids=true, to_apply=%region_13.14 | all-reduce | flops 2 | bytes 16 | tf_op jit(solution)/shard_map/psum | solution.py:103
  411.2 81.6 %all-reduce.11 = (f32[]{:T(128)}, f32[]{:T(128)}) all-reduce(f32[]{:T(128)} %get-tuple-element.25, f32[]{:T(128)} %get-tuple-element.24), channel_id=1, replica_groups=mesh['gx'=64,'gy'=4] {'gx','gy'}, use_global_device_ids=true, to_apply=%region_17.18 | all-reduce | flops 2 | bytes 16 | tf_op jit(solution)/shard_map/psum | solution.py:103
  502.3 81.6 %all-reduce.10 = (f32[]{:T(128)}, f32[]{:T(128)}) all-reduce(f32[]{:T(128)} %get-tuple-element.23, f32[]{:T(128)} %get-tuple-element.22), channel_id=1, replica_groups=mesh['gx'=64,'gy'=4] {'gx','gy'}, use_global_device_ids=true, to_apply=%region_21.22 | all-reduce | flops 2 | bytes 16 | tf_op jit(solution)/shard_map/psum | solution.py:103
  593.4 81.6 %all-reduce.9 = (f32[]{:T(128)}, f32[]{:T(128)}) all-reduce(f32[]{:T(128)} %get-tuple-element.21, f32[]{:T(128)} %get-tuple-element.20), channel_id=1, replica_groups=mesh['gx'=64,'gy'=4] {'gx','gy'}, use_global_device_ids=true, to_apply=%region_25.26 | all-reduce | flops 2 | bytes 16 | tf_op jit(solution)/shard_map/psum | solution.py:103
  684.8 81.6 %all-reduce.8 = (f32[]{:T(128)}, f32[]{:T(128)}) all-reduce(f32[]{:T(128)} %get-tuple-element.19, f32[]{:T(128)} %get-tuple-element.18), channel_id=1, replica_groups=mesh['gx'=64,'gy'=4] {'gx','gy'}, use_global_device_ids=true, to_apply=%region_29.30 | all-reduce | flops 2 | bytes 16 | tf_op jit(solution)/shard_map/psum | solution.py:103
  781.7 6.6 collective-permute-start.47
  794.6 6.5 collective-permute-start.50
  802.4 4.0 collective-permute-start.53
  807.5 5.4 collective-permute-start.55
  819.6 82.8 %all-reduce.7 = (f32[]{:T(128)}, f32[]{:T(128)}) all-reduce(f32[]{:T(128)} %get-tuple-element.17, f32[]{:T(128)} %get-tuple-element.16), channel_id=1, replica_groups=mesh['gx'=64,'gy'=4] {'gx','gy'}, use_global_device_ids=true, to_apply=%region_33.34 | all-reduce | flops 2 | bytes 16 | tf_op jit(solution)/shard_map/psum | solution.py:103
  911.9 81.6 %all-reduce.6 = (f32[]{:T(128)}, f32[]{:T(128)}) all-reduce(f32[]{:T(128)} %get-tuple-element.15, f32[]{:T(128)} %get-tuple-element.14), channel_id=1, replica_groups=mesh['gx'=64,'gy'=4] {'gx','gy'}, use_global_device_ids=true, to_apply=%region_37.38 | all-reduce | flops 2 | bytes 16 | tf_op jit(solution)/shard_map/psum | solution.py:103
  1003.0 81.6 %all-reduce.5 = (f32[]{:T(128)}, f32[]{:T(128)}) all-reduce(f32[]{:T(128)} %get-tuple-element.13, f32[]{:T(128)} %get-tuple-element.12), channel_id=1, replica_groups=mesh['gx'=64,'gy'=4] {'gx','gy'}, use_global_device_ids=true, to_apply=%region_41.42 | all-reduce | flops 2 | bytes 16 | tf_op jit(solution)/shard_map/psum | solution.py:103
  1094.4 81.6 %all-reduce.4 = (f32[]{:T(128)}, f32[]{:T(128)}) all-reduce(f32[]{:T(128)} %get-tuple-element.11, f32[]{:T(128)} %get-tuple-element.10), channel_id=1, replica_groups=mesh['gx'=64,'gy'=4] {'gx','gy'}, use_global_device_ids=true, to_apply=%region_45.46 | all-reduce | flops 2 | bytes 16 | tf_op jit(solution)/shard_map/psum | solution.py:103
  1185.5 81.6 %all-reduce.3 = (f32[]{:T(128)}, f32[]{:T(128)}) all-reduce(f32[]{:T(128)} %get-tuple-element.9, f32[]{:T(128)} %get-tuple-element.8), channel_id=1, replica_groups=mesh['gx'=64,'gy'=4] {'gx','gy'}, use_global_device_ids=true, to_apply=%region_49.50 | all-reduce | flops 2 | bytes 16 | tf_op jit(solution)/shard_map/psum | solution.py:103
  1276.6 81.6 %all-reduce.2 = (f32[]{:T(128)}, f32[]{:T(128)}) all-reduce(f32[]{:T(128)} %get-tuple-element.7, f32[]{:T(128)} %get-tuple-element.6), channel_id=1, replica_groups=mesh['gx'=64,'gy'=4] {'gx','gy'}, use_global_device_ids=true, to_apply=%region_53.54 | all-reduce | flops 2 | bytes 16 | tf_op jit(solution)/shard_map/psum | solution.py:103
  1367.9 81.7 %all-reduce.1 = (f32[]{:T(128)}, f32[]{:T(128)}) all-reduce(f32[]{:T(128)} %get-tuple-element.5, f32[]{:T(128)} %get-tuple-element.4), channel_id=1, replica_groups=mesh['gx'=64,'gy'=4] {'gx','gy'}, use_global_device_ids=true, to_apply=%region_57.58 | all-reduce | flops 2 | bytes 16 | tf_op jit(solution)/shard_map/psum | solution.py:103
  1459.1 81.6 %all-reduce = (f32[]{:T(128)}, f32[]{:T(128)}) all-reduce(f32[]{:T(128)} %get-tuple-element.3, f32[]{:T(128)} %get-tuple-element.2), channel_id=1, replica_groups=mesh['gx'=64,'gy'=4] {'gx','gy'}, use_global_device_ids=true, to_apply=%region_61.62 | all-reduce | flops 2 | bytes 16 | tf_op jit(solution)/shard_map/psum | solution.py:103
  (345 shorter events, 172.8 us)
Async XLA Ops:
  1.6 5.2 collective-permute-start
  6.8 6.9 collective-permute-start.1
  8.4 5.6 collective-permute-start.2
  14.0 4.0 collective-permute-start.3
  19.1 13.1 collective-permute-start.5
  26.2 6.1 collective-permute-start.6
  26.2 5.5 collective-permute-start.7
  27.5 4.7 collective-permute-start.8
  32.3 5.5 collective-permute-start.9
  32.4 5.7 collective-permute-start.10
  38.1 4.8 collective-permute-start.11
  775.4 6.2 collective-permute-start.45
  781.7 7.4 collective-permute-start.46
  781.7 7.5 collective-permute-start.47
  789.3 4.5 collective-permute-start.48
  789.4 4.4 collective-permute-start.49
  794.6 12.6 collective-permute-start.50
  801.1 6.1 collective-permute-start.51
  801.1 5.5 collective-permute-start.52
  802.4 4.7 collective-permute-start.53
  807.3 6.3 collective-permute-start.54
  807.5 6.2 collective-permute-start.55
  813.8 4.8 collective-permute-start.56
  907.1 3.9 collective-permute-start.60
  (71 other events, 219.8 us)
where the time goes:
time: 1570 us; the launch traced here: 1550 us
  blocking collectives  1310 us (83%)
  starting transfers between devices  129 us (8%)
  waiting for transfers between devices  64.6 us (4%)
  between operations  25.4 us (2%)
  other arithmetic  16 us (1%)
    psum x16, blocking collectives, dot_pair(): lax.psum((jnp.sum(residual * residual), jnp.sum(residual * image)), ('gx'...  1310 us
    ppermute x44, starting transfers between devices, padded_2(): lax.ppermute(head, axis, [((i + 1) % count, i) for i in range(ends)])  99.4 us
    ppermute x44, waiting for transfers between devices, padded_2(): lax.ppermute(tail, axis, [(i, (i + 1) % count) for i in range(ends)])  33.3 us
  transfers between devices with their start and end apart: 90, of which 64 were waited for; matrix products, arithmetic and copies ran while one was open for 0% of the time, Pallas kernels for 0%

commit v1 on v0

--- a/solution.py
+++ b/solution.py
@@ -1,6 +1,11 @@
+import functools
+
 import jax
 import jax.numpy as jnp
+import numpy as np
 from jax import lax
+from jax.experimental import pallas as pl
+from jax.experimental.pallas import tpu as pltpu
 from jax.sharding import PartitionSpec as P
 
 SWIMMERS = 8
@@ -8,11 +13,16 @@
 PASSES = 8
 SMAX = 2
 
-
 TIME_STEP = 0.1
 VISCOSITY = 0.5
 PENALTY = 4.0
 SCREEN = 0.05
+
+AXES = ("gx", "gy")
+NODES = 16
+NZ = 256
+DEPTH = 8
+NOISE = 1e-4
 
 
 def shifted(value, axis, steps):
@@ -99,14 +109,19 @@
     return jnp.stack([(x_plus - x_minus) * 0.5, (y_plus - y_minus) * 0.5, (z_plus - z_minus) * 0.5])
 
 
-def dot_pair(residual, image):
-    return lax.psum((jnp.sum(residual * residual), jnp.sum(residual * image)), ("gx", "gy"))
-
-
-def body(velocity, cell_swimmer, swimmer_speed, recentre_cols):
+def plain(velocity, cell_swimmer, swimmer_speed, recentre_cols):
     width_x = velocity.shape[1]
-    pressure = jnp.zeros(velocity.shape[1:], jnp.float32)
-    for step_index in range(STEPS):
+
+    def search(_, state):
+        pressure, residual = state
+        extended = pad_walls(padded_2(residual, (("gx", 0), ("gy", 1)), 1, True), 1)
+        image = operate(extended)
+        norm_sq, curvature = lax.psum((jnp.sum(residual * residual), jnp.sum(residual * image)), AXES)
+        alpha = norm_sq / curvature
+        return (pressure + alpha * residual, residual - alpha * image)
+
+    def step(step_index, state):
+        velocity, _ = state
         offset = recentre_cols[step_index]
         tail_cols = velocity[:, width_x - SMAX :]
         received = shifted(tail_cols, "gx", 1)
@@ -118,24 +133,403 @@
         flux_x = padded_2(velocity[0], (("gx", 0),), 1, True)
         flux_y = padded_2(velocity[1], (("gy", 1),), 1, False)
         source = -divergence(flux_x, flux_y, velocity[2])
-        pressure = jnp.zeros_like(source)
-        residual = source
-        for pass_index in range(PASSES):
-            extended = pad_walls(padded_2(residual, (("gx", 0), ("gy", 1)), 1, True), 1)
-            image = operate(extended)
-            norm_sq, curvature = dot_pair(residual, image)
-            alpha = norm_sq / curvature
-            pressure = pressure + alpha * residual
-            residual = residual - alpha * image
+        pressure, _ = lax.fori_loop(0, PASSES, search, (jnp.zeros_like(source), source))
         padded = pad_walls(padded_2(pressure, (("gx", 0), ("gy", 1)), 1, True), 1)
-        velocity = velocity - gradient(padded)
-    return (velocity, pressure)
+        return (velocity - gradient(padded), pressure)
+
+    start = (velocity, jnp.zeros(velocity.shape[1:], jnp.float32))
+    return lax.fori_loop(0, STEPS, step, start)
+
+
+def tables():
+    angle = (np.arange(NODES) + 0.5) * np.pi / NODES
+    cheb = np.cos(np.outer(np.arange(NODES), angle))
+    moment = np.zeros((NODES, NODES))
+    moment[0, 0] = moment[1, 1] = 1.0
+    for i in range(1, NODES // 2):
+        moment[2 * i, 2 * i], moment[2 * i, 0] = 2.0, -1.0
+        moment[2 * i + 1, 2 * i + 1], moment[2 * i + 1, 1] = 2.0, -1.0
+    scale = np.full((NODES, 1), 2.0 / NODES)
+    scale[0] = 1.0 / NODES
+    weight = cheb.T @ (scale * moment)
+    weight_map = np.zeros((NODES, 128))
+    weight_map[:, :NODES] = weight
+    node = (6.0 + SCREEN) - 6.0 * np.cos(angle)
+    node = np.broadcast_to(node[:, None], (NODES, NZ))
+    coef = np.broadcast_to((scale * cheb)[:PASSES, :, None], (PASSES, NODES, NZ))
+    return [np.ascontiguousarray(a, dtype=np.float32) for a in (weight_map, node, coef)]
+
+
+def z_next(a):
+    return pltpu.roll(a, NZ - 1, a.ndim - 1)
+
+
+def z_prev(a):
+    return pltpu.roll(a, 1, a.ndim - 1)
+
+
+def y_next(a):
+    return pltpu.roll(a, a.shape[0] - 1, 0)
+
+
+def y_prev(a):
+    return pltpu.roll(a, 1, 0)
+
+
+def window_kernel(info, own, left, right, win, to_core, to_chip):
+    core, offset = info[0], info[1]
+    joined = 2 - offset
+
+    def plane(i, _):
+        j = i + joined
+        for c in range(3):
+
+            def put(row):
+                win[c, i] = row
+                top, bottom = row[0:2], row[6:8]
+                to_core[c, i] = jnp.where(core == 0, bottom, top)
+                to_chip[c, i] = jnp.where(core == 0, top, bottom)
+
+            @pl.when(j < 4)
+            def _():
+                put(left[c, j])
+
+            @pl.when((j >= 4) & (j < 12))
+            def _():
+                put(own[c, j - 4])
+
+            @pl.when(j >= 12)
+            def _():
+                put(right[c, j - 12])
+
+        return 0
+
+    lax.fori_loop(0, 12, plane, 0)
+
+
+def source_kernel(info, flags, speed, win, from_core, from_chip, cell, cell_core, cell_chip, bodied, source, pad, body):
+    core = info[0]
+    rows = lax.broadcasted_iota(jnp.int32, (24, NZ), 0)
+    inside = jnp.where(rows < 8, flags[0], jnp.where(rows < 16, 1.0, flags[1]))
+
+    def fill(i, _):
+        for c in range(3):
+            pad[c, i, 8:16] = win[c, i]
+            a, b = from_core[c, i], from_chip[c, i]
+            pad[c, i, 6:8] = jnp.where(core == 0, b, a)
+            pad[c, i, 16:18] = jnp.where(core == 0, a, b)
+        return 0
+
+    lax.fori_loop(0, 12, fill, 0)
+
+    def move(i, _):
+        a, b = cell_core[i], cell_chip[i]
+        up = jnp.where(core == 0, b, a)
+        down = jnp.where(core == 0, a, b)
+        ids = jnp.concatenate(
+            [jnp.broadcast_to(up, (8, NZ)), cell[i], jnp.broadcast_to(down, (8, NZ))], axis=0
+        )
+        centre = [pad[c, i + 1] for c in range(3)]
+        solid = ids < SWIMMERS
+        factor = jnp.where(solid, 1.0 / (1.0 + PENALTY), 1.0) * inside
+        for c in range(3):
+            x_plus, x_minus = pad[c, i + 2], pad[c, i]
+            y_plus, y_minus = y_next(centre[c]), y_prev(centre[c])
+            z_plus, z_minus = z_next(centre[c]), z_prev(centre[c])
+            laplace = x_plus + x_minus + y_plus + y_minus + z_plus + z_minus - 6.0 * centre[c]
+            transport = (
+                centre[0] * (x_plus - x_minus)
+                + centre[1] * (y_plus - y_minus)
+                + centre[2] * (z_plus - z_minus)
+            )
+            moved = centre[c] + (TIME_STEP * VISCOSITY) * laplace - (TIME_STEP * 0.5) * transport
+            target = jnp.zeros((24, NZ), jnp.float32)
+            for swimmer in range(SWIMMERS):
+                target = jnp.where(ids == swimmer, speed[swimmer, c], target)
+            body[c, i] = (moved + PENALTY * target) * factor
+        return 0
+
+    lax.fori_loop(0, 10, move, 0)
+
+    def diverge(i, _):
+        along_x = body[0, i + 2, 8:16] - body[0, i, 8:16]
+        b1 = body[1, i + 1]
+        along_y = (y_next(b1) - y_prev(b1))[8:16]
+        b2 = body[2, i + 1, 8:16]
+        source[i] = -0.5 * (along_x + along_y + z_next(b2) - z_prev(b2))
+        for c in range(3):
+            bodied[c, i] = body[c, i + 1, 8:16]
+        return 0
+
+    lax.fori_loop(0, 8, diverge, 0)
+
+
+def powers_kernel(info, flags, own, left, right, from_core, from_chip, moments, near, t):
+    core = info[0]
+    rows = lax.broadcasted_iota(jnp.int32, (24, NZ), 0)
+    inside = jnp.where(rows < 8, flags[0], jnp.where(rows < 16, 1.0, flags[1]))
+    twice = inside * (1.0 / 3.0)
+    once = inside * (1.0 / 6.0)
+
+    def fill(i, _):
+        a, b = from_core[i], from_chip[i]
+        t[0, i, 0:8] = jnp.where(core == 0, b, a)
+        t[0, i, 16:24] = jnp.where(core == 0, a, b)
+        return 0
+
+    lax.fori_loop(0, 24, fill, 0)
+    for i in range(8):
+        t[0, i, 8:16] = left[i]
+        t[0, i + 8, 8:16] = own[i]
+        t[0, i + 16, 8:16] = right[i]
+
+    for j in range(1, PASSES + 1):
+
+        def level(i, _, j=j):
+            centre = t[j - 1, i]
+            total = (
+                t[j - 1, i - 1]
+                + t[j - 1, i + 1]
+                + (y_next(centre) + y_prev(centre))
+                + (z_next(centre) + z_prev(centre))
+            )
+            if j == 1:
+                t[j, i] = once * total
+            else:
+                t[j, i] = twice * total - t[j - 2, i]
+            return 0
+
+        lax.fori_loop(j, 24 - j, level, 0, unroll=2)
+
+    def product(i, sums):
+        values = [t[j, i, 8:16] for j in range(PASSES + 1)]
+        out = []
+        for j in range(PASSES):
+            for k in (j, j + 1):
+                both = values[j] * values[k]
+                out.append(sums[2 * j + k - j] + (both[:, :128] + both[:, 128:]))
+        return tuple(out)
+
+    zero = jnp.zeros((8, 128), jnp.float32)
+    sums = lax.fori_loop(DEPTH, 2 * DEPTH, product, (zero,) * NODES)
+    lines = [jnp.sum(a, axis=0, keepdims=True) for a in sums]
+    block = jnp.concatenate(lines + [jnp.zeros((128 - NODES, 128), jnp.float32)], axis=0)
+    line = jnp.sum(block.T, axis=0, keepdims=True)
+    moments[...] = jnp.broadcast_to(line, moments.shape)
+
+    def keep(i, _):
+        for j in range(PASSES):
+            near[j, i] = t[j, i + DEPTH - 1]
+        return 0
+
+    lax.fori_loop(0, 10, keep, 0)
+
+
+def lengths(moments, weight_map, node, coef):
+    line = jnp.sum(moments[...], axis=0, keepdims=True)
+    weight = jnp.sum(weight_map[...] * line, axis=1, keepdims=True)
+    weight = jnp.broadcast_to(weight, (NODES, NZ))
+    first = jnp.sum(weight, axis=0, keepdims=True)
+    value = node[...]
+    residual = jnp.ones((NODES, NZ), jnp.float32)
+    search = jnp.zeros((NODES, NZ), jnp.float32)
+    good = jnp.ones((1, NZ), jnp.float32)
+    for _ in range(PASSES):
+        square = residual * residual
+        norm_sq = jnp.sum(weight * square, axis=0, keepdims=True)
+        curvature = jnp.sum(weight * square * value, axis=0, keepdims=True)
+        noise = NOISE * first * jnp.sum(square, axis=0, keepdims=True)
+        noise_image = NOISE * first * jnp.sum(square * value, axis=0, keepdims=True)
+        good = jnp.where((norm_sq > noise) & (curvature > noise_image), good, 0.0)
+        alpha = norm_sq / curvature
+        search = search + alpha * residual
+        residual = residual - alpha * value * residual
+    terms = [jnp.sum(coef[j] * search, axis=0, keepdims=True) for j in range(PASSES)]
+    return terms, good
+
+
+def correct(terms, near, bodied, emit, p):
+    def combine(i, _):
+        total = terms[0] * near[0, i]
+        for j in range(1, PASSES):
+            total = total + terms[j] * near[j, i]
+        p[i] = total
+        return 0
+
+    lax.fori_loop(0, 10, combine, 0)
+
+    def apply(i, _):
+        centre = p[i + 1]
+        own = centre[8:16]
+        emit(
+            i,
+            bodied[0, i] - 0.5 * (p[i + 2, 8:16] - p[i, 8:16]),
+            bodied[1, i] - 0.5 * (y_next(centre) - y_prev(centre))[8:16],
+            bodied[2, i] - 0.5 * (z_next(own) - z_prev(own)),
+            own,
+        )
+        return 0
+
+    lax.fori_loop(0, 8, apply, 0)
+
+
+def inner_step_kernel(moments, weight_map, node, coef, near, bodied, good_out, velocity, p):
+    terms, good = lengths(moments, weight_map, node, coef)
+    good_out[...] = good
+
+    def emit(i, a, b, c, _):
+        velocity[0, i] = a
+        velocity[1, i] = b
+        velocity[2, i] = c
+
+    correct(terms, near, bodied, emit, p)
+
+
+def last_step_kernel(info, moments, weight_map, node, coef, near, bodied, good_out, kept, sent, p, fields):
+    terms, good = lengths(moments, weight_map, node, coef)
+    good_out[...] = good
+    core = info[0]
+
+    def emit(i, *values):
+        for c in range(4):
+            fields[c, i] = values[c]
+
+    correct(terms, near, bodied, emit, p)
+    for i in range(4):
+        for c in range(4):
+            kept[c, i] = fields[c, 4 * core + i]
+            sent[c, i] = fields[c, 4 * (1 - core) + i]
+
+
+SMEM = pl.BlockSpec(memory_space=pltpu.SMEM)
+VMEM = pl.BlockSpec(memory_space=pltpu.VMEM)
+
+
+def call(kernel, args, smem, outs, scratch, flops=1_000_000):
+    return pl.pallas_call(
+        kernel,
+        in_specs=[SMEM] * smem + [VMEM] * (len(args) - smem),
+        out_specs=[VMEM] * len(outs),
+        out_shape=[jax.ShapeDtypeStruct(s, jnp.float32) for s in outs],
+        scratch_shapes=[pltpu.VMEM(s, jnp.float32) for s in scratch],
+        compiler_params=pltpu.CompilerParams(vmem_limit_bytes=24 * 1024 * 1024),
+        cost_estimate=pl.CostEstimate(flops=flops, bytes_accessed=1_000_000, transcendentals=0),
+    )(*args)
+
+
+def routes(count_x, count_y):
+    chips = count_x // 2
+
+    def pairs(target):
+        out = []
+        for chip in range(chips):
+            for core in range(2):
+                for y in range(count_y):
+                    to = target(chip, core, y)
+                    if to is not None:
+                        source = (2 * chip + core) * count_y + y
+                        out.append((source, (2 * (to[0] % chips) + to[1]) * count_y + to[2]))
+        return out
+
+    def across(chip, core, y):
+        row = y + (1 if core else -1)
+        return (chip, 1 - core, row) if 0 <= row < count_y else None
+
+    return {
+        "core": pairs(lambda chip, core, y: (chip, 1 - core, y)),
+        "facing": pairs(lambda chip, core, y: (chip + (1 if core else -1), 1 - core, y)),
+        "right": pairs(lambda chip, core, y: (chip + 1, core, y)),
+        "left": pairs(lambda chip, core, y: (chip - 1, core, y)),
+        "across": pairs(across),
+    }
+
+
+def body(velocity, cell_swimmer, swimmer_speed, recentre_cols, *, count_x, count_y):
+    route = routes(count_x, count_y)
+    send = lambda value, name: lax.ppermute(value, AXES, route[name])
+    core = lax.axis_index("gx") % 2
+    y = lax.axis_index("gy")
+    flags = jnp.stack([(y > 0) | (core == 1), (y < count_y - 1) | (core == 0)]).astype(jnp.float32)
+    weight_map, node, coef = (jnp.asarray(a) for a in tables())
+    first = core == 0
+
+    cells = cell_swimmer.astype(jnp.float32)
+    edge_cells = jnp.where(first, cells[0:1], cells[3:4])
+    beside = send(jnp.concatenate([velocity.reshape(12, 16, NZ), edge_cells], axis=0), "facing")
+    chunk = jnp.concatenate([velocity.reshape(12, 16, NZ), cells, beside], axis=0)
+    mine = jnp.where(first, chunk[:, 0:8], chunk[:, 8:16])
+    theirs = send(jnp.where(first, chunk[:, 8:16], chunk[:, 0:8]), "core")
+    low = jnp.where(first, mine, theirs)
+    high = jnp.where(first, theirs, mine)
+    own = jnp.concatenate([low[0:12].reshape(3, 4, 8, NZ), high[0:12].reshape(3, 4, 8, NZ)], axis=1)
+    left = low[16:28].reshape(3, 4, 8, NZ)
+    right = high[16:28].reshape(3, 4, 8, NZ)[:, 0:2]
+    cell = jnp.concatenate([low[28:29], low[12:16], high[12:16], high[28:29]], axis=0)
+    cell_edge = cell[:, 0:1], cell[:, 7:8]
+    cell_core = send(jnp.where(first, cell_edge[1], cell_edge[0]), "core")
+    cell_chip = send(jnp.where(first, cell_edge[0], cell_edge[1]), "across")
+
+    goods = []
+    for step in range(STEPS):
+        info = jnp.stack([core, recentre_cols[step]]).astype(jnp.int32)
+        if step:
+            left = send(own[:, 4:8], "right")
+            right = send(own[:, 0:2], "left")
+        win, to_core, to_chip = call(
+            window_kernel,
+            (info, own, left, right),
+            1,
+            [(3, 12, 8, NZ), (3, 12, 2, NZ), (3, 12, 2, NZ)],
+            [],
+        )
+        bodied, source = call(
+            source_kernel,
+            (info, flags, swimmer_speed, win, send(to_core, "core"), send(to_chip, "across"), cell, cell_core, cell_chip),
+            3,
+            [(3, 8, 8, NZ), (8, 8, NZ)],
+            [(3, 12, 24, NZ), (3, 10, 24, NZ)],
+        )
+        s_left = send(source, "right")
+        s_right = send(source, "left")
+        column = jnp.concatenate([s_left, source, s_right], axis=0)
+        moments, near = call(
+            powers_kernel,
+            (info, flags, source, s_left, s_right, send(column, "core"), send(column, "across")),
+            2,
+            [(count_x * count_y, 128), (PASSES, 10, 24, NZ)],
+            [(PASSES + 1, 24, 24, NZ)],
+        )
+        moments = lax.all_to_all(moments, AXES, 0, 0)
+        shared = (moments, weight_map, node, coef, near, bodied)
+        if step < STEPS - 1:
+            good, own = call(
+                inner_step_kernel, shared, 0, [(1, NZ), (3, 8, 8, NZ)], [(10, 24, NZ)]
+            )
+        else:
+            good, kept, sent = call(
+                last_step_kernel,
+                (info,) + shared,
+                1,
+                [(1, NZ), (4, 4, 8, NZ), (4, 4, 8, NZ)],
+                [(10, 24, NZ), (4, 8, 8, NZ)],
+            )
+        goods.append(good[0, 0])
+
+    def finish(_):
+        got = send(sent, "core")
+        fields = jnp.concatenate([jnp.where(first, kept, got), jnp.where(first, got, kept)], axis=2)
+        return (fields[0:3], fields[3])
+
+    def again(_):
+        return plain(velocity, cell_swimmer, swimmer_speed, recentre_cols)
+
+    return lax.cond(goods[0] * goods[1] > 0.5, finish, again, None)
 
 
 def solution(mesh):
     placed = (P(None, "gx", "gy", None), P("gx", "gy", None), P(), P())
     return jax.shard_map(
-        body,
+        functools.partial(body, count_x=mesh.shape["gx"], count_y=mesh.shape["gy"]),
         mesh=mesh,
         in_specs=placed,
         out_specs=(P(None, "gx", "gy", None), P("gx", "gy", None)),

time: 1570 us -> 147 us (0.09); the launches traced: 1550 us -> 147 us
  blocking collectives: 1310 us -> 24.3 us
  starting transfers between devices: 129 us -> 50.2 us
  waiting for transfers between devices: 64.6 us -> 38.2 us
  Pallas kernels: 0 us -> 25 us
  between operations: 25.4 us -> 2.2 us
    psum x16 -> x0, blocking collectives: 1310 us -> none  [dot_pair(): lax.psum((jnp.sum(residual * residual), jnp.sum(residual * image)), ('gx'...]
    ppermute x90 -> x19, starting transfers between devices: 129 us -> 40.6 us  [body(): send = lambda value, name: lax.ppermute(value, AXES, route[name])]
    ppermute x90 -> x19, waiting for transfers between devices: 64.6 us -> 26.1 us  [body(): send = lambda value, name: lax.ppermute(value, AXES, route[name])]
    pallas_call x0 -> x8, Pallas kernels: none -> 25 us  [call(): pl.pallas_call(kernel, in_specs=[SMEM] * smem + [VMEM] * (len(args) - sme...]
    all_to_all x0 -> x1, blocking collectives: none -> 24.3 us  [body(): moments = lax.all_to_all(moments, AXES, 0, 0)]
  transfers between devices with their start and end apart: 90 -> 20, of which waited for: 64 -> 11; matrix products, arithmetic and copies ran while one was open for 0% -> 2% of each run, Pallas kernels for 0% -> 1%
where the time goes in v1:
time: 147 us
  starting transfers between devices  50.2 us (34%)
  waiting for transfers between devices  38.2 us (26%)
  Pallas kernels  25 us (17%)
  blocking collectives  24.3 us (17%)
  other arithmetic  3.93 us (3%)
  local copies, waits for them, and re-layouts  2.75 us (2%)
  between operations  2.2 us (1%)
    ppermute x19, starting transfers between devices, body(): send = lambda value, name: lax.ppermute(value, AXES, route[name])  40.6 us
    ppermute x19, waiting for transfers between devices, body(): send = lambda value, name: lax.ppermute(value, AXES, route[name])  26.1 us
    pallas_call x8, Pallas kernels, call(): pl.pallas_call(kernel, in_specs=[SMEM] * smem + [VMEM] * (len(args) - sme...  25 us
    all_to_all x1, blocking collectives, body(): moments = lax.all_to_all(moments, AXES, 0, 0)  24.3 us
    all_to_all x1, waiting for transfers between devices, body(): moments = lax.all_to_all(moments, AXES, 0, 0)  12.2 us
    all_to_all x1, starting transfers between devices, body(): moments = lax.all_to_all(moments, AXES, 0, 0)  9.59 us
  transfers between devices with their start and end apart: 20, of which 11 were waited for; matrix products, arithmetic and copies ran while one was open for 2% of the time, Pallas kernels for 1%

profile of v1, /device:TPU:1, one launch (start us, length us, event | category | flops | bytes accessed | tf_op | source)
XLA Modules:
  0.0 146.9 jit_solution(10240736783159299775)
XLA Ops:
  2.5 2.7 %collective-permute-start.18 = (f32[13,16,256]{2,1,0:T(8,128)S(1)}, f32[13,16,256]{2,1,0:T(8,128)S(1)}, u32[]{:S(2)}, u32[]{:S(2)}) collective-permute-start(f32[13,16,256]{2,1,0:T(8,128)S(1)} %pad_maximum_fusion.11), channel_id=1, source_target_pairs={{0,252},{1,253},{2,254},{3,255},{4,8},{5,9},{6,10},{7,11},{8,4},{9... | collective-permute-start | bytes 638984 | tf_op jit(solution)/shard_map/ppermute | solution.py:449
  5.2 3.5 %collective-permute-done.18 = f32[13,16,256]{2,1,0:T(8,128)S(1)} collective-permute-done((f32[13,16,256]{2,1,0:T(8,128)S(1)}, f32[13,16,256]{2,1,0:T(8,128)S(1)}, u32[]{:S(2)}, u32[]{:S(2)}) %collective-permute-start.18) | collective-permute-done | bytes 213024 | tf_op jit(solution)/shard_map/ppermute | solution.py:449
  8.8 6.5 %collective-permute-start.19 = (f32[29,8,256]{2,1,0:T(8,128)S(1)}, f32[29,8,256]{2,1,0:T(8,128)S(1)}, u32[]{:S(2)}, u32[]{:S(2)}) collective-permute-start(f32[29,8,256]{2,1,0:T(8,128)S(1)} %slice_select_fusion), channel_id=1, source_target_pairs={{0,4},{1,5},{2,6},{3,7},{4,0},{5,1},{6,2},{7,3},{8,12},{9,13},{10,... | collective-permute-start | bytes 712712 | tf_op jit(solution)/shard_map/ppermute | solution.py:449
  16.8 3.3 %collective-permute-start.23 = (f32[10,1,256]{2,1,0:T(1,128)S(1)}, f32[10,1,256]{2,1,0:T(1,128)S(1)}, u32[]{:S(2)}, u32[]{:S(2)}) collective-permute-start(f32[10,1,256]{2,1,0:T(1,128)S(1)} %get-tuple-element.366), channel_id=1, source_target_pairs={{1,4},{2,5},{3,6},{4,1},{5,2},{6,3},{9,12},{10,13},{11,14},{12,9},... | collective-permute-start | bytes 30728 | tf_op jit(solution)/shard_map/ppermute | solution.py:449
  22.1 3.1 %collective-permute-start.21 = (f32[3,12,2,256]{3,2,1,0:T(2,128)S(1)}, f32[3,12,2,256]{3,2,1,0:T(2,128)S(1)}, u32[]{:S(2)}, u32[]{:S(2)}) collective-permute-start(f32[3,12,2,256]{3,2,1,0:T(2,128)S(1)} %get-tuple-element.214), channel_id=1, source_target_pairs={{1,4},{2,5},{3,6},{4,1},{5,2},{6,3},{9,12},{10,13},{11,14},{12,9},... | collective-permute-start | bytes 221192 | tf_op jit(solution)/shard_map/ppermute | solution.py:449
  25.3 2.4 %collective-permute-done.21.from_chip = f32[3,12,2,256]{3,2,1,0:T(2,128)S(1)} collective-permute-done((f32[3,12,2,256]{3,2,1,0:T(2,128)S(1)}, f32[3,12,2,256]{3,2,1,0:T(2,128)S(1)}, u32[]{:S(2)}, u32[]{:S(2)}) %collective-permute-start.21) | collective-permute-done | bytes 73760 | tf_op jit(solution)/shard_map/ppermute | solution.py:449
  27.7 2.6 %shard_map.87 = (f32[3,8,8,256]{3,2,1,0:T(8,128)S(1)}, f32[8,8,256]{2,1,0:T(8,128)S(1)}) custom-call(s32[2]{0:T(128)S(1)} %pad_add_fusion.info, f32[2]{0:T(128)S(1)} %add_convert_fusion.flags, f32[8,3]{1,0:T(8,128)S(1)} %copy.21.speed, f32[3,12,8,256]{3,2,1,0:T(8,128)S(1)} %get-tuple-element.212.win, ...), custom_call_target="tpu_custom_call" | custom-call | flops 1000000 | bytes 1000000 | tf_op jit(solution)/shard_map/pallas_call | solution.py:409
  30.4 5.0 %collective-permute-start.25 = (f32[8,8,256]{2,1,0:T(8,128)S(1)}, f32[8,8,256]{2,1,0:T(8,128)S(1)}, u32[]{:S(2)}, u32[]{:S(2)}) collective-permute-start(f32[8,8,256]{2,1,0:T(8,128)S(1)} %get-tuple-element.215.own), channel_id=1, source_target_pairs={{0,248},{1,249},{2,250},{3,251},{4,252},{5,253},{6,254},{7,255},{8... | collective-permute-start | bytes 196616 | tf_op jit(solution)/shard_map/ppermute | solution.py:449
  37.0 4.5 %collective-permute-start.27 = (f32[24,8,256]{2,1,0:T(8,128)S(1)}, f32[24,8,256]{2,1,0:T(8,128)S(1)}, u32[]{:S(2)}, u32[]{:S(2)}) collective-permute-start(f32[24,8,256]{2,1,0:T(8,128)S(1)} %constant_dynamic-update-slice_fusion.6), channel_id=1, source_target_pairs={{1,4},{2,5},{3,6},{4,1},{5,2},{6,3},{9,12},{10,13},{11,14},{12,9},... | collective-permute-start | bytes 589832 | tf_op jit(solution)/shard_map/ppermute | solution.py:449
  41.6 3.2 %collective-permute-done.27.from_chip = f32[24,8,256]{2,1,0:T(8,128)S(1)} collective-permute-done((f32[24,8,256]{2,1,0:T(8,128)S(1)}, f32[24,8,256]{2,1,0:T(8,128)S(1)}, u32[]{:S(2)}, u32[]{:S(2)}) %collective-permute-start.27) | collective-permute-done | bytes 196640 | tf_op jit(solution)/shard_map/ppermute | solution.py:449
  44.9 7.0 %shard_map.88 = (f32[256,128]{1,0:T(8,128)S(1)}, f32[8,10,24,256]{3,2,1,0:T(8,128)S(1)}) custom-call(s32[2]{0:T(128)S(1)} %pad_add_fusion.info, f32[2]{0:T(128)S(1)} %add_convert_fusion.flags, f32[8,8,256]{2,1,0:T(8,128)S(1)} %get-tuple-element.215.own, f32[8,8,256]{2,1,0:T(8,128)S(1)} %collective-permute-done.24.left, ...), custom_call_target="tpu_custom_call" | custom-call | flops 1000000 | bytes 1000000 | tf_op jit(solution)/shard_map/pallas_call | solution.py:409
  51.8 24.3 %all_to_all.22 = f32[256,1,128]{2,1,0:T(1,128)S(1)} all-to-all(f32[256,1,128]{2,1,0:T(1,128)S(1)} %bitcast.86), channel_id=1, replica_groups=mesh['gx'=64,'gy'=4] {'gx','gy'}, dimensions={0} | all-to-all | bytes 262144 | tf_op jit(solution)/shard_map/all_to_all | solution.py:502
  80.3 4.4 %collective-permute-done.28.left = f32[3,4,8,256]{3,2,1,0:T(8,128)S(1)} collective-permute-done((f32[3,4,8,256]{3,2,1,0:T(8,128)S(1)}, f32[3,4,8,256]{3,2,1,0:T(8,128)S(1)}, u32[]{:S(2)}, u32[]{:S(2)}) %collective-permute-start.28) | collective-permute-done | bytes 98336 | tf_op jit(solution)/shard_map/ppermute | solution.py:449
  85.9 2.6 %collective-permute-start.30 = (f32[3,12,2,256]{3,2,1,0:T(2,128)S(1)}, f32[3,12,2,256]{3,2,1,0:T(2,128)S(1)}, u32[]{:S(2)}, u32[]{:S(2)}) collective-permute-start(f32[3,12,2,256]{3,2,1,0:T(2,128)S(1)} %get-tuple-element.222), channel_id=1, source_target_pairs={{0,4},{1,5},{2,6},{3,7},{4,0},{5,1},{6,2},{7,3},{8,12},{9,13},{10,... | collective-permute-start | bytes 221192 | tf_op jit(solution)/shard_map/ppermute | solution.py:449
  88.4 1.9 %collective-permute-start.31 = (f32[3,12,2,256]{3,2,1,0:T(2,128)S(1)}, f32[3,12,2,256]{3,2,1,0:T(2,128)S(1)}, u32[]{:S(2)}, u32[]{:S(2)}) collective-permute-start(f32[3,12,2,256]{3,2,1,0:T(2,128)S(1)} %get-tuple-element.223), channel_id=1, source_target_pairs={{1,4},{2,5},{3,6},{4,1},{5,2},{6,3},{9,12},{10,13},{11,14},{12,9},... | collective-permute-start | bytes 221192 | tf_op jit(solution)/shard_map/ppermute | solution.py:449
  90.4 3.7 %collective-permute-done.31.from_chip = f32[3,12,2,256]{3,2,1,0:T(2,128)S(1)} collective-permute-done((f32[3,12,2,256]{3,2,1,0:T(2,128)S(1)}, f32[3,12,2,256]{3,2,1,0:T(2,128)S(1)}, u32[]{:S(2)}, u32[]{:S(2)}) %collective-permute-start.31) | collective-permute-done | bytes 73760 | tf_op jit(solution)/shard_map/ppermute | solution.py:449
  94.1 2.6 %shard_map.91 = (f32[3,8,8,256]{3,2,1,0:T(8,128)S(1)}, f32[8,8,256]{2,1,0:T(8,128)S(1)}) custom-call(s32[2]{0:T(128)S(1)} %pad_add_fusion.1.info, f32[2]{0:T(128)S(1)} %add_convert_fusion.flags, f32[8,3]{1,0:T(8,128)S(1)} %copy.21.speed, f32[3,12,8,256]{3,2,1,0:T(8,128)S(1)} %get-tuple-element.221.win, ...), custom_call_target="tpu_custom_call" | custom-call | flops 1000000 | bytes 1000000 | tf_op jit(solution)/shard_map/pallas_call | solution.py:409
  96.8 4.8 %collective-permute-start.33 = (f32[8,8,256]{2,1,0:T(8,128)S(1)}, f32[8,8,256]{2,1,0:T(8,128)S(1)}, u32[]{:S(2)}, u32[]{:S(2)}) collective-permute-start(f32[8,8,256]{2,1,0:T(8,128)S(1)} %get-tuple-element.224.own), channel_id=1, source_target_pairs={{0,248},{1,249},{2,250},{3,251},{4,252},{5,253},{6,254},{7,255},{8... | collective-permute-start | bytes 196616 | tf_op jit(solution)/shard_map/ppermute | solution.py:449
  103.2 3.1 %collective-permute-start.35 = (f32[24,8,256]{2,1,0:T(8,128)S(1)}, f32[24,8,256]{2,1,0:T(8,128)S(1)}, u32[]{:S(2)}, u32[]{:S(2)}) collective-permute-start(f32[24,8,256]{2,1,0:T(8,128)S(1)} %constant_dynamic-update-slice_fusion.9), channel_id=1, source_target_pairs={{1,4},{2,5},{3,6},{4,1},{5,2},{6,3},{9,12},{10,13},{11,14},{12,9},... | collective-permute-start | bytes 589832 | tf_op jit(solution)/shard_map/ppermute | solution.py:449
  106.4 3.8 %collective-permute-done.35.from_chip = f32[24,8,256]{2,1,0:T(8,128)S(1)} collective-permute-done((f32[24,8,256]{2,1,0:T(8,128)S(1)}, f32[24,8,256]{2,1,0:T(8,128)S(1)}, u32[]{:S(2)}, u32[]{:S(2)}) %collective-permute-start.35) | collective-permute-done | bytes 196640 | tf_op jit(solution)/shard_map/ppermute | solution.py:449
  110.2 7.6 %shard_map.92 = (f32[256,128]{1,0:T(8,128)}, f32[8,10,24,256]{3,2,1,0:T(8,128)S(1)}) custom-call(s32[2]{0:T(128)S(1)} %pad_add_fusion.1.info, f32[2]{0:T(128)S(1)} %add_convert_fusion.flags, f32[8,8,256]{2,1,0:T(8,128)S(1)} %get-tuple-element.224.own, f32[8,8,256]{2,1,0:T(8,128)S(1)} %collective-permute-done.32.left, ...), custom_call_target="tpu_custom_call" | custom-call | flops 1000000 | bytes 1000000 | tf_op jit(solution)/shard_map/pallas_call | solution.py:409
  117.8 9.6 %all-to-all-start.1 = ((f32[256,1,128]{2,1,0:T(1,128)}), f32[256,1,128]{2,1,0:T(1,128)S(1)}, u32[]{:S(2)}, u32[]{:S(2)}) async-start(f32[256,1,128]{2,1,0:T(1,128)} %bitcast.37), calls=%async_computation.1 | async-start | bytes 262144 | tf_op jit(solution)/shard_map/all_to_all | solution.py:502
  127.9 12.2 %all-to-all-done.1 = f32[256,1,128]{2,1,0:T(1,128)S(1)} async-done(((f32[256,1,128]{2,1,0:T(1,128)}), f32[256,1,128]{2,1,0:T(1,128)S(1)}, u32[]{:S(2)}, u32[]{:S(2)}) %all-to-all-start.1) | async-done | bytes 131104 | tf_op jit(solution)/shard_map/all_to_all | solution.py:502
  143.5 3.3 %conditional.1 = (f32[3,4,16,256]{3,2,1,0:T(8,128)}, f32[4,16,256]{2,1,0:T(8,128)}) conditional(s32[]{:T(128)} %bitcast.39, (s32[2]{0:T(128)S(1)}, s32[4,16,256]{2,1,0:T(8,128)S(1)}, f32[8,3]{0,1:T(4,128)S(1)}, f32[3,4,16,256]{3,2,1,0:T(8,128)}) %tuple.184, (pred[]{:T(512)}, f32[4,4,8,256]{3,2,1,0:T(8,128)S(1)}, f32[4,4,8,256]{3,2,1,0:T(8,128)S(1)}) %tuple.42), branch_computations={%region_0.9_spmd, %region_9.10_spmd} | conditional | flops 3744999 | bytes 12867730 | solution.py:526
  (74 shorter events, 20.0 us)
Async XLA Ops:
  2.5 6.2 %collective-permute-start.18 = (f32[13,16,256]{2,1,0:T(8,128)S(1)}, f32[13,16,256]{2,1,0:T(8,128)S(1)}, u32[]{:S(2)}, u32[]{:S(2)}) collective-permute-start(f32[13,16,256]{2,1,0:T(8,128)S(1)} %pad_maximum_fusion.11), channel_id=1, source_target_pairs={{0,252},{1,253},{2,254},{3,255},{4,8},{5,9},{6,10},{7,11},{8,4},{9... | collective-permute-start | bytes 638984 | tf_op jit(solution)/shard_map/ppermute | solution.py:449
  8.8 7.8 %collective-permute-start.19 = (f32[29,8,256]{2,1,0:T(8,128)S(1)}, f32[29,8,256]{2,1,0:T(8,128)S(1)}, u32[]{:S(2)}, u32[]{:S(2)}) collective-permute-start(f32[29,8,256]{2,1,0:T(8,128)S(1)} %slice_select_fusion), channel_id=1, source_target_pairs={{0,4},{1,5},{2,6},{3,7},{4,0},{5,1},{6,2},{7,3},{8,12},{9,13},{10,... | collective-permute-start | bytes 712712 | tf_op jit(solution)/shard_map/ppermute | solution.py:449
  16.6 59.5 %copy-start = (f32[8,16,256]{2,1,0:T(8,128)S(1)}, f32[8,16,256]{2,1,0:T(8,128)}, u32[]{:S(2)}) copy-start(f32[8,16,256]{2,1,0:T(8,128)} %constant.261.clone.coef) | copy-start | bytes 393220
  16.7 59.5 %copy-start.1 = (f32[16,256]{1,0:T(8,128)S(1)}, f32[16,256]{1,0:T(8,128)}, u32[]{:S(2)}) copy-start(f32[16,256]{1,0:T(8,128)} %constant.260.clone.node) | copy-start | bytes 49156
  16.7 59.5 %copy-start.2 = (f32[16,128]{1,0:T(8,128)S(1)}, f32[16,128]{1,0:T(8,128)}, u32[]{:S(2)}) copy-start(f32[16,128]{1,0:T(8,128)} %constant.259.clone.weight_map) | copy-start | bytes 24580
  16.8 8.5 %collective-permute-start.23 = (f32[10,1,256]{2,1,0:T(1,128)S(1)}, f32[10,1,256]{2,1,0:T(1,128)S(1)}, u32[]{:S(2)}, u32[]{:S(2)}) collective-permute-start(f32[10,1,256]{2,1,0:T(1,128)S(1)} %get-tuple-element.366), channel_id=1, source_target_pairs={{1,4},{2,5},{3,6},{4,1},{5,2},{6,3},{9,12},{10,13},{11,14},{12,9},... | collective-permute-start | bytes 30728 | tf_op jit(solution)/shard_map/ppermute | solution.py:449
  20.1 5.2 %collective-permute-start.22 = (f32[10,1,256]{2,1,0:T(1,128)S(1)}, f32[10,1,256]{2,1,0:T(1,128)S(1)}, u32[]{:S(2)}, u32[]{:S(2)}) collective-permute-start(f32[10,1,256]{2,1,0:T(1,128)S(1)} %get-tuple-element.367), channel_id=1, source_target_pairs={{0,4},{1,5},{2,6},{3,7},{4,0},{5,1},{6,2},{7,3},{8,12},{9,13},{10,... | collective-permute-start | bytes 30728 | tf_op jit(solution)/shard_map/ppermute | solution.py:449
  21.5 3.9 %collective-permute-start.20 = (f32[3,12,2,256]{3,2,1,0:T(2,128)S(1)}, f32[3,12,2,256]{3,2,1,0:T(2,128)S(1)}, u32[]{:S(2)}, u32[]{:S(2)}) collective-permute-start(f32[3,12,2,256]{3,2,1,0:T(2,128)S(1)} %get-tuple-element.213), channel_id=1, source_target_pairs={{0,4},{1,5},{2,6},{3,7},{4,0},{5,1},{6,2},{7,3},{8,12},{9,13},{10,... | collective-permute-start | bytes 221192 | tf_op jit(solution)/shard_map/ppermute | solution.py:449
  22.1 5.7 %collective-permute-start.21 = (f32[3,12,2,256]{3,2,1,0:T(2,128)S(1)}, f32[3,12,2,256]{3,2,1,0:T(2,128)S(1)}, u32[]{:S(2)}, u32[]{:S(2)}) collective-permute-start(f32[3,12,2,256]{3,2,1,0:T(2,128)S(1)} %get-tuple-element.214), channel_id=1, source_target_pairs={{1,4},{2,5},{3,6},{4,1},{5,2},{6,3},{9,12},{10,13},{11,14},{12,9},... | collective-permute-start | bytes 221192 | tf_op jit(solution)/shard_map/ppermute | solution.py:449
  30.3 6.6 %collective-permute-start.24 = (f32[8,8,256]{2,1,0:T(8,128)S(1)}, f32[8,8,256]{2,1,0:T(8,128)S(1)}, u32[]{:S(2)}, u32[]{:S(2)}) collective-permute-start(f32[8,8,256]{2,1,0:T(8,128)S(1)} %get-tuple-element.215.own), channel_id=1, source_target_pairs={{0,8},{1,9},{2,10},{3,11},{4,12},{5,13},{6,14},{7,15},{8,16},{9,17... | collective-permute-start | bytes 196616 | tf_op jit(solution)/shard_map/ppermute | solution.py:449
  30.4 6.6 %collective-permute-start.25 = (f32[8,8,256]{2,1,0:T(8,128)S(1)}, f32[8,8,256]{2,1,0:T(8,128)S(1)}, u32[]{:S(2)}, u32[]{:S(2)}) collective-permute-start(f32[8,8,256]{2,1,0:T(8,128)S(1)} %get-tuple-element.215.own), channel_id=1, source_target_pairs={{0,248},{1,249},{2,250},{3,251},{4,252},{5,253},{6,254},{7,255},{8... | collective-permute-start | bytes 196616 | tf_op jit(solution)/shard_map/ppermute | solution.py:449
  37.0 7.8 %collective-permute-start.27 = (f32[24,8,256]{2,1,0:T(8,128)S(1)}, f32[24,8,256]{2,1,0:T(8,128)S(1)}, u32[]{:S(2)}, u32[]{:S(2)}) collective-permute-start(f32[24,8,256]{2,1,0:T(8,128)S(1)} %constant_dynamic-update-slice_fusion.6), channel_id=1, source_target_pairs={{1,4},{2,5},{3,6},{4,1},{5,2},{6,3},{9,12},{10,13},{11,14},{12,9},... | collective-permute-start | bytes 589832 | tf_op jit(solution)/shard_map/ppermute | solution.py:449
  41.5 3.3 %collective-permute-start.26 = (f32[24,8,256]{2,1,0:T(8,128)S(1)}, f32[24,8,256]{2,1,0:T(8,128)S(1)}, u32[]{:S(2)}, u32[]{:S(2)}) collective-permute-start(f32[24,8,256]{2,1,0:T(8,128)S(1)} %constant_dynamic-update-slice_fusion.6), channel_id=1, source_target_pairs={{0,4},{1,5},{2,6},{3,7},{4,0},{5,1},{6,2},{7,3},{8,12},{9,13},{10,... | collective-permute-start | bytes 589832 | tf_op jit(solution)/shard_map/ppermute | solution.py:449
  77.3 3.0 %collective-permute-start.29 = (f32[3,2,8,256]{3,2,1,0:T(8,128)S(1)}, f32[3,2,8,256]{3,2,1,0:T(8,128)S(1)}, u32[]{:S(2)}, u32[]{:S(2)}) collective-permute-start(f32[3,2,8,256]{3,2,1,0:T(8,128)S(1)} %slice.687), channel_id=1, source_target_pairs={{0,248},{1,249},{2,250},{3,251},{4,252},{5,253},{6,254},{7,255},{8... | collective-permute-start | bytes 147464 | tf_op jit(solution)/shard_map/ppermute | solution.py:449
  77.9 6.8 %collective-permute-start.28 = (f32[3,4,8,256]{3,2,1,0:T(8,128)S(1)}, f32[3,4,8,256]{3,2,1,0:T(8,128)S(1)}, u32[]{:S(2)}, u32[]{:S(2)}) collective-permute-start(f32[3,4,8,256]{3,2,1,0:T(8,128)S(1)} %slice.686), channel_id=1, source_target_pairs={{0,8},{1,9},{2,10},{3,11},{4,12},{5,13},{6,14},{7,15},{8,16},{9,17... | collective-permute-start | bytes 294920 | tf_op jit(solution)/shard_map/ppermute | solution.py:449
  85.9 4.5 %collective-permute-start.30 = (f32[3,12,2,256]{3,2,1,0:T(2,128)S(1)}, f32[3,12,2,256]{3,2,1,0:T(2,128)S(1)}, u32[]{:S(2)}, u32[]{:S(2)}) collective-permute-start(f32[3,12,2,256]{3,2,1,0:T(2,128)S(1)} %get-tuple-element.222), channel_id=1, source_target_pairs={{0,4},{1,5},{2,6},{3,7},{4,0},{5,1},{6,2},{7,3},{8,12},{9,13},{10,... | collective-permute-start | bytes 221192 | tf_op jit(solution)/shard_map/ppermute | solution.py:449
  88.4 5.7 %collective-permute-start.31 = (f32[3,12,2,256]{3,2,1,0:T(2,128)S(1)}, f32[3,12,2,256]{3,2,1,0:T(2,128)S(1)}, u32[]{:S(2)}, u32[]{:S(2)}) collective-permute-start(f32[3,12,2,256]{3,2,1,0:T(2,128)S(1)} %get-tuple-element.223), channel_id=1, source_target_pairs={{1,4},{2,5},{3,6},{4,1},{5,2},{6,3},{9,12},{10,13},{11,14},{12,9},... | collective-permute-start | bytes 221192 | tf_op jit(solution)/shard_map/ppermute | solution.py:449
  96.7 46.8 %copy-start.5 = (s32[4,16,256]{2,1,0:T(8,128)S(1)}, s32[4,16,256]{2,1,0:T(8,128)}, u32[]{:S(2)}) copy-start(s32[4,16,256]{2,1,0:T(8,128)} %param.14) | copy-start | bytes 196612
  96.7 6.5 %collective-permute-start.32 = (f32[8,8,256]{2,1,0:T(8,128)S(1)}, f32[8,8,256]{2,1,0:T(8,128)S(1)}, u32[]{:S(2)}, u32[]{:S(2)}) collective-permute-start(f32[8,8,256]{2,1,0:T(8,128)S(1)} %get-tuple-element.224.own), channel_id=1, source_target_pairs={{0,8},{1,9},{2,10},{3,11},{4,12},{5,13},{6,14},{7,15},{8,16},{9,17... | collective-permute-start | bytes 196616 | tf_op jit(solution)/shard_map/ppermute | solution.py:449
  96.8 6.4 %collective-permute-start.33 = (f32[8,8,256]{2,1,0:T(8,128)S(1)}, f32[8,8,256]{2,1,0:T(8,128)S(1)}, u32[]{:S(2)}, u32[]{:S(2)}) collective-permute-start(f32[8,8,256]{2,1,0:T(8,128)S(1)} %get-tuple-element.224.own), channel_id=1, source_target_pairs={{0,248},{1,249},{2,250},{3,251},{4,252},{5,253},{6,254},{7,255},{8... | collective-permute-start | bytes 196616 | tf_op jit(solution)/shard_map/ppermute | solution.py:449
  103.2 7.0 %collective-permute-start.35 = (f32[24,8,256]{2,1,0:T(8,128)S(1)}, f32[24,8,256]{2,1,0:T(8,128)S(1)}, u32[]{:S(2)}, u32[]{:S(2)}) collective-permute-start(f32[24,8,256]{2,1,0:T(8,128)S(1)} %constant_dynamic-update-slice_fusion.9), channel_id=1, source_target_pairs={{1,4},{2,5},{3,6},{4,1},{5,2},{6,3},{9,12},{10,13},{11,14},{12,9},... | collective-permute-start | bytes 589832 | tf_op jit(solution)/shard_map/ppermute | solution.py:449
  106.3 3.9 %collective-permute-start.34 = (f32[24,8,256]{2,1,0:T(8,128)S(1)}, f32[24,8,256]{2,1,0:T(8,128)S(1)}, u32[]{:S(2)}, u32[]{:S(2)}) collective-permute-start(f32[24,8,256]{2,1,0:T(8,128)S(1)} %constant_dynamic-update-slice_fusion.9), channel_id=1, source_target_pairs={{0,4},{1,5},{2,6},{3,7},{4,0},{5,1},{6,2},{7,3},{8,12},{9,13},{10,... | collective-permute-start | bytes 589832 | tf_op jit(solution)/shard_map/ppermute | solution.py:449
  117.8 22.3 %all-to-all-start.1 = ((f32[256,1,128]{2,1,0:T(1,128)}), f32[256,1,128]{2,1,0:T(1,128)S(1)}, u32[]{:S(2)}, u32[]{:S(2)}) async-start(f32[256,1,128]{2,1,0:T(1,128)} %bitcast.37), calls=%async_computation.1 | async-start | bytes 262144 | tf_op jit(solution)/shard_map/all_to_all | solution.py:502
  143.8 1.7 %collective-permute-start = (f32[4,4,8,256]{3,2,1,0:T(8,128)S(1)}, f32[4,4,8,256]{3,2,1,0:T(8,128)S(1)}, u32[]{:S(2)}, u32[]{:S(2)}) collective-permute-start(f32[4,4,8,256]{3,2,1,0:T(8,128)S(1)} %get-tuple-element.190), channel_id=1, source_target_pairs={{0,4},{1,5},{2,6},{3,7},{4,0},{5,1},{6,2},{7,3},{8,12},{9,13},{10,... | collective-permute-start | bytes 393224 | tf_op jit(solution)/shard_map/cond/branch_1_fun/ppermute | solution.py:449
  (3 other events, 46.3 us)

commit v2 on v0

--- a/solution.py
+++ b/solution.py
@@ -1,6 +1,11 @@
+import functools
+
 import jax
 import jax.numpy as jnp
+import numpy as np
 from jax import lax
+from jax.experimental import pallas as pl
+from jax.experimental.pallas import tpu as pltpu
 from jax.sharding import PartitionSpec as P
 
 SWIMMERS = 8
@@ -8,11 +13,16 @@
 PASSES = 8
 SMAX = 2
 
-
 TIME_STEP = 0.1
 VISCOSITY = 0.5
 PENALTY = 4.0
 SCREEN = 0.05
+
+AXES = ("gx", "gy")
+NODES = 16
+NZ = 256
+DEPTH = 8
+NOISE = 1e-4
 
 
 def shifted(value, axis, steps):
@@ -99,14 +109,19 @@
     return jnp.stack([(x_plus - x_minus) * 0.5, (y_plus - y_minus) * 0.5, (z_plus - z_minus) * 0.5])
 
 
-def dot_pair(residual, image):
-    return lax.psum((jnp.sum(residual * residual), jnp.sum(residual * image)), ("gx", "gy"))
-
-
-def body(velocity, cell_swimmer, swimmer_speed, recentre_cols):
+def plain(velocity, cell_swimmer, swimmer_speed, recentre_cols):
     width_x = velocity.shape[1]
-    pressure = jnp.zeros(velocity.shape[1:], jnp.float32)
-    for step_index in range(STEPS):
+
+    def search(_, state):
+        pressure, residual = state
+        extended = pad_walls(padded_2(residual, (("gx", 0), ("gy", 1)), 1, True), 1)
+        image = operate(extended)
+        norm_sq, curvature = lax.psum((jnp.sum(residual * residual), jnp.sum(residual * image)), AXES)
+        alpha = norm_sq / curvature
+        return (pressure + alpha * residual, residual - alpha * image)
+
+    def step(step_index, state):
+        velocity, _ = state
         offset = recentre_cols[step_index]
         tail_cols = velocity[:, width_x - SMAX :]
         received = shifted(tail_cols, "gx", 1)
@@ -118,24 +133,397 @@
         flux_x = padded_2(velocity[0], (("gx", 0),), 1, True)
         flux_y = padded_2(velocity[1], (("gy", 1),), 1, False)
         source = -divergence(flux_x, flux_y, velocity[2])
-        pressure = jnp.zeros_like(source)
-        residual = source
-        for pass_index in range(PASSES):
-            extended = pad_walls(padded_2(residual, (("gx", 0), ("gy", 1)), 1, True), 1)
-            image = operate(extended)
-            norm_sq, curvature = dot_pair(residual, image)
-            alpha = norm_sq / curvature
-            pressure = pressure + alpha * residual
-            residual = residual - alpha * image
+        pressure, _ = lax.fori_loop(0, PASSES, search, (jnp.zeros_like(source), source))
         padded = pad_walls(padded_2(pressure, (("gx", 0), ("gy", 1)), 1, True), 1)
-        velocity = velocity - gradient(padded)
-    return (velocity, pressure)
+        return (velocity - gradient(padded), pressure)
+
+    start = (velocity, jnp.zeros(velocity.shape[1:], jnp.float32))
+    return lax.fori_loop(0, STEPS, step, start)
+
+
+def tables():
+    angle = (np.arange(NODES) + 0.5) * np.pi / NODES
+    cheb = np.cos(np.outer(np.arange(NODES), angle))
+    moment = np.zeros((NODES, NODES))
+    moment[0, 0] = moment[1, 1] = 1.0
+    for i in range(1, NODES // 2):
+        moment[2 * i, 2 * i], moment[2 * i, 0] = 2.0, -1.0
+        moment[2 * i + 1, 2 * i + 1], moment[2 * i + 1, 1] = 2.0, -1.0
+    scale = np.full((NODES, 1), 2.0 / NODES)
+    scale[0] = 1.0 / NODES
+    weight = cheb.T @ (scale * moment)
+    weight_map = np.zeros((NODES, 128))
+    weight_map[:, :NODES] = weight
+    node = (6.0 + SCREEN) - 6.0 * np.cos(angle)
+    node = np.broadcast_to(node[:, None], (NODES, NZ // 2))
+    coef = np.broadcast_to((scale * cheb)[:PASSES, :, None], (PASSES, NODES, NZ // 2))
+    return [np.ascontiguousarray(a, dtype=np.float32) for a in (weight_map, node, coef)]
+
+
+HALF = NZ // 2
+
+
+def halves(a):
+    return a[:, :HALF], a[:, HALF:]
+
+
+def z_pair(a, b):
+    lane = lax.broadcasted_iota(jnp.int32, a.shape, 1)
+    a_next, b_next = pltpu.roll(a, HALF - 1, 1), pltpu.roll(b, HALF - 1, 1)
+    a_prev, b_prev = pltpu.roll(a, 1, 1), pltpu.roll(b, 1, 1)
+    last, start = lane == HALF - 1, lane == 0
+    return (
+        (jnp.where(last, b_next, a_next), jnp.where(start, b_prev, a_prev)),
+        (jnp.where(last, a_next, b_next), jnp.where(start, a_prev, b_prev)),
+    )
+
+
+def source_kernel(
+    info, flags, speed, left, own, right, from_core, from_chip, cell, cell_core, cell_chip, bodied, source, pad, ids, body, *, step
+):
+    core = info[0]
+    joined = 2 - info[1 + step]
+    up_flag, down_flag = flags[0], flags[1]
+
+    def put(c, i, value):
+        for h, part in enumerate(halves(value)):
+            pad[c, i, h, 8:16] = part
+
+    for c in range(3):
+        for i in range(4):
+            put(c, i, left[c, i])
+        for i in range(8):
+            put(c, i + 4, own[c, i])
+        for i in range(2):
+            put(c, i + 12, right[c, i])
+        for i in range(14):
+            a, b = from_core[c, i], from_chip[c, i]
+            up = jnp.where(core == 0, b, a) * up_flag
+            down = jnp.where(core == 0, a, b) * down_flag
+            for h in range(2):
+                pad[c, i, h, 6:8] = halves(up)[h]
+                pad[c, i, h, 16:18] = halves(down)[h]
+    for i in range(10):
+        a, b = cell_core[i], cell_chip[i]
+        up, down = jnp.where(core == 0, b, a), jnp.where(core == 0, a, b)
+        for h in range(2):
+            ids[i, h, 8:16] = halves(cell[i])[h]
+            ids[i, h, 6:8] = halves(up)[h]
+            ids[i, h, 16:18] = halves(down)[h]
+
+    row = lax.broadcasted_iota(jnp.int32, (8, HALF), 0)
+    inside = (jnp.where(row == 0, up_flag, 1.0), jnp.where(row == 0, 1.0, down_flag))
+
+    def move(i, _):
+        p = i + 1 + joined
+        for block in range(2):
+            r = 7 + 8 * block
+            centre = [[pad[c, p, h, r : r + 8] for h in range(2)] for c in range(3)]
+            beside = [z_pair(*centre[c]) for c in range(3)]
+            for h in range(2):
+                cells = ids[i, h, r : r + 8]
+                marks = [cells == swimmer for swimmer in range(SWIMMERS)]
+                factor = jnp.where(cells < SWIMMERS, 1.0 / (1.0 + PENALTY), 1.0) * inside[block]
+                for c in range(3):
+                    here = centre[c][h]
+                    x_plus, x_minus = pad[c, p + 1, h, r : r + 8], pad[c, p - 1, h, r : r + 8]
+                    y_plus, y_minus = pad[c, p, h, r + 1 : r + 9], pad[c, p, h, r - 1 : r + 7]
+                    z_plus, z_minus = beside[c][h]
+                    laplace = x_plus + x_minus + y_plus + y_minus + z_plus + z_minus - 6.0 * here
+                    transport = (
+                        centre[0][h] * (x_plus - x_minus)
+                        + centre[1][h] * (y_plus - y_minus)
+                        + centre[2][h] * (z_plus - z_minus)
+                    )
+                    moved = here + (TIME_STEP * VISCOSITY) * laplace - (TIME_STEP * 0.5) * transport
+                    target = jnp.zeros((8, HALF), jnp.float32)
+                    for swimmer in range(SWIMMERS):
+                        target = jnp.where(marks[swimmer], PENALTY * speed[swimmer, c], target)
+                    body[c, i, h, 8 * block : 8 * block + 8] = (moved + target) * factor
+        return 0
+
+    for i in range(10):
+        move(i, 0)
+
+    for i in range(8):
+        b2 = [body[2, i + 1, h, 1:9] for h in range(2)]
+        beside = z_pair(*b2)
+        for h in range(2):
+            lanes = slice(h * HALF, (h + 1) * HALF)
+            along_x = body[0, i + 2, h, 1:9] - body[0, i, h, 1:9]
+            along_y = body[1, i + 1, h, 2:10] - body[1, i + 1, h, 0:8]
+            along_z = beside[h][0] - beside[h][1]
+            source[i, :, lanes] = -0.5 * (along_x + along_y + along_z)
+            bodied[2, i, :, lanes] = b2[h]
+            for c in range(2):
+                bodied[c, i, :, lanes] = body[c, i + 1, h, 1:9]
+
+
+def powers_kernel(info, flags, own, left, right, from_core, from_chip, moments, near, *t):
+    core = info[0]
+    scale = (flags[0], 1.0, flags[1])
+
+    for i in range(24):
+        a, b = from_core[i], from_chip[i]
+        up, down = jnp.where(core == 0, b, a) * scale[0], jnp.where(core == 0, a, b) * scale[2]
+        middle = (left, own, right)[i // 8][i % 8]
+        for h in range(2):
+            t[0][i, h, 8:16] = halves(up)[h]
+            t[0][i, h, 16:24] = halves(middle)[h]
+            t[0][i, h, 24:32] = halves(down)[h]
+
+    for j in range(1, PASSES + 1):
+        blocks = (0, 1, 2) if j < PASSES else (1,)
+
+        def level(i, _, j=j, blocks=blocks):
+            for block in blocks:
+                r = 8 + 8 * block
+                factor = scale[block] * (1.0 / 6.0 if j == 1 else 1.0 / 3.0)
+                beside = z_pair(t[j - 1][i, 0, r : r + 8], t[j - 1][i, 1, r : r + 8])
+                for h in range(2):
+                    total = (
+                        (t[j - 1][i - 1, h, r : r + 8] + t[j - 1][i + 1, h, r : r + 8])
+                        + (t[j - 1][i, h, r - 1 : r + 7] + t[j - 1][i, h, r + 1 : r + 9])
+                        + (beside[h][0] + beside[h][1])
+                    )
+                    value = total * factor
+                    if j > 1:
+                        value = value - t[j - 2][i, h, r : r + 8]
+                    t[j][i, h, r : r + 8] = value
+            return 0
+
+        for i in range(j, 24 - j):
+            level(i, 0)
+
+    def product(i, sums):
+        out = list(sums)
+        for h in range(2):
+            values = [t[j][i, h, 16:24] for j in range(PASSES + 1)]
+            for j in range(PASSES):
+                out[2 * j] = out[2 * j] + values[j] * values[j]
+                out[2 * j + 1] = out[2 * j + 1] + values[j] * values[j + 1]
+        return tuple(out)
+
+    zero = jnp.zeros((8, HALF), jnp.float32)
+    sums = (zero,) * NODES
+    for i in range(DEPTH, 2 * DEPTH):
+        sums = product(i, sums)
+    lines = [jnp.sum(a, axis=0, keepdims=True) for a in sums]
+    block = jnp.concatenate(lines + [jnp.zeros((128 - NODES, 128), jnp.float32)], axis=0)
+    line = jnp.sum(block.T, axis=0, keepdims=True)
+    moments[...] = jnp.broadcast_to(line, moments.shape)
+
+    def keep(i, _):
+        for j in range(PASSES):
+            for h in range(2):
+                near[j, i, h, 0:8] = t[j][i + DEPTH - 1, h, 15:23]
+                near[j, i, h, 8:16] = t[j][i + DEPTH - 1, h, 23:31]
+        return 0
+
+    for i in range(10):
+        keep(i, 0)
+
+
+def lengths(moments, weight_map, node, coef):
+    line = jnp.sum(moments[...], axis=0, keepdims=True)
+    weight = jnp.sum(weight_map[...] * line, axis=1, keepdims=True)
+    weight = jnp.broadcast_to(weight, (NODES, HALF))
+    first = jnp.sum(weight, axis=0, keepdims=True)
+    value = node[...]
+    residual = jnp.ones((NODES, HALF), jnp.float32)
+    search = jnp.zeros((NODES, HALF), jnp.float32)
+    good = jnp.ones((1, HALF), jnp.float32)
+    for _ in range(PASSES):
+        square = residual * residual
+        norm_sq = jnp.sum(weight * square, axis=0, keepdims=True)
+        curvature = jnp.sum(weight * square * value, axis=0, keepdims=True)
+        noise = NOISE * first * jnp.sum(square, axis=0, keepdims=True)
+        noise_image = NOISE * first * jnp.sum(square * value, axis=0, keepdims=True)
+        good = jnp.where((norm_sq > noise) & (curvature > noise_image), good, 0.0)
+        alpha = norm_sq / curvature
+        search = search + alpha * residual
+        residual = residual - alpha * value * residual
+    terms = [jnp.sum(coef[j] * search, axis=0, keepdims=True) for j in range(PASSES)]
+    return terms, good
+
+
+def correct(terms, near, bodied, emit, p):
+    def combine(i, _):
+        for h in range(2):
+            for r in (0, 8):
+                total = terms[0] * near[0, i, h, r : r + 8]
+                for j in range(1, PASSES):
+                    total = total + terms[j] * near[j, i, h, r : r + 8]
+                p[i, h, r : r + 8] = total
+        return 0
+
+    for i in range(10):
+        combine(i, 0)
+    for i in range(8):
+        own = [p[i + 1, h, 1:9] for h in range(2)]
+        beside = z_pair(*own)
+        for h in range(2):
+            lanes = slice(h * HALF, (h + 1) * HALF)
+            emit(0, i, lanes, bodied[0, i, :, lanes] - 0.5 * (p[i + 2, h, 1:9] - p[i, h, 1:9]))
+            emit(1, i, lanes, bodied[1, i, :, lanes] - 0.5 * (p[i + 1, h, 2:10] - p[i + 1, h, 0:8]))
+            emit(2, i, lanes, bodied[2, i, :, lanes] - 0.5 * (beside[h][0] - beside[h][1]))
+            emit(3, i, lanes, own[h])
+
+
+def inner_step_kernel(moments, weight_map, node, coef, near, bodied, good_out, velocity, p):
+    terms, good = lengths(moments, weight_map, node, coef)
+    good_out[...] = good
+
+    def emit(c, i, lanes, value):
+        if c < 3:
+            velocity[c, i, :, lanes] = value
+
+    correct(terms, near, bodied, emit, p)
+
+
+def last_step_kernel(info, moments, weight_map, node, coef, near, bodied, good_in, good_out, kept, sent, p, fields):
+    terms, good = lengths(moments, weight_map, node, coef)
+    good_out[0] = (jnp.min(good * good_in[...]) > 0.5).astype(jnp.int32)
+    core = info[0]
+
+    def emit(c, i, lanes, value):
+        fields[c, i, :, lanes] = value
+
+    correct(terms, near, bodied, emit, p)
+    for i in range(4):
+        for c in range(4):
+            kept[c, i] = fields[c, 4 * core + i]
+            sent[c, i] = fields[c, 4 * (1 - core) + i]
+
+
+SMEM = pl.BlockSpec(memory_space=pltpu.SMEM)
+VMEM = pl.BlockSpec(memory_space=pltpu.VMEM)
+
+
+def call(kernel, args, smem, outs, scratch, flags_out=0):
+    specs, shapes = [VMEM] * len(outs), [jax.ShapeDtypeStruct(o, jnp.float32) for o in outs]
+    if flags_out:
+        specs, shapes = [SMEM] + specs, [jax.ShapeDtypeStruct((1,), jnp.int32)] + shapes
+    return pl.pallas_call(
+        kernel,
+        in_specs=[SMEM] * smem + [VMEM] * (len(args) - smem),
+        out_specs=specs,
+        out_shape=shapes,
+        scratch_shapes=[pltpu.VMEM(o, jnp.float32) for o in scratch],
+        compiler_params=pltpu.CompilerParams(vmem_limit_bytes=24 * 1024 * 1024),
+        cost_estimate=pl.CostEstimate(flops=1_000_000, bytes_accessed=1_000_000, transcendentals=0),
+    )(*args)
+
+
+def routes(count_x, count_y):
+    chips = count_x // 2
+
+    def pairs(target):
+        out = []
+        for chip in range(chips):
+            for core in range(2):
+                for y in range(count_y):
+                    to = target(chip, core, y)
+                    source = (2 * chip + core) * count_y + y
+                    out.append((source, (2 * (to[0] % chips) + to[1]) * count_y + to[2]))
+        return out
+
+    def across(chip, core, y):
+        return (chip, 1 - core, (y + (1 if core else -1)) % count_y)
+
+    return {
+        "core": pairs(lambda chip, core, y: (chip, 1 - core, y)),
+        "facing": pairs(lambda chip, core, y: (chip + (1 if core else -1), 1 - core, y)),
+        "right": pairs(lambda chip, core, y: (chip + 1, core, y)),
+        "left": pairs(lambda chip, core, y: (chip - 1, core, y)),
+        "across": pairs(across),
+    }
+
+
+def body(velocity, cell_swimmer, swimmer_speed, recentre_cols, *, count_x, count_y):
+    route = routes(count_x, count_y)
+    send = lambda value, name: lax.ppermute(value, AXES, route[name])
+    core = lax.axis_index("gx") % 2
+    y = lax.axis_index("gy")
+    flags = jnp.stack([(y > 0) | (core == 1), (y < count_y - 1) | (core == 0)]).astype(jnp.float32)
+    info = jnp.stack([core, recentre_cols[0], recentre_cols[1]]).astype(jnp.int32)
+    weight_map, node, coef = (jnp.asarray(a) for a in tables())
+    first = core == 0
+    pick = lambda a, b: jnp.where(first, a, b)
+
+    cells = cell_swimmer.astype(jnp.float32)
+    rows = velocity.reshape(12, 16, NZ)
+    outer = send(jnp.concatenate([rows, pick(cells[0:1], cells[3:4])], axis=0), "facing")
+    chunk = jnp.concatenate([rows, cells], axis=0)
+    theirs = send(pick(chunk[:, 8:16], chunk[:, 0:8]), "core")
+    mine = pick(chunk[:, 0:8], chunk[:, 8:16])
+    outer_theirs = send(pick(outer[:, 8:16], outer[:, 0:8]), "core")
+    outer_mine = pick(outer[:, 0:8], outer[:, 8:16])
+    low, high = pick(mine, theirs), pick(theirs, mine)
+    outer_low, outer_high = pick(outer_mine, outer_theirs), pick(outer_theirs, outer_mine)
+    planes = lambda a: a[0:12].reshape(3, 4, 8, NZ)
+    own = jnp.concatenate([planes(low), planes(high)], axis=1)
+    left, right = planes(outer_low), planes(outer_high)[:, 0:2]
+    cell = jnp.concatenate([outer_low[12:13], low[12:16], high[12:16], outer_high[12:13]], axis=0)
+
+    for step in range(STEPS):
+        if step:
+            left = send(own[:, 4:8], "right")
+            right = send(own[:, 0:2], "left")
+        joined = jnp.concatenate([left, own, right], axis=1)
+        if not step:
+            spare = jnp.concatenate([cell, cell[0:4]], axis=0)
+            joined = jnp.concatenate([joined, spare[None]], axis=0)
+        top, bottom = joined[:, :, 0:2], joined[:, :, 6:8]
+        from_core, from_chip = send(pick(bottom, top), "core"), send(pick(top, bottom), "across")
+        if not step:
+            cell_core, cell_chip = from_core[3, 0:10], from_chip[3, 0:10]
+        bodied, source = call(
+            functools.partial(source_kernel, step=step),
+            (info, flags, swimmer_speed, left, own, right, from_core, from_chip, cell, cell_core, cell_chip),
+            3,
+            [(3, 8, 8, NZ), (8, 8, NZ)],
+            [(3, 14, 2, 24, HALF), (10, 2, 24, HALF), (3, 10, 2, 16, HALF)],
+        )
+        s_left = send(source, "right")
+        s_right = send(source, "left")
+        column = jnp.concatenate([s_left, source, s_right], axis=0)
+        moments, near = call(
+            powers_kernel,
+            (info, flags, source, s_left, s_right, send(column, "core"), send(column, "across")),
+            2,
+            [(count_x * count_y, 128), (PASSES, 10, 2, 16, HALF)],
+            [(24, 2, 40, HALF)] * (PASSES + 1),
+        )
+        moments = lax.all_to_all(moments, AXES, 0, 0)
+        shared = (moments, weight_map, node, coef, near, bodied)
+        if step < STEPS - 1:
+            good, own = call(inner_step_kernel, shared, 0, [(1, HALF), (3, 8, 8, NZ)], [(10, 2, 16, HALF)])
+        else:
+            good, kept, sent = call(
+                last_step_kernel,
+                (info,) + shared + (good,),
+                1,
+                [(4, 4, 8, NZ), (4, 4, 8, NZ)],
+                [(10, 2, 16, HALF), (4, 8, 8, NZ)],
+                flags_out=1,
+            )
+
+    def finish(_):
+        got = send(sent, "core")
+        fields = jnp.concatenate([pick(kept, got), pick(got, kept)], axis=2)
+        return (fields[0:3], fields[3])
+
+    def again(_):
+        return plain(velocity, cell_swimmer, swimmer_speed, recentre_cols)
+
+    return lax.cond(good[0] > 0, finish, again, None)
 
 
 def solution(mesh):
     placed = (P(None, "gx", "gy", None), P("gx", "gy", None), P(), P())
     return jax.shard_map(
-        body,
+        functools.partial(body, count_x=mesh.shape["gx"], count_y=mesh.shape["gy"]),
         mesh=mesh,
         in_specs=placed,
         out_specs=(P(None, "gx", "gy", None), P("gx", "gy", None)),

time: 1570 us -> 123 us (0.08); the launches traced: 1550 us -> 123 us
  blocking collectives: 1310 us -> 24.4 us
  starting transfers between devices: 129 us -> 45 us
  waiting for transfers between devices: 64.6 us -> 37.6 us
  between operations: 25.4 us -> 1.63 us
    psum x16 -> x0, blocking collectives: 1310 us -> none  [dot_pair(): lax.psum((jnp.sum(residual * residual), jnp.sum(residual * image)), ('gx'...]
    ppermute x90 -> x18, starting transfers between devices: 129 us -> 36.9 us  [body(): send = lambda value, name: lax.ppermute(value, AXES, route[name])]
    ppermute x90 -> x18, waiting for transfers between devices: 64.6 us -> 24.9 us  [body(): send = lambda value, name: lax.ppermute(value, AXES, route[name])]
    all_to_all x0 -> x1, blocking collectives: none -> 24.4 us  [body(): moments = lax.all_to_all(moments, AXES, 0, 0)]
  transfers between devices with their start and end apart: 90 -> 19, of which waited for: 64 -> 13; matrix products, arithmetic and copies ran while one was open for 0% -> 0% of each run, Pallas kernels for 0% -> 0%
where the time goes in v2:
time: 123 us
  starting transfers between devices  45 us (37%)
  waiting for transfers between devices  37.6 us (31%)
  blocking collectives  24.4 us (20%)
  Pallas kernels  10.3 us (8%)
  other arithmetic  2.73 us (2%)
  between operations  1.63 us (1%)
    ppermute x18, starting transfers between devices, body(): send = lambda value, name: lax.ppermute(value, AXES, route[name])  36.9 us
    ppermute x18, waiting for transfers between devices, body(): send = lambda value, name: lax.ppermute(value, AXES, route[name])  24.9 us
    all_to_all x1, blocking collectives, body(): moments = lax.all_to_all(moments, AXES, 0, 0)  24.4 us
    all_to_all x1, waiting for transfers between devices, body(): moments = lax.all_to_all(moments, AXES, 0, 0)  12.7 us
    pallas_call x6, Pallas kernels, call(): pl.pallas_call(kernel, in_specs=[SMEM] * smem + [VMEM] * (len(args) - sme...  10.3 us
    all_to_all x1, starting transfers between devices, body(): moments = lax.all_to_all(moments, AXES, 0, 0)  8.19 us
  transfers between devices with their start and end apart: 19, of which 13 were waited for; matrix products, arithmetic and copies ran while one was open for 0% of the time, Pallas kernels for 0%

profile of v2, /device:TPU:1, one launch (start us, length us, event | category | flops | bytes accessed | tf_op | source)
XLA Modules:
  0.0 122.9 jit_solution(1136736234257698198)
XLA Ops:
  2.5 2.7 %collective-permute-start.18 = (f32[13,16,256]{2,1,0:T(8,128)S(1)}, f32[13,16,256]{2,1,0:T(8,128)S(1)}, u32[]{:S(2)}, u32[]{:S(2)}) collective-permute-start(f32[13,16,256]{2,1,0:T(8,128)S(1)} %pad_maximum_fusion.10), channel_id=1, source_target_pairs={{0,252},{1,253},{2,254},{3,255},{4,8},{5,9},{6,10},{7,11},{8,4},{9... | collective-permute-start | bytes 638984 | tf_op jit(solution)/shard_map/ppermute | solution.py:445
  5.2 6.5 %collective-permute-start.20 = (f32[16,8,256]{2,1,0:T(8,128)S(1)}, f32[16,8,256]{2,1,0:T(8,128)S(1)}, u32[]{:S(2)}, u32[]{:S(2)}) collective-permute-start(f32[16,8,256]{2,1,0:T(8,128)S(1)} %broadcast_select_fusion.8), channel_id=1, source_target_pairs={{0,4},{1,5},{2,6},{3,7},{4,0},{5,1},{6,2},{7,3},{8,12},{9,13},{10,... | collective-permute-start | bytes 393224 | tf_op jit(solution)/shard_map/ppermute | solution.py:445
  12.0 3.3 %collective-permute-start.19 = (f32[13,8,256]{2,1,0:T(8,128)S(1)}, f32[13,8,256]{2,1,0:T(8,128)S(1)}, u32[]{:S(2)}, u32[]{:S(2)}) collective-permute-start(f32[13,8,256]{2,1,0:T(8,128)S(1)} %slice_select_fusion), channel_id=1, source_target_pairs={{0,4},{1,5},{2,6},{3,7},{4,0},{5,1},{6,2},{7,3},{8,12},{9,13},{10,... | collective-permute-start | bytes 319496 | tf_op jit(solution)/shard_map/ppermute | solution.py:445
  17.0 1.4 %collective-permute-start.22 = (f32[4,14,2,256]{3,2,1,0:T(2,128)S(1)}, f32[4,14,2,256]{3,2,1,0:T(2,128)S(1)}, u32[]{:S(2)}, u32[]{:S(2)}) collective-permute-start(f32[4,14,2,256]{3,2,1,0:T(2,128)S(1)} %get-tuple-element.287), channel_id=1, source_target_pairs={{0,7},{1,4},{2,5},{3,6},{4,1},{5,2},{6,3},{7,0},{8,15},{9,12},{10,... | collective-permute-start | bytes 344072 | tf_op jit(solution)/shard_map/ppermute | solution.py:445
  18.5 3.2 %collective-permute-done.22.from_chip = f32[4,14,2,256]{3,2,1,0:T(2,128)S(1)} collective-permute-done((f32[4,14,2,256]{3,2,1,0:T(2,128)S(1)}, f32[4,14,2,256]{3,2,1,0:T(2,128)S(1)}, u32[]{:S(2)}, u32[]{:S(2)}) %collective-permute-start.22) | collective-permute-done | bytes 114720 | tf_op jit(solution)/shard_map/ppermute | solution.py:445
  23.1 4.9 %collective-permute-start.24 = (f32[8,8,256]{2,1,0:T(8,128)S(1)}, f32[8,8,256]{2,1,0:T(8,128)S(1)}, u32[]{:S(2)}, u32[]{:S(2)}) collective-permute-start(f32[8,8,256]{2,1,0:T(8,128)S(1)} %get-tuple-element.206.own), channel_id=1, source_target_pairs={{0,248},{1,249},{2,250},{3,251},{4,252},{5,253},{6,254},{7,255},{8... | collective-permute-start | bytes 196616 | tf_op jit(solution)/shard_map/ppermute | solution.py:445
  28.0 1.6 %collective-permute-done.23.left = f32[8,8,256]{2,1,0:T(8,128)S(1)} collective-permute-done((f32[8,8,256]{2,1,0:T(8,128)S(1)}, f32[8,8,256]{2,1,0:T(8,128)S(1)}, u32[]{:S(2)}, u32[]{:S(2)}) %collective-permute-start.23) | collective-permute-done | bytes 65568 | tf_op jit(solution)/shard_map/ppermute | solution.py:445
  29.6 2.3 %collective-permute-start.25 = (f32[24,8,256]{2,1,0:T(8,128)S(1)}, f32[24,8,256]{2,1,0:T(8,128)S(1)}, u32[]{:S(2)}, u32[]{:S(2)}) collective-permute-start(f32[24,8,256]{2,1,0:T(8,128)S(1)} %constant_dynamic-update-slice_fusion.10), channel_id=1, source_target_pairs={{0,4},{1,5},{2,6},{3,7},{4,0},{5,1},{6,2},{7,3},{8,12},{9,13},{10,... | collective-permute-start | bytes 589832 | tf_op jit(solution)/shard_map/ppermute | solution.py:445
  33.0 4.3 %collective-permute-done.26.from_chip = f32[24,8,256]{2,1,0:T(8,128)S(1)} collective-permute-done((f32[24,8,256]{2,1,0:T(8,128)S(1)}, f32[24,8,256]{2,1,0:T(8,128)S(1)}, u32[]{:S(2)}, u32[]{:S(2)}) %collective-permute-start.26) | collective-permute-done | bytes 196640 | tf_op jit(solution)/shard_map/ppermute | solution.py:445
  37.3 2.4 %shard_map.87 = (f32[256,128]{1,0:T(8,128)S(1)}, f32[8,10,2,16,128]{4,3,2,1,0:T(8,128)S(1)}) custom-call(s32[3]{0:T(128)S(1)} %pad_add_fusion.info, f32[2]{0:T(128)S(1)} %add_convert_fusion.flags, f32[8,8,256]{2,1,0:T(8,128)S(1)} %get-tuple-element.206.own, f32[8,8,256]{2,1,0:T(8,128)S(1)} %collective-permute-done.23.left, ...), custom_call_target="tpu_custom_call" | custom-call | flops 1000000 | bytes 1000000 | tf_op jit(solution)/shard_map/pallas_call | solution.py:407
  39.7 24.4 %all_to_all.22 = f32[256,1,128]{2,1,0:T(1,128)S(1)} all-to-all(f32[256,1,128]{2,1,0:T(1,128)S(1)} %bitcast.92), channel_id=1, replica_groups=mesh['gx'=64,'gy'=4] {'gx','gy'}, dimensions={0} | all-to-all | bytes 262144 | tf_op jit(solution)/shard_map/all_to_all | solution.py:498
  64.8 4.7 %collective-permute-start.28 = (f32[3,2,8,256]{3,2,1,0:T(8,128)S(1)}, f32[3,2,8,256]{3,2,1,0:T(8,128)S(1)}, u32[]{:S(2)}, u32[]{:S(2)}) collective-permute-start(f32[3,2,8,256]{3,2,1,0:T(8,128)S(1)} %slice.704), channel_id=1, source_target_pairs={{0,248},{1,249},{2,250},{3,251},{4,252},{5,253},{6,254},{7,255},{8... | collective-permute-start | bytes 147464 | tf_op jit(solution)/shard_map/ppermute | solution.py:445
  69.5 2.0 %collective-permute-done.27.left = f32[3,4,8,256]{3,2,1,0:T(8,128)S(1)} collective-permute-done((f32[3,4,8,256]{3,2,1,0:T(8,128)S(1)}, f32[3,4,8,256]{3,2,1,0:T(8,128)S(1)}, u32[]{:S(2)}, u32[]{:S(2)}) %collective-permute-start.27) | collective-permute-done | bytes 98336 | tf_op jit(solution)/shard_map/ppermute | solution.py:445
  71.6 2.1 %collective-permute-start.29 = (f32[3,14,2,256]{3,2,1,0:T(2,128)S(1)}, f32[3,14,2,256]{3,2,1,0:T(2,128)S(1)}, u32[]{:S(2)}, u32[]{:S(2)}) collective-permute-start(f32[3,14,2,256]{3,2,1,0:T(2,128)S(1)} %get-tuple-element.354), channel_id=1, source_target_pairs={{0,4},{1,5},{2,6},{3,7},{4,0},{5,1},{6,2},{7,3},{8,12},{9,13},{10,... | collective-permute-start | bytes 258056 | tf_op jit(solution)/shard_map/ppermute | solution.py:445
  74.6 3.3 %collective-permute-done.30.from_chip = f32[3,14,2,256]{3,2,1,0:T(2,128)S(1)} collective-permute-done((f32[3,14,2,256]{3,2,1,0:T(2,128)S(1)}, f32[3,14,2,256]{3,2,1,0:T(2,128)S(1)}, u32[]{:S(2)}, u32[]{:S(2)}) %collective-permute-start.30) | collective-permute-done | bytes 86048 | tf_op jit(solution)/shard_map/ppermute | solution.py:445
  79.4 4.8 %collective-permute-start.32 = (f32[8,8,256]{2,1,0:T(8,128)S(1)}, f32[8,8,256]{2,1,0:T(8,128)S(1)}, u32[]{:S(2)}, u32[]{:S(2)}) collective-permute-start(f32[8,8,256]{2,1,0:T(8,128)S(1)} %get-tuple-element.211.own), channel_id=1, source_target_pairs={{0,248},{1,249},{2,250},{3,251},{4,252},{5,253},{6,254},{7,255},{8... | collective-permute-start | bytes 196616 | tf_op jit(solution)/shard_map/ppermute | solution.py:445
  84.2 1.6 %collective-permute-done.31.left = f32[8,8,256]{2,1,0:T(8,128)S(1)} collective-permute-done((f32[8,8,256]{2,1,0:T(8,128)S(1)}, f32[8,8,256]{2,1,0:T(8,128)S(1)}, u32[]{:S(2)}, u32[]{:S(2)}) %collective-permute-start.31) | collective-permute-done | bytes 65568 | tf_op jit(solution)/shard_map/ppermute | solution.py:445
  85.9 2.3 %collective-permute-start.33 = (f32[24,8,256]{2,1,0:T(8,128)S(1)}, f32[24,8,256]{2,1,0:T(8,128)S(1)}, u32[]{:S(2)}, u32[]{:S(2)}) collective-permute-start(f32[24,8,256]{2,1,0:T(8,128)S(1)} %constant_dynamic-update-slice_fusion.16), channel_id=1, source_target_pairs={{0,4},{1,5},{2,6},{3,7},{4,0},{5,1},{6,2},{7,3},{8,12},{9,13},{10,... | collective-permute-start | bytes 589832 | tf_op jit(solution)/shard_map/ppermute | solution.py:445
  89.2 4.3 %collective-permute-done.34.from_chip = f32[24,8,256]{2,1,0:T(8,128)S(1)} collective-permute-done((f32[24,8,256]{2,1,0:T(8,128)S(1)}, f32[24,8,256]{2,1,0:T(8,128)S(1)}, u32[]{:S(2)}, u32[]{:S(2)}) %collective-permute-start.34) | collective-permute-done | bytes 196640 | tf_op jit(solution)/shard_map/ppermute | solution.py:445
  93.5 3.1 %shard_map.90 = (f32[256,128]{1,0:T(8,128)}, f32[8,10,2,16,128]{4,3,2,1,0:T(8,128)S(1)}) custom-call(s32[3]{0:T(128)S(1)} %pad_add_fusion.info, f32[2]{0:T(128)S(1)} %add_convert_fusion.flags, f32[8,8,256]{2,1,0:T(8,128)S(1)} %get-tuple-element.211.own, f32[8,8,256]{2,1,0:T(8,128)S(1)} %collective-permute-done.31.left, ...), custom_call_target="tpu_custom_call" | custom-call | flops 1000000 | bytes 1000000 | tf_op jit(solution)/shard_map/pallas_call | solution.py:407
  96.6 8.2 %all-to-all-start.1 = ((f32[256,1,128]{2,1,0:T(1,128)}), f32[256,1,128]{2,1,0:T(1,128)S(1)}, u32[]{:S(2)}, u32[]{:S(2)}) async-start(f32[256,1,128]{2,1,0:T(1,128)} %bitcast.40), calls=%async_computation.1 | async-start | bytes 262144 | tf_op jit(solution)/shard_map/all_to_all | solution.py:498
  104.8 12.7 %all-to-all-done.1 = f32[256,1,128]{2,1,0:T(1,128)S(1)} async-done(((f32[256,1,128]{2,1,0:T(1,128)}), f32[256,1,128]{2,1,0:T(1,128)S(1)}, u32[]{:S(2)}, u32[]{:S(2)}) %all-to-all-start.1) | async-done | bytes 131104 | tf_op jit(solution)/shard_map/all_to_all | solution.py:498
  117.5 1.5 %shard_map.91 = (s32[1]{0:T(128)}, f32[4,4,8,256]{3,2,1,0:T(8,128)S(1)}, f32[4,4,8,256]{3,2,1,0:T(8,128)S(1)}) custom-call(s32[3]{0:T(128)S(1)} %pad_add_fusion.info, f32[256,128]{1,0:T(8,128)S(1)} %bitcast.90, f32[16,128]{1,0:T(8,128)S(1)} %copy-done.1, f32[16,128]{1,0:T(8,128)S(1)} %copy-done.2, f32[8,16,128]{2,1,0:T(8,128)S(1)} %copy-done, ...), custom_call_target="tpu_custom_call" | custom-call | flops 1000000 | bytes 1000000 | tf_op jit(solution)/shard_map/pallas_call | solution.py:407
  119.7 3.1 %conditional.1 = (f32[3,4,16,256]{3,2,1,0:T(8,128)}, f32[4,16,256]{2,1,0:T(8,128)}) conditional(s32[]{:T(128)} %bitcast.42, (s32[2]{0:T(128)S(1)}, s32[4,16,256]{2,1,0:T(8,128)S(1)}, f32[8,3]{0,1:T(4,128)S(1)}, f32[3,4,16,256]{3,2,1,0:T(8,128)}) %tuple.186, (pred[]{:T(512)}, f32[4,4,8,256]{3,2,1,0:T(8,128)S(1)}, f32[4,4,8,256]{3,2,1,0:T(8,128)S(1)}) %tuple.42), branch_computations={%region_0.9_spmd, %region_9.10_spmd} | conditional | flops 3744999 | bytes 12867730 | solution.py:520
  (78 shorter events, 13.7 us)
Async XLA Ops:
  1.6 14.6 %copy-start.4 = (f32[3,4,16,256]{3,2,1,0:T(8,128)}, f32[3,4,16,256]{3,2,1,0:T(8,128)S(1)}, u32[]{:S(2)}) copy-start(f32[3,4,16,256]{3,2,1,0:T(8,128)S(1)} %copy.67) | copy-start | bytes 589828
  2.5 9.4 %collective-permute-start.18 = (f32[13,16,256]{2,1,0:T(8,128)S(1)}, f32[13,16,256]{2,1,0:T(8,128)S(1)}, u32[]{:S(2)}, u32[]{:S(2)}) collective-permute-start(f32[13,16,256]{2,1,0:T(8,128)S(1)} %pad_maximum_fusion.10), channel_id=1, source_target_pairs={{0,252},{1,253},{2,254},{3,255},{4,8},{5,9},{6,10},{7,11},{8,4},{9... | collective-permute-start | bytes 638984 | tf_op jit(solution)/shard_map/ppermute | solution.py:445
  5.2 10.0 %collective-permute-start.20 = (f32[16,8,256]{2,1,0:T(8,128)S(1)}, f32[16,8,256]{2,1,0:T(8,128)S(1)}, u32[]{:S(2)}, u32[]{:S(2)}) collective-permute-start(f32[16,8,256]{2,1,0:T(8,128)S(1)} %broadcast_select_fusion.8), channel_id=1, source_target_pairs={{0,4},{1,5},{2,6},{3,7},{4,0},{5,1},{6,2},{7,3},{8,12},{9,13},{10,... | collective-permute-start | bytes 393224 | tf_op jit(solution)/shard_map/ppermute | solution.py:445
  12.0 4.2 %collective-permute-start.19 = (f32[13,8,256]{2,1,0:T(8,128)S(1)}, f32[13,8,256]{2,1,0:T(8,128)S(1)}, u32[]{:S(2)}, u32[]{:S(2)}) collective-permute-start(f32[13,8,256]{2,1,0:T(8,128)S(1)} %slice_select_fusion), channel_id=1, source_target_pairs={{0,4},{1,5},{2,6},{3,7},{4,0},{5,1},{6,2},{7,3},{8,12},{9,13},{10,... | collective-permute-start | bytes 319496 | tf_op jit(solution)/shard_map/ppermute | solution.py:445
  16.5 47.6 %copy-start = (f32[8,16,128]{2,1,0:T(8,128)S(1)}, f32[8,16,128]{2,1,0:T(8,128)}, u32[]{:S(2)}) copy-start(f32[8,16,128]{2,1,0:T(8,128)} %constant.260.clone.coef) | copy-start | bytes 196612
  16.5 47.6 %copy-start.1 = (f32[16,128]{1,0:T(8,128)S(1)}, f32[16,128]{1,0:T(8,128)}, u32[]{:S(2)}) copy-start(f32[16,128]{1,0:T(8,128)} %constant.258.clone.weight_map) | copy-start | bytes 24580
  16.5 47.6 %copy-start.2 = (f32[16,128]{1,0:T(8,128)S(1)}, f32[16,128]{1,0:T(8,128)}, u32[]{:S(2)}) copy-start(f32[16,128]{1,0:T(8,128)} %constant.259.clone.node) | copy-start | bytes 24580
  16.5 1.9 %collective-permute-start.21 = (f32[4,14,2,256]{3,2,1,0:T(2,128)S(1)}, f32[4,14,2,256]{3,2,1,0:T(2,128)S(1)}, u32[]{:S(2)}, u32[]{:S(2)}) collective-permute-start(f32[4,14,2,256]{3,2,1,0:T(2,128)S(1)} %broadcast_select_fusion.3), channel_id=1, source_target_pairs={{0,4},{1,5},{2,6},{3,7},{4,0},{5,1},{6,2},{7,3},{8,12},{9,13},{10,... | collective-permute-start | bytes 344072 | tf_op jit(solution)/shard_map/ppermute | solution.py:445
  17.0 4.6 %collective-permute-start.22 = (f32[4,14,2,256]{3,2,1,0:T(2,128)S(1)}, f32[4,14,2,256]{3,2,1,0:T(2,128)S(1)}, u32[]{:S(2)}, u32[]{:S(2)}) collective-permute-start(f32[4,14,2,256]{3,2,1,0:T(2,128)S(1)} %get-tuple-element.287), channel_id=1, source_target_pairs={{0,7},{1,4},{2,5},{3,6},{4,1},{5,2},{6,3},{7,0},{8,15},{9,12},{10,... | collective-permute-start | bytes 344072 | tf_op jit(solution)/shard_map/ppermute | solution.py:445
  23.0 6.5 %collective-permute-start.23 = (f32[8,8,256]{2,1,0:T(8,128)S(1)}, f32[8,8,256]{2,1,0:T(8,128)S(1)}, u32[]{:S(2)}, u32[]{:S(2)}) collective-permute-start(f32[8,8,256]{2,1,0:T(8,128)S(1)} %get-tuple-element.206.own), channel_id=1, source_target_pairs={{0,8},{1,9},{2,10},{3,11},{4,12},{5,13},{6,14},{7,15},{8,16},{9,17... | collective-permute-start | bytes 196616 | tf_op jit(solution)/shard_map/ppermute | solution.py:445
  23.1 6.5 %collective-permute-start.24 = (f32[8,8,256]{2,1,0:T(8,128)S(1)}, f32[8,8,256]{2,1,0:T(8,128)S(1)}, u32[]{:S(2)}, u32[]{:S(2)}) collective-permute-start(f32[8,8,256]{2,1,0:T(8,128)S(1)} %get-tuple-element.206.own), channel_id=1, source_target_pairs={{0,248},{1,249},{2,250},{3,251},{4,252},{5,253},{6,254},{7,255},{8... | collective-permute-start | bytes 196616 | tf_op jit(solution)/shard_map/ppermute | solution.py:445
  29.6 3.4 %collective-permute-start.25 = (f32[24,8,256]{2,1,0:T(8,128)S(1)}, f32[24,8,256]{2,1,0:T(8,128)S(1)}, u32[]{:S(2)}, u32[]{:S(2)}) collective-permute-start(f32[24,8,256]{2,1,0:T(8,128)S(1)} %constant_dynamic-update-slice_fusion.10), channel_id=1, source_target_pairs={{0,4},{1,5},{2,6},{3,7},{4,0},{5,1},{6,2},{7,3},{8,12},{9,13},{10,... | collective-permute-start | bytes 589832 | tf_op jit(solution)/shard_map/ppermute | solution.py:445
  31.9 5.4 %collective-permute-start.26 = (f32[24,8,256]{2,1,0:T(8,128)S(1)}, f32[24,8,256]{2,1,0:T(8,128)S(1)}, u32[]{:S(2)}, u32[]{:S(2)}) collective-permute-start(f32[24,8,256]{2,1,0:T(8,128)S(1)} %constant_dynamic-update-slice_fusion.10), channel_id=1, source_target_pairs={{0,7},{1,4},{2,5},{3,6},{4,1},{5,2},{6,3},{7,0},{8,15},{9,12},{10,... | collective-permute-start | bytes 589832 | tf_op jit(solution)/shard_map/ppermute | solution.py:445
  64.6 6.9 %collective-permute-start.27 = (f32[3,4,8,256]{3,2,1,0:T(8,128)S(1)}, f32[3,4,8,256]{3,2,1,0:T(8,128)S(1)}, u32[]{:S(2)}, u32[]{:S(2)}) collective-permute-start(f32[3,4,8,256]{3,2,1,0:T(8,128)S(1)} %slice.703), channel_id=1, source_target_pairs={{0,8},{1,9},{2,10},{3,11},{4,12},{5,13},{6,14},{7,15},{8,16},{9,17... | collective-permute-start | bytes 294920 | tf_op jit(solution)/shard_map/ppermute | solution.py:445
  64.8 6.7 %collective-permute-start.28 = (f32[3,2,8,256]{3,2,1,0:T(8,128)S(1)}, f32[3,2,8,256]{3,2,1,0:T(8,128)S(1)}, u32[]{:S(2)}, u32[]{:S(2)}) collective-permute-start(f32[3,2,8,256]{3,2,1,0:T(8,128)S(1)} %slice.704), channel_id=1, source_target_pairs={{0,248},{1,249},{2,250},{3,251},{4,252},{5,253},{6,254},{7,255},{8... | collective-permute-start | bytes 147464 | tf_op jit(solution)/shard_map/ppermute | solution.py:445
  71.6 3.1 %collective-permute-start.29 = (f32[3,14,2,256]{3,2,1,0:T(2,128)S(1)}, f32[3,14,2,256]{3,2,1,0:T(2,128)S(1)}, u32[]{:S(2)}, u32[]{:S(2)}) collective-permute-start(f32[3,14,2,256]{3,2,1,0:T(2,128)S(1)} %get-tuple-element.354), channel_id=1, source_target_pairs={{0,4},{1,5},{2,6},{3,7},{4,0},{5,1},{6,2},{7,3},{8,12},{9,13},{10,... | collective-permute-start | bytes 258056 | tf_op jit(solution)/shard_map/ppermute | solution.py:445
  73.7 4.2 %collective-permute-start.30 = (f32[3,14,2,256]{3,2,1,0:T(2,128)S(1)}, f32[3,14,2,256]{3,2,1,0:T(2,128)S(1)}, u32[]{:S(2)}, u32[]{:S(2)}) collective-permute-start(f32[3,14,2,256]{3,2,1,0:T(2,128)S(1)} %get-tuple-element.353), channel_id=1, source_target_pairs={{0,7},{1,4},{2,5},{3,6},{4,1},{5,2},{6,3},{7,0},{8,15},{9,12},{10,... | collective-permute-start | bytes 258056 | tf_op jit(solution)/shard_map/ppermute | solution.py:445
  79.3 6.5 %collective-permute-start.31 = (f32[8,8,256]{2,1,0:T(8,128)S(1)}, f32[8,8,256]{2,1,0:T(8,128)S(1)}, u32[]{:S(2)}, u32[]{:S(2)}) collective-permute-start(f32[8,8,256]{2,1,0:T(8,128)S(1)} %get-tuple-element.211.own), channel_id=1, source_target_pairs={{0,8},{1,9},{2,10},{3,11},{4,12},{5,13},{6,14},{7,15},{8,16},{9,17... | collective-permute-start | bytes 196616 | tf_op jit(solution)/shard_map/ppermute | solution.py:445
  79.4 6.4 %collective-permute-start.32 = (f32[8,8,256]{2,1,0:T(8,128)S(1)}, f32[8,8,256]{2,1,0:T(8,128)S(1)}, u32[]{:S(2)}, u32[]{:S(2)}) collective-permute-start(f32[8,8,256]{2,1,0:T(8,128)S(1)} %get-tuple-element.211.own), channel_id=1, source_target_pairs={{0,248},{1,249},{2,250},{3,251},{4,252},{5,253},{6,254},{7,255},{8... | collective-permute-start | bytes 196616 | tf_op jit(solution)/shard_map/ppermute | solution.py:445
  85.9 33.8 %copy-start.5 = (s32[4,16,256]{2,1,0:T(8,128)S(1)}, s32[4,16,256]{2,1,0:T(8,128)}, u32[]{:S(2)}) copy-start(s32[4,16,256]{2,1,0:T(8,128)} %param.14) | copy-start | bytes 196612
  85.9 3.3 %collective-permute-start.33 = (f32[24,8,256]{2,1,0:T(8,128)S(1)}, f32[24,8,256]{2,1,0:T(8,128)S(1)}, u32[]{:S(2)}, u32[]{:S(2)}) collective-permute-start(f32[24,8,256]{2,1,0:T(8,128)S(1)} %constant_dynamic-update-slice_fusion.16), channel_id=1, source_target_pairs={{0,4},{1,5},{2,6},{3,7},{4,0},{5,1},{6,2},{7,3},{8,12},{9,13},{10,... | collective-permute-start | bytes 589832 | tf_op jit(solution)/shard_map/ppermute | solution.py:445
  88.1 5.4 %collective-permute-start.34 = (f32[24,8,256]{2,1,0:T(8,128)S(1)}, f32[24,8,256]{2,1,0:T(8,128)S(1)}, u32[]{:S(2)}, u32[]{:S(2)}) collective-permute-start(f32[24,8,256]{2,1,0:T(8,128)S(1)} %constant_dynamic-update-slice_fusion.16), channel_id=1, source_target_pairs={{0,7},{1,4},{2,5},{3,6},{4,1},{5,2},{6,3},{7,0},{8,15},{9,12},{10,... | collective-permute-start | bytes 589832 | tf_op jit(solution)/shard_map/ppermute | solution.py:445
  96.6 20.9 %all-to-all-start.1 = ((f32[256,1,128]{2,1,0:T(1,128)}), f32[256,1,128]{2,1,0:T(1,128)S(1)}, u32[]{:S(2)}, u32[]{:S(2)}) async-start(f32[256,1,128]{2,1,0:T(1,128)} %bitcast.40), calls=%async_computation.1 | async-start | bytes 262144 | tf_op jit(solution)/shard_map/all_to_all | solution.py:498
  119.7 1.8 %collective-permute-start = (f32[4,4,8,256]{3,2,1,0:T(8,128)S(1)}, f32[4,4,8,256]{3,2,1,0:T(8,128)S(1)}, u32[]{:S(2)}, u32[]{:S(2)}) collective-permute-start(f32[4,4,8,256]{3,2,1,0:T(8,128)S(1)} %get-tuple-element.190), channel_id=1, source_target_pairs={{0,4},{1,5},{2,6},{3,7},{4,0},{5,1},{6,2},{7,3},{8,12},{9,13},{10,... | collective-permute-start | bytes 393224 | tf_op jit(solution)/shard_map/cond/branch_1_fun/ppermute | solution.py:445
  (2 other events, 22.3 us)

commit v3 on v2

--- a/solution.py
+++ b/solution.py
@@ -196,8 +196,8 @@
             put(c, i + 4, own[c, i])
         for i in range(2):
             put(c, i + 12, right[c, i])
-        for i in range(14):
-            a, b = from_core[c, i], from_chip[c, i]
+        for i in range(1, 13):
+            a, b = from_core[c, i - 1], from_chip[c, i - 1]
             up = jnp.where(core == 0, b, a) * up_flag
             down = jnp.where(core == 0, a, b) * down_flag
             for h in range(2):
@@ -264,7 +264,8 @@
     scale = (flags[0], 1.0, flags[1])
 
     for i in range(24):
-        a, b = from_core[i], from_chip[i]
+        k = min(max(i - 1, 0), 21)
+        a, b = from_core[k], from_chip[k]
         up, down = jnp.where(core == 0, b, a) * scale[0], jnp.where(core == 0, a, b) * scale[2]
         middle = (left, own, right)[i // 8][i % 8]
         for h in range(2):
@@ -347,53 +348,66 @@
     return terms, good
 
 
-def correct(terms, near, bodied, emit, p):
-    def combine(i, _):
+def combine(terms, near, p):
+    for i in range(10):
         for h in range(2):
             for r in (0, 8):
                 total = terms[0] * near[0, i, h, r : r + 8]
                 for j in range(1, PASSES):
                     total = total + terms[j] * near[j, i, h, r : r + 8]
                 p[i, h, r : r + 8] = total
-        return 0
-
-    for i in range(10):
-        combine(i, 0)
-    for i in range(8):
-        own = [p[i + 1, h, 1:9] for h in range(2)]
-        beside = z_pair(*own)
-        for h in range(2):
-            lanes = slice(h * HALF, (h + 1) * HALF)
-            emit(0, i, lanes, bodied[0, i, :, lanes] - 0.5 * (p[i + 2, h, 1:9] - p[i, h, 1:9]))
-            emit(1, i, lanes, bodied[1, i, :, lanes] - 0.5 * (p[i + 1, h, 2:10] - p[i + 1, h, 0:8]))
-            emit(2, i, lanes, bodied[2, i, :, lanes] - 0.5 * (beside[h][0] - beside[h][1]))
-            emit(3, i, lanes, own[h])
+
+
+def corrected(i, bodied, p, put):
+    own = [p[i + 1, h, 1:9] for h in range(2)]
+    beside = z_pair(*own)
+    for h in range(2):
+        lanes = slice(h * HALF, (h + 1) * HALF)
+        put(0, lanes, bodied[0, i, :, lanes] - 0.5 * (p[i + 2, h, 1:9] - p[i, h, 1:9]))
+        put(1, lanes, bodied[1, i, :, lanes] - 0.5 * (p[i + 1, h, 2:10] - p[i + 1, h, 0:8]))
+        put(2, lanes, bodied[2, i, :, lanes] - 0.5 * (beside[h][0] - beside[h][1]))
+        put(3, lanes, own[h])
 
 
 def inner_step_kernel(moments, weight_map, node, coef, near, bodied, good_out, velocity, p):
     terms, good = lengths(moments, weight_map, node, coef)
     good_out[...] = good
-
-    def emit(c, i, lanes, value):
-        if c < 3:
-            velocity[c, i, :, lanes] = value
-
-    correct(terms, near, bodied, emit, p)
-
-
-def last_step_kernel(info, moments, weight_map, node, coef, near, bodied, good_in, good_out, kept, sent, p, fields):
+    combine(terms, near, p)
+    for i in range(8):
+
+        def put(c, lanes, value, i=i):
+            if c < 3:
+                velocity[c, i, :, lanes] = value
+
+        corrected(i, bodied, p, put)
+
+
+def last_step_kernel(info, moments, weight_map, node, coef, near, bodied, good_in, good_out, kept, sent, p):
     terms, good = lengths(moments, weight_map, node, coef)
     good_out[0] = (jnp.min(good * good_in[...]) > 0.5).astype(jnp.int32)
     core = info[0]
-
-    def emit(c, i, lanes, value):
-        fields[c, i, :, lanes] = value
-
-    correct(terms, near, bodied, emit, p)
+    combine(terms, near, p)
+    for i in range(4):
+        for out, start in ((sent, 4 * (1 - core)), (kept, 4 * core)):
+
+            def put(c, lanes, value, i=i, out=out):
+                out[c, i, :, lanes] = value
+
+            corrected(start + i, bodied, p, put)
+
+
+def place_kernel(info, kept, got, velocity, pressure):
+    first = info[0] == 0
     for i in range(4):
         for c in range(4):
-            kept[c, i] = fields[c, 4 * core + i]
-            sent[c, i] = fields[c, 4 * (1 - core) + i]
+            a, b = kept[c, i], got[c, i]
+            low, high = jnp.where(first, a, b), jnp.where(first, b, a)
+            if c < 3:
+                velocity[c, i, 0:8] = low
+                velocity[c, i, 8:16] = high
+            else:
+                pressure[i, 0:8] = low
+                pressure[i, 8:16] = high
 
 
 SMEM = pl.BlockSpec(memory_space=pltpu.SMEM)
@@ -434,8 +448,8 @@
     return {
         "core": pairs(lambda chip, core, y: (chip, 1 - core, y)),
         "facing": pairs(lambda chip, core, y: (chip + (1 if core else -1), 1 - core, y)),
-        "right": pairs(lambda chip, core, y: (chip + 1, core, y)),
-        "left": pairs(lambda chip, core, y: (chip - 1, core, y)),
+        "inner": pairs(lambda chip, core, y: (chip + (1 if chip % 2 == 0 else -1), core, y)),
+        "outer": pairs(lambda chip, core, y: (chip + (-1 if chip % 2 == 0 else 1), core, y)),
         "across": pairs(across),
     }
 
@@ -450,6 +464,13 @@
     weight_map, node, coef = (jnp.asarray(a) for a in tables())
     first = core == 0
     pick = lambda a, b: jnp.where(first, a, b)
+    even = (lax.axis_index("gx") // 2) % 2 == 0
+
+    def beside(to_left, to_right):
+        outer = send(jnp.where(even, to_left, to_right), "outer")
+        inner = send(jnp.where(even, to_right, to_left), "inner")
+        return jnp.where(even, outer, inner), jnp.where(even, inner, outer)
+
 
     cells = cell_swimmer.astype(jnp.float32)
     rows = velocity.reshape(12, 16, NZ)
@@ -468,13 +489,13 @@
 
     for step in range(STEPS):
         if step:
-            left = send(own[:, 4:8], "right")
-            right = send(own[:, 0:2], "left")
+            left, right = beside(own[:, 0:4], own[:, 4:8])
+            right = right[:, 0:2]
         joined = jnp.concatenate([left, own, right], axis=1)
         if not step:
-            spare = jnp.concatenate([cell, cell[0:4]], axis=0)
+            spare = jnp.concatenate([cell[0:1], cell, cell[0:3]], axis=0)
             joined = jnp.concatenate([joined, spare[None]], axis=0)
-        top, bottom = joined[:, :, 0:2], joined[:, :, 6:8]
+        top, bottom = joined[:, 1:13, 0:2], joined[:, 1:13, 6:8]
         from_core, from_chip = send(pick(bottom, top), "core"), send(pick(top, bottom), "across")
         if not step:
             cell_core, cell_chip = from_core[3, 0:10], from_chip[3, 0:10]
@@ -485,9 +506,8 @@
             [(3, 8, 8, NZ), (8, 8, NZ)],
             [(3, 14, 2, 24, HALF), (10, 2, 24, HALF), (3, 10, 2, 16, HALF)],
         )
-        s_left = send(source, "right")
-        s_right = send(source, "left")
-        column = jnp.concatenate([s_left, source, s_right], axis=0)
+        s_left, s_right = beside(source, source)
+        column = jnp.concatenate([s_left[1:], source, s_right[:7]], axis=0)
         moments, near = call(
             powers_kernel,
             (info, flags, source, s_left, s_right, send(column, "core"), send(column, "across")),
@@ -505,14 +525,13 @@
                 (info,) + shared + (good,),
                 1,
                 [(4, 4, 8, NZ), (4, 4, 8, NZ)],
-                [(10, 2, 16, HALF), (4, 8, 8, NZ)],
+                [(10, 2, 16, HALF)],
                 flags_out=1,
             )
 
     def finish(_):
         got = send(sent, "core")
-        fields = jnp.concatenate([pick(kept, got), pick(got, kept)], axis=2)
-        return (fields[0:3], fields[3])
+        return tuple(call(place_kernel, (info, kept, got), 1, [(3, 4, 16, NZ), (4, 16, NZ)], []))
 
     def again(_):
         return plain(velocity, cell_swimmer, swimmer_speed, recentre_cols)

time: 123 us -> 118 us (0.959)
  starting transfers between devices: 45 us -> 35.7 us
  waiting for transfers between devices: 37.6 us -> 46.1 us
  blocking collectives: 24.4 us -> 20.4 us
  other arithmetic: 2.73 us -> 1.44 us
    ppermute x18, waiting for transfers between devices: 24.9 us -> 33.3 us  [body(): send = lambda value, name: lax.ppermute(value, AXES, route[name])]
    ppermute x18, starting transfers between devices: 36.9 us -> 29.7 us  [body(): send = lambda value, name: lax.ppermute(value, AXES, route[name])]
    all_to_all x1, blocking collectives: 24.4 us -> 20.4 us  [body(): moments = lax.all_to_all(moments, AXES, 0, 0)]
    all_to_all x1, starting transfers between devices: 8.19 us -> 6.03 us  [body(): moments = lax.all_to_all(moments, AXES, 0, 0)]
    pallas_call x6 -> x7, Pallas kernels: 10.3 us -> 11.5 us  [call(): pl.pallas_call(kernel, in_specs=[SMEM] * smem + [VMEM] * (len(args) - sme...]
  transfers between devices with their start and end apart: 19 -> 19, of which waited for: 13 -> 15; matrix products, arithmetic and copies ran while one was open for 0% -> 0% of each run, Pallas kernels for 0% -> 0%
where the time goes in v3:
time: 118 us
  waiting for transfers between devices  46.1 us (39%)
  starting transfers between devices  35.7 us (30%)
  blocking collectives  20.4 us (17%)
  Pallas kernels  11.5 us (10%)
  between operations  1.63 us (1%)
  other arithmetic  1.44 us (1%)
    ppermute x18, waiting for transfers between devices, body(): send = lambda value, name: lax.ppermute(value, AXES, route[name])  33.3 us
    ppermute x18, starting transfers between devices, body(): send = lambda value, name: lax.ppermute(value, AXES, route[name])  29.7 us
    all_to_all x1, blocking collectives, body(): moments = lax.all_to_all(moments, AXES, 0, 0)  20.4 us
    all_to_all x1, waiting for transfers between devices, body(): moments = lax.all_to_all(moments, AXES, 0, 0)  12.9 us
    pallas_call x7, Pallas kernels, call(): pl.pallas_call(kernel, in_specs=[SMEM] * smem + [VMEM] * (len(args) - sme...  11.5 us
    all_to_all x1, starting transfers between devices, body(): moments = lax.all_to_all(moments, AXES, 0, 0)  6.03 us
  transfers between devices with their start and end apart: 19, of which 15 were waited for; matrix products, arithmetic and copies ran while one was open for 0% of the time, Pallas kernels for 0%

profile of v3, /device:TPU:1, one launch (start us, length us, event | category | flops | bytes accessed | tf_op | source)
XLA Modules:
  0.0 118.0 jit_solution(6474574561025002871)
XLA Ops:
  2.5 2.7 %collective-permute-start.18 = (f32[13,16,256]{2,1,0:T(8,128)S(1)}, f32[13,16,256]{2,1,0:T(8,128)S(1)}, u32[]{:S(2)}, u32[]{:S(2)}) collective-permute-start(f32[13,16,256]{2,1,0:T(8,128)S(1)} %pad_maximum_fusion.9), channel_id=1, source_target_pairs={{0,252},{1,253},{2,254},{3,255},{4,8},{5,9},{6,10},{7,11},{8,4},{9... | collective-permute-start | bytes 638984 | tf_op jit(solution)/shard_map/ppermute | solution.py:459
  5.2 6.5 %collective-permute-start.20 = (f32[16,8,256]{2,1,0:T(8,128)S(1)}, f32[16,8,256]{2,1,0:T(8,128)S(1)}, u32[]{:S(2)}, u32[]{:S(2)}) collective-permute-start(f32[16,8,256]{2,1,0:T(8,128)S(1)} %broadcast_select_fusion.6), channel_id=1, source_target_pairs={{0,4},{1,5},{2,6},{3,7},{4,0},{5,1},{6,2},{7,3},{8,12},{9,13},{10,... | collective-permute-start | bytes 393224 | tf_op jit(solution)/shard_map/ppermute | solution.py:459
  12.8 2.4 %collective-permute-start.19 = (f32[13,8,256]{2,1,0:T(8,128)S(1)}, f32[13,8,256]{2,1,0:T(8,128)S(1)}, u32[]{:S(2)}, u32[]{:S(2)}) collective-permute-start(f32[13,8,256]{2,1,0:T(8,128)S(1)} %slice_select_fusion), channel_id=1, source_target_pairs={{0,4},{1,5},{2,6},{3,7},{4,0},{5,1},{6,2},{7,3},{8,12},{9,13},{10,... | collective-permute-start | bytes 319496 | tf_op jit(solution)/shard_map/ppermute | solution.py:459
  18.3 3.0 %collective-permute-done.22.from_chip = f32[4,12,2,256]{3,2,1,0:T(2,128)S(1)} collective-permute-done((f32[4,12,2,256]{3,2,1,0:T(2,128)S(1)}, f32[4,12,2,256]{3,2,1,0:T(2,128)S(1)}, u32[]{:S(2)}, u32[]{:S(2)}) %collective-permute-start.22) | collective-permute-done | bytes 98336 | tf_op jit(solution)/shard_map/ppermute | solution.py:459
  21.2 1.4 %shard_map.86 = (f32[3,8,8,256]{3,2,1,0:T(8,128)S(1)}, f32[8,8,256]{2,1,0:T(8,128)S(1)}) custom-call(s32[3]{0:T(128)S(1)} %pad_add_fusion.info, f32[2]{0:T(128)S(1)} %add_convert_fusion.flags, f32[8,3]{1,0:T(8,128)S(1)} %copy.23.speed, f32[3,4,8,256]{3,2,1,0:T(8,128)S(1)} %bitcast.93, f32[3,8,8,256]{3,2,1,0:T(8,128)S(1)} %pad_maximum_fusion.10.own, ...), custom_call_target="tpu_custom_call" | custom-call | flops 1000000 | bytes 1000000 | tf_op jit(solution)/shard_map/pallas_call | solution.py:421
  22.6 4.9 %collective-permute-start.23 = (f32[8,8,256]{2,1,0:T(8,128)S(1)}, f32[8,8,256]{2,1,0:T(8,128)S(1)}, u32[]{:S(2)}, u32[]{:S(2)}) collective-permute-start(f32[8,8,256]{2,1,0:T(8,128)S(1)} %get-tuple-element.206.own), channel_id=1, source_target_pairs={{0,248},{1,249},{2,250},{3,251},{4,252},{5,253},{6,254},{7,255},{8... | collective-permute-start | bytes 196616 | tf_op jit(solution)/shard_map/ppermute | solution.py:459
  27.5 1.7 %collective-permute-done.23 = f32[8,8,256]{2,1,0:T(8,128)S(1)} collective-permute-done((f32[8,8,256]{2,1,0:T(8,128)S(1)}, f32[8,8,256]{2,1,0:T(8,128)S(1)}, u32[]{:S(2)}, u32[]{:S(2)}) %collective-permute-start.23) | collective-permute-done | bytes 65568 | tf_op jit(solution)/shard_map/ppermute | solution.py:459
  29.2 1.8 %collective-permute-done.24 = f32[8,8,256]{2,1,0:T(8,128)S(1)} collective-permute-done((f32[8,8,256]{2,1,0:T(8,128)S(1)}, f32[8,8,256]{2,1,0:T(8,128)S(1)}, u32[]{:S(2)}, u32[]{:S(2)}) %collective-permute-start.24) | collective-permute-done | bytes 65568 | tf_op jit(solution)/shard_map/ppermute | solution.py:459
  31.0 2.5 %collective-permute-start.25 = (f32[22,8,256]{2,1,0:T(8,128)S(1)}, f32[22,8,256]{2,1,0:T(8,128)S(1)}, u32[]{:S(2)}, u32[]{:S(2)}) collective-permute-start(f32[22,8,256]{2,1,0:T(8,128)S(1)} %pad_maximum_fusion.11), channel_id=1, source_target_pairs={{0,4},{1,5},{2,6},{3,7},{4,0},{5,1},{6,2},{7,3},{8,12},{9,13},{10,... | collective-permute-start | bytes 540680 | tf_op jit(solution)/shard_map/ppermute | solution.py:459
  34.5 4.2 %collective-permute-done.26.from_chip = f32[22,8,256]{2,1,0:T(8,128)S(1)} collective-permute-done((f32[22,8,256]{2,1,0:T(8,128)S(1)}, f32[22,8,256]{2,1,0:T(8,128)S(1)}, u32[]{:S(2)}, u32[]{:S(2)}) %collective-permute-start.26) | collective-permute-done | bytes 180256 | tf_op jit(solution)/shard_map/ppermute | solution.py:459
  38.7 2.4 %shard_map.87 = (f32[256,128]{1,0:T(8,128)S(1)}, f32[8,10,2,16,128]{4,3,2,1,0:T(8,128)S(1)}) custom-call(s32[3]{0:T(128)S(1)} %pad_add_fusion.info, f32[2]{0:T(128)S(1)} %add_convert_fusion.flags, f32[8,8,256]{2,1,0:T(8,128)S(1)} %get-tuple-element.206.own, f32[8,8,256]{2,1,0:T(8,128)S(1)} %get-tuple-element.361.left, ...), custom_call_target="tpu_custom_call" | custom-call | flops 1000000 | bytes 1000000 | tf_op jit(solution)/shard_map/pallas_call | solution.py:421
  41.2 20.4 %all_to_all.22 = f32[256,1,128]{2,1,0:T(1,128)S(1)} all-to-all(f32[256,1,128]{2,1,0:T(1,128)S(1)} %bitcast.96), channel_id=1, replica_groups=mesh['gx'=64,'gy'=4] {'gx','gy'}, dimensions={0} | all-to-all | bytes 262144 | tf_op jit(solution)/shard_map/all_to_all | solution.py:518
  63.2 5.8 %collective-permute-done.27 = f32[3,4,8,256]{3,2,1,0:T(8,128)S(1)} collective-permute-done((f32[3,4,8,256]{3,2,1,0:T(8,128)S(1)}, f32[3,4,8,256]{3,2,1,0:T(8,128)S(1)}, u32[]{:S(2)}, u32[]{:S(2)}) %collective-permute-start.27) | collective-permute-done | bytes 98336 | tf_op jit(solution)/shard_map/ppermute | solution.py:459
  69.1 2.0 %collective-permute-start.29 = (f32[3,12,2,256]{3,2,1,0:T(2,128)S(1)}, f32[3,12,2,256]{3,2,1,0:T(2,128)S(1)}, u32[]{:S(2)}, u32[]{:S(2)}) collective-permute-start(f32[3,12,2,256]{3,2,1,0:T(2,128)S(1)} %bitcast.111), channel_id=1, source_target_pairs={{0,4},{1,5},{2,6},{3,7},{4,0},{5,1},{6,2},{7,3},{8,12},{9,13},{10,... | collective-permute-start | bytes 221192 | tf_op jit(solution)/shard_map/ppermute | solution.py:459
  72.0 2.9 %collective-permute-done.30.from_chip = f32[3,12,2,256]{3,2,1,0:T(2,128)S(1)} collective-permute-done((f32[3,12,2,256]{3,2,1,0:T(2,128)S(1)}, f32[3,12,2,256]{3,2,1,0:T(2,128)S(1)}, u32[]{:S(2)}, u32[]{:S(2)}) %collective-permute-start.30) | collective-permute-done | bytes 73760 | tf_op jit(solution)/shard_map/ppermute | solution.py:459
  76.2 1.8 %collective-permute-start.31 = (f32[8,8,256]{2,1,0:T(8,128)S(1)}, f32[8,8,256]{2,1,0:T(8,128)S(1)}, u32[]{:S(2)}, u32[]{:S(2)}) collective-permute-start(f32[8,8,256]{2,1,0:T(8,128)S(1)} %get-tuple-element.211.own), channel_id=1, source_target_pairs={{0,248},{1,249},{2,250},{3,251},{4,252},{5,253},{6,254},{7,255},{8... | collective-permute-start | bytes 196616 | tf_op jit(solution)/shard_map/ppermute | solution.py:459
  78.1 4.7 %collective-permute-done.31 = f32[8,8,256]{2,1,0:T(8,128)S(1)} collective-permute-done((f32[8,8,256]{2,1,0:T(8,128)S(1)}, f32[8,8,256]{2,1,0:T(8,128)S(1)}, u32[]{:S(2)}, u32[]{:S(2)}) %collective-permute-start.31) | collective-permute-done | bytes 65568 | tf_op jit(solution)/shard_map/ppermute | solution.py:459
  82.8 2.7 %collective-permute-start.33 = (f32[22,8,256]{2,1,0:T(8,128)S(1)}, f32[22,8,256]{2,1,0:T(8,128)S(1)}, u32[]{:S(2)}, u32[]{:S(2)}) collective-permute-start(f32[22,8,256]{2,1,0:T(8,128)S(1)} %pad_maximum_fusion.12), channel_id=1, source_target_pairs={{0,4},{1,5},{2,6},{3,7},{4,0},{5,1},{6,2},{7,3},{8,12},{9,13},{10,... | collective-permute-start | bytes 540680 | tf_op jit(solution)/shard_map/ppermute | solution.py:459
  86.6 4.2 %collective-permute-done.34.from_chip = f32[22,8,256]{2,1,0:T(8,128)S(1)} collective-permute-done((f32[22,8,256]{2,1,0:T(8,128)S(1)}, f32[22,8,256]{2,1,0:T(8,128)S(1)}, u32[]{:S(2)}, u32[]{:S(2)}) %collective-permute-start.34) | collective-permute-done | bytes 180256 | tf_op jit(solution)/shard_map/ppermute | solution.py:459
  90.8 3.1 %shard_map.90 = (f32[256,128]{1,0:T(8,128)}, f32[8,10,2,16,128]{4,3,2,1,0:T(8,128)S(1)}) custom-call(s32[3]{0:T(128)S(1)} %pad_add_fusion.info, f32[2]{0:T(128)S(1)} %add_convert_fusion.flags, f32[8,8,256]{2,1,0:T(8,128)S(1)} %get-tuple-element.211.own, f32[8,8,256]{2,1,0:T(8,128)S(1)} %get-tuple-element.359.left, ...), custom_call_target="tpu_custom_call" | custom-call | flops 1000000 | bytes 1000000 | tf_op jit(solution)/shard_map/pallas_call | solution.py:421
  93.9 6.0 %all-to-all-start.1 = ((f32[256,1,128]{2,1,0:T(1,128)}), f32[256,1,128]{2,1,0:T(1,128)S(1)}, u32[]{:S(2)}, u32[]{:S(2)}) async-start(f32[256,1,128]{2,1,0:T(1,128)} %bitcast.39), calls=%async_computation.1 | async-start | bytes 262144 | tf_op jit(solution)/shard_map/all_to_all | solution.py:518
  99.9 12.9 %all-to-all-done.1 = f32[256,1,128]{2,1,0:T(1,128)S(1)} async-done(((f32[256,1,128]{2,1,0:T(1,128)}), f32[256,1,128]{2,1,0:T(1,128)S(1)}, u32[]{:S(2)}, u32[]{:S(2)}) %all-to-all-start.1) | async-done | bytes 131104 | tf_op jit(solution)/shard_map/all_to_all | solution.py:518
  112.8 1.5 %shard_map.91 = (s32[1]{0:T(128)}, f32[4,4,8,256]{3,2,1,0:T(8,128)S(1)}, f32[4,4,8,256]{3,2,1,0:T(8,128)S(1)}) custom-call(s32[3]{0:T(128)S(1)} %pad_add_fusion.info, f32[256,128]{1,0:T(8,128)S(1)} %bitcast.94, f32[16,128]{1,0:T(8,128)S(1)} %copy-done.1, f32[16,128]{1,0:T(8,128)S(1)} %copy-done.2, f32[8,16,128]{2,1,0:T(8,128)S(1)} %copy-done, ...), custom_call_target="tpu_custom_call" | custom-call | flops 1000000 | bytes 1000000 | tf_op jit(solution)/shard_map/pallas_call | solution.py:421
  114.9 3.1 %conditional.1 = ((f32[3,4,16,256]{3,2,1,0:T(8,128)}, f32[4,16,256]{2,1,0:T(8,128)})) conditional(s32[]{:T(128)} %bitcast.41, (s32[2]{0:T(128)S(1)}, s32[4,16,256]{2,1,0:T(8,128)S(1)}, f32[8,3]{0,1:T(4,128)S(1)}, f32[3,4,16,256]{3,2,1,0:T(8,128)}) %tuple.190, (f32[4,4,8,256]{3,2,1,0:T(8,128)S(1)}, s32[3]{0:T(128)S(1)}, ...), branch_computations={%region_0.9_spmd, %region_9.10_spmd} | conditional | flops 3744999 | bytes 12867738 | solution.py:539
  (78 shorter events, 15.1 us)
Async XLA Ops:
  1.6 60.0 %copy-start.4 = (f32[3,4,16,256]{3,2,1,0:T(8,128)}, f32[3,4,16,256]{3,2,1,0:T(8,128)S(1)}, u32[]{:S(2)}) copy-start(f32[3,4,16,256]{3,2,1,0:T(8,128)S(1)} %copy.62) | copy-start | bytes 589828
  2.5 10.2 %collective-permute-start.18 = (f32[13,16,256]{2,1,0:T(8,128)S(1)}, f32[13,16,256]{2,1,0:T(8,128)S(1)}, u32[]{:S(2)}, u32[]{:S(2)}) collective-permute-start(f32[13,16,256]{2,1,0:T(8,128)S(1)} %pad_maximum_fusion.9), channel_id=1, source_target_pairs={{0,252},{1,253},{2,254},{3,255},{4,8},{5,9},{6,10},{7,11},{8,4},{9... | collective-permute-start | bytes 638984 | tf_op jit(solution)/shard_map/ppermute | solution.py:459
  5.2 7.5 %collective-permute-start.20 = (f32[16,8,256]{2,1,0:T(8,128)S(1)}, f32[16,8,256]{2,1,0:T(8,128)S(1)}, u32[]{:S(2)}, u32[]{:S(2)}) collective-permute-start(f32[16,8,256]{2,1,0:T(8,128)S(1)} %broadcast_select_fusion.6), channel_id=1, source_target_pairs={{0,4},{1,5},{2,6},{3,7},{4,0},{5,1},{6,2},{7,3},{8,12},{9,13},{10,... | collective-permute-start | bytes 393224 | tf_op jit(solution)/shard_map/ppermute | solution.py:459
  12.8 3.4 %collective-permute-start.19 = (f32[13,8,256]{2,1,0:T(8,128)S(1)}, f32[13,8,256]{2,1,0:T(8,128)S(1)}, u32[]{:S(2)}, u32[]{:S(2)}) collective-permute-start(f32[13,8,256]{2,1,0:T(8,128)S(1)} %slice_select_fusion), channel_id=1, source_target_pairs={{0,4},{1,5},{2,6},{3,7},{4,0},{5,1},{6,2},{7,3},{8,12},{9,13},{10,... | collective-permute-start | bytes 319496 | tf_op jit(solution)/shard_map/ppermute | solution.py:459
  16.4 1.8 %collective-permute-start.21 = (f32[4,12,2,256]{3,2,1,0:T(2,128)S(1)}, f32[4,12,2,256]{3,2,1,0:T(2,128)S(1)}, u32[]{:S(2)}, u32[]{:S(2)}) collective-permute-start(f32[4,12,2,256]{3,2,1,0:T(2,128)S(1)} %bitcast.110), channel_id=1, source_target_pairs={{0,4},{1,5},{2,6},{3,7},{4,0},{5,1},{6,2},{7,3},{8,12},{9,13},{10,... | collective-permute-start | bytes 294920 | tf_op jit(solution)/shard_map/ppermute | solution.py:459
  16.9 4.3 %collective-permute-start.22 = (f32[4,12,2,256]{3,2,1,0:T(2,128)S(1)}, f32[4,12,2,256]{3,2,1,0:T(2,128)S(1)}, u32[]{:S(2)}, u32[]{:S(2)}) collective-permute-start(f32[4,12,2,256]{3,2,1,0:T(2,128)S(1)} %get-tuple-element.290), channel_id=1, source_target_pairs={{0,7},{1,4},{2,5},{3,6},{4,1},{5,2},{6,3},{7,0},{8,15},{9,12},{10,... | collective-permute-start | bytes 294920 | tf_op jit(solution)/shard_map/ppermute | solution.py:459
  18.2 43.3 %copy-start = (f32[8,16,128]{2,1,0:T(8,128)S(1)}, f32[8,16,128]{2,1,0:T(8,128)}, u32[]{:S(2)}) copy-start(f32[8,16,128]{2,1,0:T(8,128)} %constant.275.clone.coef) | copy-start | bytes 196612
  18.2 43.3 %copy-start.1 = (f32[16,128]{1,0:T(8,128)S(1)}, f32[16,128]{1,0:T(8,128)}, u32[]{:S(2)}) copy-start(f32[16,128]{1,0:T(8,128)} %constant.273.clone.weight_map) | copy-start | bytes 24580
  18.2 43.3 %copy-start.2 = (f32[16,128]{1,0:T(8,128)S(1)}, f32[16,128]{1,0:T(8,128)}, u32[]{:S(2)}) copy-start(f32[16,128]{1,0:T(8,128)} %constant.274.clone.node) | copy-start | bytes 24580
  22.6 6.6 %collective-permute-start.23 = (f32[8,8,256]{2,1,0:T(8,128)S(1)}, f32[8,8,256]{2,1,0:T(8,128)S(1)}, u32[]{:S(2)}, u32[]{:S(2)}) collective-permute-start(f32[8,8,256]{2,1,0:T(8,128)S(1)} %get-tuple-element.206.own), channel_id=1, source_target_pairs={{0,248},{1,249},{2,250},{3,251},{4,252},{5,253},{6,254},{7,255},{8... | collective-permute-start | bytes 196616 | tf_op jit(solution)/shard_map/ppermute | solution.py:459
  27.5 3.4 %collective-permute-start.24 = (f32[8,8,256]{2,1,0:T(8,128)S(1)}, f32[8,8,256]{2,1,0:T(8,128)S(1)}, u32[]{:S(2)}, u32[]{:S(2)}) collective-permute-start(f32[8,8,256]{2,1,0:T(8,128)S(1)} %get-tuple-element.206.own), channel_id=1, source_target_pairs={{0,8},{1,9},{2,10},{3,11},{4,12},{5,13},{6,14},{7,15},{8,0},{9,1},... | collective-permute-start | bytes 196616 | tf_op jit(solution)/shard_map/ppermute | solution.py:459
  31.0 3.5 %collective-permute-start.25 = (f32[22,8,256]{2,1,0:T(8,128)S(1)}, f32[22,8,256]{2,1,0:T(8,128)S(1)}, u32[]{:S(2)}, u32[]{:S(2)}) collective-permute-start(f32[22,8,256]{2,1,0:T(8,128)S(1)} %pad_maximum_fusion.11), channel_id=1, source_target_pairs={{0,4},{1,5},{2,6},{3,7},{4,0},{5,1},{6,2},{7,3},{8,12},{9,13},{10,... | collective-permute-start | bytes 540680 | tf_op jit(solution)/shard_map/ppermute | solution.py:459
  33.5 5.2 %collective-permute-start.26 = (f32[22,8,256]{2,1,0:T(8,128)S(1)}, f32[22,8,256]{2,1,0:T(8,128)S(1)}, u32[]{:S(2)}, u32[]{:S(2)}) collective-permute-start(f32[22,8,256]{2,1,0:T(8,128)S(1)} %pad_maximum_fusion.11), channel_id=1, source_target_pairs={{0,7},{1,4},{2,5},{3,6},{4,1},{5,2},{6,3},{7,0},{8,15},{9,12},{10,... | collective-permute-start | bytes 540680 | tf_op jit(solution)/shard_map/ppermute | solution.py:459
  62.1 6.9 %collective-permute-start.27 = (f32[3,4,8,256]{3,2,1,0:T(8,128)S(1)}, f32[3,4,8,256]{3,2,1,0:T(8,128)S(1)}, u32[]{:S(2)}, u32[]{:S(2)}) collective-permute-start(f32[3,4,8,256]{3,2,1,0:T(8,128)S(1)} %get-tuple-element.357), channel_id=1, source_target_pairs={{0,248},{1,249},{2,250},{3,251},{4,252},{5,253},{6,254},{7,255},{8... | collective-permute-start | bytes 294920 | tf_op jit(solution)/shard_map/ppermute | solution.py:459
  62.7 6.2 %collective-permute-start.28 = (f32[3,4,8,256]{3,2,1,0:T(8,128)S(1)}, f32[3,4,8,256]{3,2,1,0:T(8,128)S(1)}, u32[]{:S(2)}, u32[]{:S(2)}) collective-permute-start(f32[3,4,8,256]{3,2,1,0:T(8,128)S(1)} %get-tuple-element.356), channel_id=1, source_target_pairs={{0,8},{1,9},{2,10},{3,11},{4,12},{5,13},{6,14},{7,15},{8,0},{9,1},... | collective-permute-start | bytes 294920 | tf_op jit(solution)/shard_map/ppermute | solution.py:459
  69.1 2.9 %collective-permute-start.29 = (f32[3,12,2,256]{3,2,1,0:T(2,128)S(1)}, f32[3,12,2,256]{3,2,1,0:T(2,128)S(1)}, u32[]{:S(2)}, u32[]{:S(2)}) collective-permute-start(f32[3,12,2,256]{3,2,1,0:T(2,128)S(1)} %bitcast.111), channel_id=1, source_target_pairs={{0,4},{1,5},{2,6},{3,7},{4,0},{5,1},{6,2},{7,3},{8,12},{9,13},{10,... | collective-permute-start | bytes 221192 | tf_op jit(solution)/shard_map/ppermute | solution.py:459
  71.1 3.8 %collective-permute-start.30 = (f32[3,12,2,256]{3,2,1,0:T(2,128)S(1)}, f32[3,12,2,256]{3,2,1,0:T(2,128)S(1)}, u32[]{:S(2)}, u32[]{:S(2)}) collective-permute-start(f32[3,12,2,256]{3,2,1,0:T(2,128)S(1)} %get-tuple-element.287), channel_id=1, source_target_pairs={{0,7},{1,4},{2,5},{3,6},{4,1},{5,2},{6,3},{7,0},{8,15},{9,12},{10,... | collective-permute-start | bytes 221192 | tf_op jit(solution)/shard_map/ppermute | solution.py:459
  76.2 6.5 %collective-permute-start.31 = (f32[8,8,256]{2,1,0:T(8,128)S(1)}, f32[8,8,256]{2,1,0:T(8,128)S(1)}, u32[]{:S(2)}, u32[]{:S(2)}) collective-permute-start(f32[8,8,256]{2,1,0:T(8,128)S(1)} %get-tuple-element.211.own), channel_id=1, source_target_pairs={{0,248},{1,249},{2,250},{3,251},{4,252},{5,253},{6,254},{7,255},{8... | collective-permute-start | bytes 196616 | tf_op jit(solution)/shard_map/ppermute | solution.py:459
  78.1 4.7 %collective-permute-start.32 = (f32[8,8,256]{2,1,0:T(8,128)S(1)}, f32[8,8,256]{2,1,0:T(8,128)S(1)}, u32[]{:S(2)}, u32[]{:S(2)}) collective-permute-start(f32[8,8,256]{2,1,0:T(8,128)S(1)} %get-tuple-element.211.own), channel_id=1, source_target_pairs={{0,8},{1,9},{2,10},{3,11},{4,12},{5,13},{6,14},{7,15},{8,0},{9,1},... | collective-permute-start | bytes 196616 | tf_op jit(solution)/shard_map/ppermute | solution.py:459
  82.8 32.1 %copy-start.5 = (s32[4,16,256]{2,1,0:T(8,128)S(1)}, s32[4,16,256]{2,1,0:T(8,128)}, u32[]{:S(2)}) copy-start(s32[4,16,256]{2,1,0:T(8,128)} %param.14) | copy-start | bytes 196612
  82.8 3.8 %collective-permute-start.33 = (f32[22,8,256]{2,1,0:T(8,128)S(1)}, f32[22,8,256]{2,1,0:T(8,128)S(1)}, u32[]{:S(2)}, u32[]{:S(2)}) collective-permute-start(f32[22,8,256]{2,1,0:T(8,128)S(1)} %pad_maximum_fusion.12), channel_id=1, source_target_pairs={{0,4},{1,5},{2,6},{3,7},{4,0},{5,1},{6,2},{7,3},{8,12},{9,13},{10,... | collective-permute-start | bytes 540680 | tf_op jit(solution)/shard_map/ppermute | solution.py:459
  85.6 5.2 %collective-permute-start.34 = (f32[22,8,256]{2,1,0:T(8,128)S(1)}, f32[22,8,256]{2,1,0:T(8,128)S(1)}, u32[]{:S(2)}, u32[]{:S(2)}) collective-permute-start(f32[22,8,256]{2,1,0:T(8,128)S(1)} %pad_maximum_fusion.12), channel_id=1, source_target_pairs={{0,7},{1,4},{2,5},{3,6},{4,1},{5,2},{6,3},{7,0},{8,15},{9,12},{10,... | collective-permute-start | bytes 540680 | tf_op jit(solution)/shard_map/ppermute | solution.py:459
  93.9 18.9 %all-to-all-start.1 = ((f32[256,1,128]{2,1,0:T(1,128)}), f32[256,1,128]{2,1,0:T(1,128)S(1)}, u32[]{:S(2)}, u32[]{:S(2)}) async-start(f32[256,1,128]{2,1,0:T(1,128)} %bitcast.39), calls=%async_computation.1 | async-start | bytes 262144 | tf_op jit(solution)/shard_map/all_to_all | solution.py:518
  114.9 1.8 %collective-permute-start = (f32[4,4,8,256]{3,2,1,0:T(8,128)S(1)}, f32[4,4,8,256]{3,2,1,0:T(8,128)S(1)}, u32[]{:S(2)}, u32[]{:S(2)}) collective-permute-start(f32[4,4,8,256]{3,2,1,0:T(8,128)S(1)} %get-tuple-element.190), channel_id=1, source_target_pairs={{0,4},{1,5},{2,6},{3,7},{4,0},{5,1},{6,2},{7,3},{8,12},{9,13},{10,... | collective-permute-start | bytes 393224 | tf_op jit(solution)/shard_map/cond/branch_1_fun/ppermute | solution.py:459
  (2 other events, 22.4 us)

commit v4 on v3

--- a/solution.py
+++ b/solution.py
@@ -22,7 +22,7 @@
 NODES = 16
 NZ = 256
 DEPTH = 8
-NOISE = 1e-4
+NOISE = 1e-5
 
 
 def shifted(value, axis, steps):
@@ -176,6 +176,24 @@
         (jnp.where(last, b_next, a_next), jnp.where(start, b_prev, a_prev)),
         (jnp.where(last, a_next, b_next), jnp.where(start, a_prev, b_prev)),
     )
+
+
+def pack_kernel(velocity, cells, facing, along, theirs, mine):
+    first = lax.axis_index("gx") % 2 == 0
+
+    def put(i, plane, outputs):
+        low, high = plane[0:8], plane[8:16]
+        same, other = jnp.where(first, low, high), jnp.where(first, high, low)
+        for out, value in zip(outputs, (same, other, same, other)):
+            out[i] = value
+
+    for i in range(4):
+        for c in range(3):
+            put(4 * c + i, velocity[c, i], (mine, theirs, along, facing))
+        put(12 + i, cells[i].astype(jnp.float32), (mine, theirs))
+    edge = jnp.where(first, cells[0], cells[3]).astype(jnp.float32)
+    along[12] = jnp.where(first, edge[0:8], edge[8:16])
+    facing[12] = jnp.where(first, edge[8:16], edge[0:8])
 
 
 def source_kernel(
@@ -448,6 +466,7 @@
     return {
         "core": pairs(lambda chip, core, y: (chip, 1 - core, y)),
         "facing": pairs(lambda chip, core, y: (chip + (1 if core else -1), 1 - core, y)),
+        "along": pairs(lambda chip, core, y: (chip + (1 if core else -1), core, y)),
         "inner": pairs(lambda chip, core, y: (chip + (1 if chip % 2 == 0 else -1), core, y)),
         "outer": pairs(lambda chip, core, y: (chip + (-1 if chip % 2 == 0 else 1), core, y)),
         "across": pairs(across),
@@ -464,24 +483,23 @@
     weight_map, node, coef = (jnp.asarray(a) for a in tables())
     first = core == 0
     pick = lambda a, b: jnp.where(first, a, b)
-    even = (lax.axis_index("gx") // 2) % 2 == 0
-
-    def beside(to_left, to_right):
-        outer = send(jnp.where(even, to_left, to_right), "outer")
-        inner = send(jnp.where(even, to_right, to_left), "inner")
+    odd = (lax.axis_index("gx") // 2) % 2 == 1
+    even = jnp.logical_not(odd)
+
+    def beside(to_left, to_right, inner_first):
+        inner = send(jnp.where(odd, to_left, to_right), "inner")
+        outer = send(jnp.where(odd, to_right, to_left), "outer")
+        if inner_first:
+            return jnp.where(odd, inner, outer), jnp.where(odd, outer, inner)
         return jnp.where(even, outer, inner), jnp.where(even, inner, outer)
 
 
-    cells = cell_swimmer.astype(jnp.float32)
-    rows = velocity.reshape(12, 16, NZ)
-    outer = send(jnp.concatenate([rows, pick(cells[0:1], cells[3:4])], axis=0), "facing")
-    chunk = jnp.concatenate([rows, cells], axis=0)
-    theirs = send(pick(chunk[:, 8:16], chunk[:, 0:8]), "core")
-    mine = pick(chunk[:, 0:8], chunk[:, 8:16])
-    outer_theirs = send(pick(outer[:, 8:16], outer[:, 0:8]), "core")
-    outer_mine = pick(outer[:, 0:8], outer[:, 8:16])
+    facing, along, given, mine = call(
+        pack_kernel, (velocity, cell_swimmer), 0, [(13, 8, NZ), (13, 8, NZ), (16, 8, NZ), (16, 8, NZ)], []
+    )
+    facing, theirs, along = send(facing, "facing"), send(given, "core"), send(along, "along")
     low, high = pick(mine, theirs), pick(theirs, mine)
-    outer_low, outer_high = pick(outer_mine, outer_theirs), pick(outer_theirs, outer_mine)
+    outer_low, outer_high = pick(facing, along), pick(along, facing)
     planes = lambda a: a[0:12].reshape(3, 4, 8, NZ)
     own = jnp.concatenate([planes(low), planes(high)], axis=1)
     left, right = planes(outer_low), planes(outer_high)[:, 0:2]
@@ -489,7 +507,7 @@
 
     for step in range(STEPS):
         if step:
-            left, right = beside(own[:, 0:4], own[:, 4:8])
+            left, right = beside(own[:, 0:4], own[:, 4:8], False)
             right = right[:, 0:2]
         joined = jnp.concatenate([left, own, right], axis=1)
         if not step:
@@ -506,7 +524,7 @@
             [(3, 8, 8, NZ), (8, 8, NZ)],
             [(3, 14, 2, 24, HALF), (10, 2, 24, HALF), (3, 10, 2, 16, HALF)],
         )
-        s_left, s_right = beside(source, source)
+        s_left, s_right = beside(source, source, step == 0)
         column = jnp.concatenate([s_left[1:], source, s_right[:7]], axis=0)
         moments, near = call(
             powers_kernel,
@@ -534,7 +552,10 @@
         return tuple(call(place_kernel, (info, kept, got), 1, [(3, 4, 16, NZ), (4, 16, NZ)], []))
 
     def again(_):
-        return plain(velocity, cell_swimmer, swimmer_speed, recentre_cols)
+        whole = jnp.concatenate([pick(mine, given), pick(given, mine)], axis=1)
+        return plain(
+            whole[0:12].reshape(3, 4, 16, NZ), whole[12:16].astype(jnp.int32), swimmer_speed, recentre_cols
+        )
 
     return lax.cond(good[0] > 0, finish, again, None)
 

time: 118 us -> 117 us (level)
  waiting for transfers between devices: 46.1 us -> 43.6 us
  local copies, waits for them, and re-layouts: 1.14 us -> 2.63 us
    ppermute x18, waiting for transfers between devices: 33.3 us -> 30.8 us  [body(): send = lambda value, name: lax.ppermute(value, AXES, route[name])]
    unnamed x17 -> x16, local copies, waits for them, and re-layouts: 1.05 us -> 2.54 us
    pallas_call x7 -> x8, Pallas kernels: 11.5 us -> 11.5 us  [call(): pl.pallas_call(kernel, in_specs=[SMEM] * smem + [VMEM] * (len(args) - sme...]
  transfers between devices with their start and end apart: 19 -> 19, of which waited for: 15 -> 13; matrix products, arithmetic and copies ran while one was open for 0% -> 1% of each run, Pallas kernels for 0% -> 0%
where the time goes in v4:
time: 117 us
  waiting for transfers between devices  43.6 us (37%)
  starting transfers between devices  34.8 us (30%)
  blocking collectives  21.2 us (18%)
  Pallas kernels  11.5 us (10%)
  local copies, waits for them, and re-layouts  2.63 us (2%)
  between operations  1.62 us (1%)
    ppermute x18, waiting for transfers between devices, body(): send = lambda value, name: lax.ppermute(value, AXES, route[name])  30.8 us
    ppermute x18, starting transfers between devices, body(): send = lambda value, name: lax.ppermute(value, AXES, route[name])  28.8 us
    all_to_all x1, blocking collectives, body(): moments = lax.all_to_all(moments, AXES, 0, 0)  21.2 us
    all_to_all x1, waiting for transfers between devices, body(): moments = lax.all_to_all(moments, AXES, 0, 0)  12.8 us
    pallas_call x8, Pallas kernels, call(): pl.pallas_call(kernel, in_specs=[SMEM] * smem + [VMEM] * (len(args) - sme...  11.5 us
    all_to_all x1, starting transfers between devices, body(): moments = lax.all_to_all(moments, AXES, 0, 0)  6.02 us
    unnamed x16, local copies, waits for them, and re-layouts  2.54 us
  transfers between devices with their start and end apart: 19, of which 13 were waited for; matrix products, arithmetic and copies ran while one was open for 1% of the time, Pallas kernels for 0%

profile of v4, /device:TPU:1, one launch (start us, length us, event | category | flops | bytes accessed | tf_op | source)
XLA Modules:
  0.0 116.6 jit_solution(6269185578267189473)
XLA Ops:
  2.4 2.7 %collective-permute-start.18 = (f32[13,8,256]{2,1,0:T(8,128)S(1)}, f32[13,8,256]{2,1,0:T(8,128)S(1)}, u32[]{:S(2)}, u32[]{:S(2)}) collective-permute-start(f32[13,8,256]{2,1,0:T(8,128)S(1)} %get-tuple-element.213), channel_id=1, source_target_pairs={{0,252},{1,253},{2,254},{3,255},{4,8},{5,9},{6,10},{7,11},{8,4},{9... | collective-permute-start | bytes 319496 | tf_op jit(solution)/shard_map/ppermute | solution.py:478
  6.3 6.0 %collective-permute-start.20 = (f32[16,8,256]{2,1,0:T(8,128)S(1)}, f32[16,8,256]{2,1,0:T(8,128)S(1)}, u32[]{:S(2)}, u32[]{:S(2)}) collective-permute-start(f32[16,8,256]{2,1,0:T(8,128)S(1)} %get-tuple-element.216), channel_id=1, source_target_pairs={{0,4},{1,5},{2,6},{3,7},{4,0},{5,1},{6,2},{7,3},{8,12},{9,13},{10,... | collective-permute-start | bytes 393224 | tf_op jit(solution)/shard_map/ppermute | solution.py:478
  14.7 2.0 %collective-permute-start.21 = (f32[4,12,2,256]{3,2,1,0:T(2,128)S(1)}, f32[4,12,2,256]{3,2,1,0:T(2,128)S(1)}, u32[]{:S(2)}, u32[]{:S(2)}) collective-permute-start(f32[4,12,2,256]{3,2,1,0:T(2,128)S(1)} %bitcast.108), channel_id=1, source_target_pairs={{0,4},{1,5},{2,6},{3,7},{4,0},{5,1},{6,2},{7,3},{8,12},{9,13},{10,... | collective-permute-start | bytes 294920 | tf_op jit(solution)/shard_map/ppermute | solution.py:478
  18.0 3.0 %collective-permute-done.22.from_chip = f32[4,12,2,256]{3,2,1,0:T(2,128)S(1)} collective-permute-done((f32[4,12,2,256]{3,2,1,0:T(2,128)S(1)}, f32[4,12,2,256]{3,2,1,0:T(2,128)S(1)}, u32[]{:S(2)}, u32[]{:S(2)}) %collective-permute-start.22) | collective-permute-done | bytes 98336 | tf_op jit(solution)/shard_map/ppermute | solution.py:478
  21.0 1.4 %shard_map.87 = (f32[3,8,8,256]{3,2,1,0:T(8,128)S(1)}, f32[8,8,256]{2,1,0:T(8,128)S(1)}) custom-call(s32[3]{0:T(128)S(1)} %pad_add_fusion.info, f32[2]{0:T(128)S(1)} %add_convert_fusion.flags, f32[8,3]{1,0:T(8,128)S(1)} %copy.23.speed, f32[3,4,8,256]{3,2,1,0:T(8,128)S(1)} %bitcast.93, f32[3,8,8,256]{3,2,1,0:T(8,128)S(1)} %pad_maximum_fusion.10.own, ...), custom_call_target="tpu_custom_call" | custom-call | flops 1000000 | bytes 1000000 | tf_op jit(solution)/shard_map/pallas_call | solution.py:439
  22.5 4.3 %collective-permute-start.24 = (f32[8,8,256]{2,1,0:T(8,128)S(1)}, f32[8,8,256]{2,1,0:T(8,128)S(1)}, u32[]{:S(2)}, u32[]{:S(2)}) collective-permute-start(f32[8,8,256]{2,1,0:T(8,128)S(1)} %get-tuple-element.217.own), channel_id=1, source_target_pairs={{0,248},{1,249},{2,250},{3,251},{4,252},{5,253},{6,254},{7,255},{8... | collective-permute-start | bytes 196616 | tf_op jit(solution)/shard_map/ppermute | solution.py:478
  26.8 2.3 %collective-permute-done.24 = f32[8,8,256]{2,1,0:T(8,128)S(1)} collective-permute-done((f32[8,8,256]{2,1,0:T(8,128)S(1)}, f32[8,8,256]{2,1,0:T(8,128)S(1)}, u32[]{:S(2)}, u32[]{:S(2)}) %collective-permute-start.24) | collective-permute-done | bytes 65568 | tf_op jit(solution)/shard_map/ppermute | solution.py:478
  29.1 2.3 %collective-permute-start.25 = (f32[22,8,256]{2,1,0:T(8,128)S(1)}, f32[22,8,256]{2,1,0:T(8,128)S(1)}, u32[]{:S(2)}, u32[]{:S(2)}) collective-permute-start(f32[22,8,256]{2,1,0:T(8,128)S(1)} %pad_maximum_fusion.11), channel_id=1, source_target_pairs={{0,4},{1,5},{2,6},{3,7},{4,0},{5,1},{6,2},{7,3},{8,12},{9,13},{10,... | collective-permute-start | bytes 540680 | tf_op jit(solution)/shard_map/ppermute | solution.py:478
  32.5 4.2 %collective-permute-done.26.from_chip = f32[22,8,256]{2,1,0:T(8,128)S(1)} collective-permute-done((f32[22,8,256]{2,1,0:T(8,128)S(1)}, f32[22,8,256]{2,1,0:T(8,128)S(1)}, u32[]{:S(2)}, u32[]{:S(2)}) %collective-permute-start.26) | collective-permute-done | bytes 180256 | tf_op jit(solution)/shard_map/ppermute | solution.py:478
  36.6 2.4 %shard_map.88 = (f32[256,128]{1,0:T(8,128)S(1)}, f32[8,10,2,16,128]{4,3,2,1,0:T(8,128)S(1)}) custom-call(s32[3]{0:T(128)S(1)} %pad_add_fusion.info, f32[2]{0:T(128)S(1)} %add_convert_fusion.flags, f32[8,8,256]{2,1,0:T(8,128)S(1)} %get-tuple-element.217.own, f32[8,8,256]{2,1,0:T(8,128)S(1)} %get-tuple-element.377.left, ...), custom_call_target="tpu_custom_call" | custom-call | flops 1000000 | bytes 1000000 | tf_op jit(solution)/shard_map/pallas_call | solution.py:439
  39.1 21.2 %all_to_all.22 = f32[256,1,128]{2,1,0:T(1,128)S(1)} all-to-all(f32[256,1,128]{2,1,0:T(1,128)S(1)} %bitcast.96), channel_id=1, replica_groups=mesh['gx'=64,'gy'=4] {'gx','gy'}, dimensions={0} | all-to-all | bytes 262144 | tf_op jit(solution)/shard_map/all_to_all | solution.py:536
  61.9 5.8 %collective-permute-done.27 = f32[3,4,8,256]{3,2,1,0:T(8,128)S(1)} collective-permute-done((f32[3,4,8,256]{3,2,1,0:T(8,128)S(1)}, f32[3,4,8,256]{3,2,1,0:T(8,128)S(1)}, u32[]{:S(2)}, u32[]{:S(2)}) %collective-permute-start.27) | collective-permute-done | bytes 98336 | tf_op jit(solution)/shard_map/ppermute | solution.py:478
  67.8 2.0 %collective-permute-start.29 = (f32[3,12,2,256]{3,2,1,0:T(2,128)S(1)}, f32[3,12,2,256]{3,2,1,0:T(2,128)S(1)}, u32[]{:S(2)}, u32[]{:S(2)}) collective-permute-start(f32[3,12,2,256]{3,2,1,0:T(2,128)S(1)} %bitcast.109), channel_id=1, source_target_pairs={{0,4},{1,5},{2,6},{3,7},{4,0},{5,1},{6,2},{7,3},{8,12},{9,13},{10,... | collective-permute-start | bytes 221192 | tf_op jit(solution)/shard_map/ppermute | solution.py:478
  70.7 2.9 %collective-permute-done.30.from_chip = f32[3,12,2,256]{3,2,1,0:T(2,128)S(1)} collective-permute-done((f32[3,12,2,256]{3,2,1,0:T(2,128)S(1)}, f32[3,12,2,256]{3,2,1,0:T(2,128)S(1)}, u32[]{:S(2)}, u32[]{:S(2)}) %collective-permute-start.30) | collective-permute-done | bytes 73760 | tf_op jit(solution)/shard_map/ppermute | solution.py:478
  73.5 1.4 %shard_map.90 = (f32[3,8,8,256]{3,2,1,0:T(8,128)S(1)}, f32[8,8,256]{2,1,0:T(8,128)S(1)}) custom-call(s32[3]{0:T(128)S(1)} %pad_add_fusion.info, f32[2]{0:T(128)S(1)} %add_convert_fusion.flags, f32[8,3]{1,0:T(8,128)S(1)} %copy.23.speed, f32[3,4,8,256]{3,2,1,0:T(8,128)S(1)} %broadcast_select_fusion.10.left, f32[3,8,8,256]{3,2,1,0:T(8,128)S(1)} %get-tuple-element.221.own, ...), custom_call_target="tpu_custom_call" | custom-call | flops 1000000 | bytes 1000000 | tf_op jit(solution)/shard_map/pallas_call | solution.py:439
  74.9 1.8 %collective-permute-start.31 = (f32[8,8,256]{2,1,0:T(8,128)S(1)}, f32[8,8,256]{2,1,0:T(8,128)S(1)}, u32[]{:S(2)}, u32[]{:S(2)}) collective-permute-start(f32[8,8,256]{2,1,0:T(8,128)S(1)} %get-tuple-element.222.own), channel_id=1, source_target_pairs={{0,248},{1,249},{2,250},{3,251},{4,252},{5,253},{6,254},{7,255},{8... | collective-permute-start | bytes 196616 | tf_op jit(solution)/shard_map/ppermute | solution.py:478
  76.7 4.7 %collective-permute-done.31 = f32[8,8,256]{2,1,0:T(8,128)S(1)} collective-permute-done((f32[8,8,256]{2,1,0:T(8,128)S(1)}, f32[8,8,256]{2,1,0:T(8,128)S(1)}, u32[]{:S(2)}, u32[]{:S(2)}) %collective-permute-start.31) | collective-permute-done | bytes 65568 | tf_op jit(solution)/shard_map/ppermute | solution.py:478
  81.5 2.7 %collective-permute-start.33 = (f32[22,8,256]{2,1,0:T(8,128)S(1)}, f32[22,8,256]{2,1,0:T(8,128)S(1)}, u32[]{:S(2)}, u32[]{:S(2)}) collective-permute-start(f32[22,8,256]{2,1,0:T(8,128)S(1)} %pad_maximum_fusion.12), channel_id=1, source_target_pairs={{0,4},{1,5},{2,6},{3,7},{4,0},{5,1},{6,2},{7,3},{8,12},{9,13},{10,... | collective-permute-start | bytes 540680 | tf_op jit(solution)/shard_map/ppermute | solution.py:478
  85.3 4.2 %collective-permute-done.34.from_chip = f32[22,8,256]{2,1,0:T(8,128)S(1)} collective-permute-done((f32[22,8,256]{2,1,0:T(8,128)S(1)}, f32[22,8,256]{2,1,0:T(8,128)S(1)}, u32[]{:S(2)}, u32[]{:S(2)}) %collective-permute-start.34) | collective-permute-done | bytes 180256 | tf_op jit(solution)/shard_map/ppermute | solution.py:478
  89.5 3.1 %shard_map.91 = (f32[256,128]{1,0:T(8,128)}, f32[8,10,2,16,128]{4,3,2,1,0:T(8,128)S(1)}) custom-call(s32[3]{0:T(128)S(1)} %pad_add_fusion.info, f32[2]{0:T(128)S(1)} %add_convert_fusion.flags, f32[8,8,256]{2,1,0:T(8,128)S(1)} %get-tuple-element.222.own, f32[8,8,256]{2,1,0:T(8,128)S(1)} %get-tuple-element.375.left, ...), custom_call_target="tpu_custom_call" | custom-call | flops 1000000 | bytes 1000000 | tf_op jit(solution)/shard_map/pallas_call | solution.py:439
  92.6 6.0 %all-to-all-start.1 = ((f32[256,1,128]{2,1,0:T(1,128)}), f32[256,1,128]{2,1,0:T(1,128)S(1)}, u32[]{:S(2)}, u32[]{:S(2)}) async-start(f32[256,1,128]{2,1,0:T(1,128)} %bitcast.39), calls=%async_computation.1 | async-start | bytes 262144 | tf_op jit(solution)/shard_map/all_to_all | solution.py:536
  98.6 12.8 %all-to-all-done.1 = f32[256,1,128]{2,1,0:T(1,128)S(1)} async-done(((f32[256,1,128]{2,1,0:T(1,128)}), f32[256,1,128]{2,1,0:T(1,128)S(1)}, u32[]{:S(2)}, u32[]{:S(2)}) %all-to-all-start.1) | async-done | bytes 131104 | tf_op jit(solution)/shard_map/all_to_all | solution.py:536
  111.4 1.5 %shard_map.92 = (s32[1]{0:T(128)}, f32[4,4,8,256]{3,2,1,0:T(8,128)S(1)}, f32[4,4,8,256]{3,2,1,0:T(8,128)S(1)}) custom-call(s32[3]{0:T(128)S(1)} %pad_add_fusion.info, f32[256,128]{1,0:T(8,128)S(1)} %bitcast.94, f32[16,128]{1,0:T(8,128)S(1)} %copy-done.3, f32[16,128]{1,0:T(8,128)S(1)} %copy-done.4, f32[8,16,128]{2,1,0:T(8,128)S(1)} %copy-done, ...), custom_call_target="tpu_custom_call" | custom-call | flops 1000000 | bytes 1000000 | tf_op jit(solution)/shard_map/pallas_call | solution.py:439
  113.5 3.1 %conditional.1 = ((f32[3,4,16,256]{3,2,1,0:T(8,128)}, f32[4,16,256]{2,1,0:T(8,128)})) conditional(s32[]{:T(128)} %bitcast.41, (pred[]{:T(512)}, f32[16,8,256]{2,1,0:T(8,128)S(1)}, f32[16,8,256]{2,1,0:T(8,128)S(1)}, s32[2]{0:T(128)S(1)}, f32[8,3]{0,1:T(4,128)S(1)}) %tuple.191, (f32[4,4,8,256]{3,2,1,0:T(8,128)S(1)}, s32[3]{0:T(128)S(1)}, ...), branch_computations={%region_0.9_spmd, %region_9.10_spmd} | conditional | flops 3892455 | bytes 14964919 | solution.py:560
  (73 shorter events, 14.5 us)
Async XLA Ops:
  2.4 11.5 %collective-permute-start.18 = (f32[13,8,256]{2,1,0:T(8,128)S(1)}, f32[13,8,256]{2,1,0:T(8,128)S(1)}, u32[]{:S(2)}, u32[]{:S(2)}) collective-permute-start(f32[13,8,256]{2,1,0:T(8,128)S(1)} %get-tuple-element.213), channel_id=1, source_target_pairs={{0,252},{1,253},{2,254},{3,255},{4,8},{5,9},{6,10},{7,11},{8,4},{9... | collective-permute-start | bytes 319496 | tf_op jit(solution)/shard_map/ppermute | solution.py:478
  5.1 9.2 %collective-permute-start.19 = (f32[13,8,256]{2,1,0:T(8,128)S(1)}, f32[13,8,256]{2,1,0:T(8,128)S(1)}, u32[]{:S(2)}, u32[]{:S(2)}) collective-permute-start(f32[13,8,256]{2,1,0:T(8,128)S(1)} %get-tuple-element.214), channel_id=1, source_target_pairs={{0,248},{1,249},{2,250},{3,251},{4,12},{5,13},{6,14},{7,15},{8,0},... | collective-permute-start | bytes 319496 | tf_op jit(solution)/shard_map/ppermute | solution.py:478
  6.3 8.1 %collective-permute-start.20 = (f32[16,8,256]{2,1,0:T(8,128)S(1)}, f32[16,8,256]{2,1,0:T(8,128)S(1)}, u32[]{:S(2)}, u32[]{:S(2)}) collective-permute-start(f32[16,8,256]{2,1,0:T(8,128)S(1)} %get-tuple-element.216), channel_id=1, source_target_pairs={{0,4},{1,5},{2,6},{3,7},{4,0},{5,1},{6,2},{7,3},{8,12},{9,13},{10,... | collective-permute-start | bytes 393224 | tf_op jit(solution)/shard_map/ppermute | solution.py:478
  14.7 3.3 %collective-permute-start.21 = (f32[4,12,2,256]{3,2,1,0:T(2,128)S(1)}, f32[4,12,2,256]{3,2,1,0:T(2,128)S(1)}, u32[]{:S(2)}, u32[]{:S(2)}) collective-permute-start(f32[4,12,2,256]{3,2,1,0:T(2,128)S(1)} %bitcast.108), channel_id=1, source_target_pairs={{0,4},{1,5},{2,6},{3,7},{4,0},{5,1},{6,2},{7,3},{8,12},{9,13},{10,... | collective-permute-start | bytes 294920 | tf_op jit(solution)/shard_map/ppermute | solution.py:478
  16.7 4.3 %collective-permute-start.22 = (f32[4,12,2,256]{3,2,1,0:T(2,128)S(1)}, f32[4,12,2,256]{3,2,1,0:T(2,128)S(1)}, u32[]{:S(2)}, u32[]{:S(2)}) collective-permute-start(f32[4,12,2,256]{3,2,1,0:T(2,128)S(1)} %get-tuple-element.304), channel_id=1, source_target_pairs={{0,7},{1,4},{2,5},{3,6},{4,1},{5,2},{6,3},{7,0},{8,15},{9,12},{10,... | collective-permute-start | bytes 294920 | tf_op jit(solution)/shard_map/ppermute | solution.py:478
  17.9 42.3 %copy-start = (f32[8,16,128]{2,1,0:T(8,128)S(1)}, f32[8,16,128]{2,1,0:T(8,128)}, u32[]{:S(2)}) copy-start(f32[8,16,128]{2,1,0:T(8,128)} %constant.275.clone.coef) | copy-start | bytes 196612
  17.9 42.3 %copy-start.3 = (f32[16,128]{1,0:T(8,128)S(1)}, f32[16,128]{1,0:T(8,128)}, u32[]{:S(2)}) copy-start(f32[16,128]{1,0:T(8,128)} %constant.273.clone.weight_map) | copy-start | bytes 24580
  18.0 42.3 %copy-start.4 = (f32[16,128]{1,0:T(8,128)S(1)}, f32[16,128]{1,0:T(8,128)}, u32[]{:S(2)}) copy-start(f32[16,128]{1,0:T(8,128)} %constant.274.clone.node) | copy-start | bytes 24580
  22.4 4.4 %collective-permute-start.23 = (f32[8,8,256]{2,1,0:T(8,128)S(1)}, f32[8,8,256]{2,1,0:T(8,128)S(1)}, u32[]{:S(2)}, u32[]{:S(2)}) collective-permute-start(f32[8,8,256]{2,1,0:T(8,128)S(1)} %get-tuple-element.217.own), channel_id=1, source_target_pairs={{0,8},{1,9},{2,10},{3,11},{4,12},{5,13},{6,14},{7,15},{8,0},{9,1},... | collective-permute-start | bytes 196616 | tf_op jit(solution)/shard_map/ppermute | solution.py:478
  22.5 6.5 %collective-permute-start.24 = (f32[8,8,256]{2,1,0:T(8,128)S(1)}, f32[8,8,256]{2,1,0:T(8,128)S(1)}, u32[]{:S(2)}, u32[]{:S(2)}) collective-permute-start(f32[8,8,256]{2,1,0:T(8,128)S(1)} %get-tuple-element.217.own), channel_id=1, source_target_pairs={{0,248},{1,249},{2,250},{3,251},{4,252},{5,253},{6,254},{7,255},{8... | collective-permute-start | bytes 196616 | tf_op jit(solution)/shard_map/ppermute | solution.py:478
  29.1 3.4 %collective-permute-start.25 = (f32[22,8,256]{2,1,0:T(8,128)S(1)}, f32[22,8,256]{2,1,0:T(8,128)S(1)}, u32[]{:S(2)}, u32[]{:S(2)}) collective-permute-start(f32[22,8,256]{2,1,0:T(8,128)S(1)} %pad_maximum_fusion.11), channel_id=1, source_target_pairs={{0,4},{1,5},{2,6},{3,7},{4,0},{5,1},{6,2},{7,3},{8,12},{9,13},{10,... | collective-permute-start | bytes 540680 | tf_op jit(solution)/shard_map/ppermute | solution.py:478
  31.4 5.2 %collective-permute-start.26 = (f32[22,8,256]{2,1,0:T(8,128)S(1)}, f32[22,8,256]{2,1,0:T(8,128)S(1)}, u32[]{:S(2)}, u32[]{:S(2)}) collective-permute-start(f32[22,8,256]{2,1,0:T(8,128)S(1)} %pad_maximum_fusion.11), channel_id=1, source_target_pairs={{0,7},{1,4},{2,5},{3,6},{4,1},{5,2},{6,3},{7,0},{8,15},{9,12},{10,... | collective-permute-start | bytes 540680 | tf_op jit(solution)/shard_map/ppermute | solution.py:478
  60.8 6.9 %collective-permute-start.27 = (f32[3,4,8,256]{3,2,1,0:T(8,128)S(1)}, f32[3,4,8,256]{3,2,1,0:T(8,128)S(1)}, u32[]{:S(2)}, u32[]{:S(2)}) collective-permute-start(f32[3,4,8,256]{3,2,1,0:T(8,128)S(1)} %get-tuple-element.373), channel_id=1, source_target_pairs={{0,248},{1,249},{2,250},{3,251},{4,252},{5,253},{6,254},{7,255},{8... | collective-permute-start | bytes 294920 | tf_op jit(solution)/shard_map/ppermute | solution.py:478
  61.4 6.2 %collective-permute-start.28 = (f32[3,4,8,256]{3,2,1,0:T(8,128)S(1)}, f32[3,4,8,256]{3,2,1,0:T(8,128)S(1)}, u32[]{:S(2)}, u32[]{:S(2)}) collective-permute-start(f32[3,4,8,256]{3,2,1,0:T(8,128)S(1)} %get-tuple-element.372), channel_id=1, source_target_pairs={{0,8},{1,9},{2,10},{3,11},{4,12},{5,13},{6,14},{7,15},{8,0},{9,1},... | collective-permute-start | bytes 294920 | tf_op jit(solution)/shard_map/ppermute | solution.py:478
  67.8 2.9 %collective-permute-start.29 = (f32[3,12,2,256]{3,2,1,0:T(2,128)S(1)}, f32[3,12,2,256]{3,2,1,0:T(2,128)S(1)}, u32[]{:S(2)}, u32[]{:S(2)}) collective-permute-start(f32[3,12,2,256]{3,2,1,0:T(2,128)S(1)} %bitcast.109), channel_id=1, source_target_pairs={{0,4},{1,5},{2,6},{3,7},{4,0},{5,1},{6,2},{7,3},{8,12},{9,13},{10,... | collective-permute-start | bytes 221192 | tf_op jit(solution)/shard_map/ppermute | solution.py:478
  69.7 3.8 %collective-permute-start.30 = (f32[3,12,2,256]{3,2,1,0:T(2,128)S(1)}, f32[3,12,2,256]{3,2,1,0:T(2,128)S(1)}, u32[]{:S(2)}, u32[]{:S(2)}) collective-permute-start(f32[3,12,2,256]{3,2,1,0:T(2,128)S(1)} %get-tuple-element.301), channel_id=1, source_target_pairs={{0,7},{1,4},{2,5},{3,6},{4,1},{5,2},{6,3},{7,0},{8,15},{9,12},{10,... | collective-permute-start | bytes 221192 | tf_op jit(solution)/shard_map/ppermute | solution.py:478
  74.9 6.5 %collective-permute-start.31 = (f32[8,8,256]{2,1,0:T(8,128)S(1)}, f32[8,8,256]{2,1,0:T(8,128)S(1)}, u32[]{:S(2)}, u32[]{:S(2)}) collective-permute-start(f32[8,8,256]{2,1,0:T(8,128)S(1)} %get-tuple-element.222.own), channel_id=1, source_target_pairs={{0,248},{1,249},{2,250},{3,251},{4,252},{5,253},{6,254},{7,255},{8... | collective-permute-start | bytes 196616 | tf_op jit(solution)/shard_map/ppermute | solution.py:478
  76.7 4.7 %collective-permute-start.32 = (f32[8,8,256]{2,1,0:T(8,128)S(1)}, f32[8,8,256]{2,1,0:T(8,128)S(1)}, u32[]{:S(2)}, u32[]{:S(2)}) collective-permute-start(f32[8,8,256]{2,1,0:T(8,128)S(1)} %get-tuple-element.222.own), channel_id=1, source_target_pairs={{0,8},{1,9},{2,10},{3,11},{4,12},{5,13},{6,14},{7,15},{8,0},{9,1},... | collective-permute-start | bytes 196616 | tf_op jit(solution)/shard_map/ppermute | solution.py:478
  81.5 32.0 %copy-start.7 = (f32[8,3]{0,1:T(4,128)S(1)}, f32[8,3]{0,1:T(4,128)}, u32[]{:S(2)}) copy-start(f32[8,3]{0,1:T(4,128)} %param.15) | copy-start | bytes 292
  81.5 32.0 %copy-start.8 = (s32[2]{0:T(128)S(1)}, s32[2]{0:T(128)}, u32[]{:S(2)}) copy-start(s32[2]{0:T(128)} %param.16) | copy-start | bytes 28
  81.5 3.8 %collective-permute-start.33 = (f32[22,8,256]{2,1,0:T(8,128)S(1)}, f32[22,8,256]{2,1,0:T(8,128)S(1)}, u32[]{:S(2)}, u32[]{:S(2)}) collective-permute-start(f32[22,8,256]{2,1,0:T(8,128)S(1)} %pad_maximum_fusion.12), channel_id=1, source_target_pairs={{0,4},{1,5},{2,6},{3,7},{4,0},{5,1},{6,2},{7,3},{8,12},{9,13},{10,... | collective-permute-start | bytes 540680 | tf_op jit(solution)/shard_map/ppermute | solution.py:478
  84.2 5.2 %collective-permute-start.34 = (f32[22,8,256]{2,1,0:T(8,128)S(1)}, f32[22,8,256]{2,1,0:T(8,128)S(1)}, u32[]{:S(2)}, u32[]{:S(2)}) collective-permute-start(f32[22,8,256]{2,1,0:T(8,128)S(1)} %pad_maximum_fusion.12), channel_id=1, source_target_pairs={{0,7},{1,4},{2,5},{3,6},{4,1},{5,2},{6,3},{7,0},{8,15},{9,12},{10,... | collective-permute-start | bytes 540680 | tf_op jit(solution)/shard_map/ppermute | solution.py:478
  92.6 18.8 %all-to-all-start.1 = ((f32[256,1,128]{2,1,0:T(1,128)}), f32[256,1,128]{2,1,0:T(1,128)S(1)}, u32[]{:S(2)}, u32[]{:S(2)}) async-start(f32[256,1,128]{2,1,0:T(1,128)} %bitcast.39), calls=%async_computation.1 | async-start | bytes 262144 | tf_op jit(solution)/shard_map/all_to_all | solution.py:536
  113.5 1.8 %collective-permute-start = (f32[4,4,8,256]{3,2,1,0:T(8,128)S(1)}, f32[4,4,8,256]{3,2,1,0:T(8,128)S(1)}, u32[]{:S(2)}, u32[]{:S(2)}) collective-permute-start(f32[4,4,8,256]{3,2,1,0:T(8,128)S(1)} %get-tuple-element.193), channel_id=1, source_target_pairs={{0,4},{1,5},{2,6},{3,7},{4,0},{5,1},{6,2},{7,3},{8,12},{9,13},{10,... | collective-permute-start | bytes 393224 | tf_op jit(solution)/shard_map/cond/branch_1_fun/ppermute | solution.py:478
  (2 other events, 1.8 us)

commit v5 on v4

--- a/solution.py
+++ b/solution.py
@@ -277,19 +277,32 @@
                 bodied[c, i, :, lanes] = body[c, i + 1, h, 1:9]
 
 
-def powers_kernel(info, flags, own, left, right, from_core, from_chip, moments, near, *t):
+def powers_kernel(info, flags, own, inner, outer, core_a, chip_a, core_b, chip_b, moments, near, *t):
     core = info[0]
     scale = (flags[0], 1.0, flags[1])
 
-    for i in range(24):
-        k = min(max(i - 1, 0), 21)
-        a, b = from_core[k], from_chip[k]
-        up, down = jnp.where(core == 0, b, a) * scale[0], jnp.where(core == 0, a, b) * scale[2]
-        middle = (left, own, right)[i // 8][i % 8]
+    odd = info[3] == 1
+
+    def rows_beside(k, a, b):
+        up = jnp.where(core == 0, b[k], a[k]) * scale[0]
+        down = jnp.where(core == 0, a[k], b[k]) * scale[2]
+        return up, down
+
+    def put(i, up, middle, down):
         for h in range(2):
             t[0][i, h, 8:16] = halves(up)[h]
             t[0][i, h, 16:24] = halves(middle)[h]
             t[0][i, h, 24:32] = halves(down)[h]
+
+    for i in range(8):
+        up, down = rows_beside(i, core_a, chip_a)
+        put(8 + i, up, own[i], down)
+        k_left, k_right = max(i - 1, 0), min(i, 6)
+        for plane, k, swap in ((i, k_left, odd), (16 + i, k_right, jnp.logical_not(odd))):
+            near_rows = rows_beside(8 + k, core_a, chip_a)
+            far_rows = rows_beside(k, core_b, chip_b)
+            up, down = (jnp.where(swap, n, f) for n, f in zip(near_rows, far_rows))
+            put(plane, up, jnp.where(swap, inner[i], outer[i]), down)
 
     for j in range(1, PASSES + 1):
         blocks = (0, 1, 2) if j < PASSES else (1,)
@@ -479,7 +492,7 @@
     core = lax.axis_index("gx") % 2
     y = lax.axis_index("gy")
     flags = jnp.stack([(y > 0) | (core == 1), (y < count_y - 1) | (core == 0)]).astype(jnp.float32)
-    info = jnp.stack([core, recentre_cols[0], recentre_cols[1]]).astype(jnp.int32)
+    info = jnp.stack([core, recentre_cols[0], recentre_cols[1], (lax.axis_index("gx") // 2) % 2]).astype(jnp.int32)
     weight_map, node, coef = (jnp.asarray(a) for a in tables())
     first = core == 0
     pick = lambda a, b: jnp.where(first, a, b)
@@ -524,11 +537,14 @@
             [(3, 8, 8, NZ), (8, 8, NZ)],
             [(3, 14, 2, 24, HALF), (10, 2, 24, HALF), (3, 10, 2, 16, HALF)],
         )
-        s_left, s_right = beside(source, source, step == 0)
-        column = jnp.concatenate([s_left[1:], source, s_right[:7]], axis=0)
+        inner, outer = send(source, "inner"), send(source, "outer")
+        early = jnp.concatenate([source, jnp.where(odd, inner[1:8], inner[0:7])], axis=0)
+        early_core, early_chip = send(early, "core"), send(early, "across")
+        late = jnp.where(odd, outer[0:7], outer[1:8])
+        late_core, late_chip = send(late, "core"), send(late, "across")
         moments, near = call(
             powers_kernel,
-            (info, flags, source, s_left, s_right, send(column, "core"), send(column, "across")),
+            (info, flags, source, inner, outer, early_core, early_chip, late_core, late_chip),
             2,
             [(count_x * count_y, 128), (PASSES, 10, 2, 16, HALF)],
             [(24, 2, 40, HALF)] * (PASSES + 1),

time: 117 us -> 114 us (0.974)
  waiting for transfers between devices: 43.6 us -> 37.1 us
  starting transfers between devices: 34.8 us -> 38.3 us
    ppermute x18 -> x22, waiting for transfers between devices: 30.8 us -> 24.3 us  [body(): send = lambda value, name: lax.ppermute(value, AXES, route[name])]
    ppermute x18 -> x22, starting transfers between devices: 28.8 us -> 32 us  [body(): send = lambda value, name: lax.ppermute(value, AXES, route[name])]
  transfers between devices with their start and end apart: 19 -> 23, of which waited for: 13 -> 14; matrix products, arithmetic and copies ran while one was open for 1% -> 1% of each run, Pallas kernels for 0% -> 0%
where the time goes in v5:
time: 114 us
  starting transfers between devices  38.3 us (34%)
  waiting for transfers between devices  37.1 us (33%)
  blocking collectives  21.5 us (19%)
  Pallas kernels  11.6 us (10%)
  local copies, waits for them, and re-layouts  2.62 us (2%)
  between operations  1.61 us (1%)
  other arithmetic  1.15 us (1%)
    ppermute x22, starting transfers between devices, body(): send = lambda value, name: lax.ppermute(value, AXES, route[name])  32 us
    ppermute x22, waiting for transfers between devices, body(): send = lambda value, name: lax.ppermute(value, AXES, route[name])  24.3 us
    all_to_all x1, blocking collectives, body(): moments = lax.all_to_all(moments, AXES, 0, 0)  21.5 us
    all_to_all x1, waiting for transfers between devices, body(): moments = lax.all_to_all(moments, AXES, 0, 0)  12.8 us
    pallas_call x8, Pallas kernels, call(): pl.pallas_call(kernel, in_specs=[SMEM] * smem + [VMEM] * (len(args) - sme...  11.6 us
    all_to_all x1, starting transfers between devices, body(): moments = lax.all_to_all(moments, AXES, 0, 0)  6.32 us
    unnamed x16, local copies, waits for them, and re-layouts  2.55 us
  transfers between devices with their start and end apart: 23, of which 14 were waited for; matrix products, arithmetic and copies ran while one was open for 1% of the time, Pallas kernels for 0%

profile of v5, /device:TPU:1, one launch (start us, length us, event | category | flops | bytes accessed | tf_op | source)
XLA Modules:
  0.0 113.8 jit_solution(13222045025028762039)
XLA Ops:
  2.4 2.7 %collective-permute-start.18 = (f32[13,8,256]{2,1,0:T(8,128)S(1)}, f32[13,8,256]{2,1,0:T(8,128)S(1)}, u32[]{:S(2)}, u32[]{:S(2)}) collective-permute-start(f32[13,8,256]{2,1,0:T(8,128)S(1)} %get-tuple-element.213), channel_id=1, source_target_pairs={{0,252},{1,253},{2,254},{3,255},{4,8},{5,9},{6,10},{7,11},{8,4},{9... | collective-permute-start | bytes 319496 | tf_op jit(solution)/shard_map/ppermute | solution.py:491
  6.3 6.0 %collective-permute-start.20 = (f32[16,8,256]{2,1,0:T(8,128)S(1)}, f32[16,8,256]{2,1,0:T(8,128)S(1)}, u32[]{:S(2)}, u32[]{:S(2)}) collective-permute-start(f32[16,8,256]{2,1,0:T(8,128)S(1)} %get-tuple-element.216), channel_id=1, source_target_pairs={{0,4},{1,5},{2,6},{3,7},{4,0},{5,1},{6,2},{7,3},{8,12},{9,13},{10,... | collective-permute-start | bytes 393224 | tf_op jit(solution)/shard_map/ppermute | solution.py:491
  14.8 2.0 %collective-permute-start.21 = (f32[4,12,2,256]{3,2,1,0:T(2,128)S(1)}, f32[4,12,2,256]{3,2,1,0:T(2,128)S(1)}, u32[]{:S(2)}, u32[]{:S(2)}) collective-permute-start(f32[4,12,2,256]{3,2,1,0:T(2,128)S(1)} %bitcast.109), channel_id=1, source_target_pairs={{0,4},{1,5},{2,6},{3,7},{4,0},{5,1},{6,2},{7,3},{8,12},{9,13},{10,... | collective-permute-start | bytes 294920 | tf_op jit(solution)/shard_map/ppermute | solution.py:491
  18.0 3.0 %collective-permute-done.22.from_chip = f32[4,12,2,256]{3,2,1,0:T(2,128)S(1)} collective-permute-done((f32[4,12,2,256]{3,2,1,0:T(2,128)S(1)}, f32[4,12,2,256]{3,2,1,0:T(2,128)S(1)}, u32[]{:S(2)}, u32[]{:S(2)}) %collective-permute-start.22) | collective-permute-done | bytes 98336 | tf_op jit(solution)/shard_map/ppermute | solution.py:491
  21.0 1.4 %shard_map.87 = (f32[3,8,8,256]{3,2,1,0:T(8,128)S(1)}, f32[8,8,256]{2,1,0:T(8,128)S(1)}) custom-call(s32[4]{0:T(128)S(1)} %pad_add_fusion.info, f32[2]{0:T(128)S(1)} %add_convert_fusion.flags, f32[8,3]{1,0:T(8,128)S(1)} %copy.23.speed, f32[3,4,8,256]{3,2,1,0:T(8,128)S(1)} %bitcast.94, f32[3,8,8,256]{3,2,1,0:T(8,128)S(1)} %pad_maximum_fusion.10.own, ...), custom_call_target="tpu_custom_call" | custom-call | flops 1000000 | bytes 1000000 | tf_op jit(solution)/shard_map/pallas_call | solution.py:452
  22.5 4.3 %collective-permute-start.24 = (f32[8,8,256]{2,1,0:T(8,128)S(1)}, f32[8,8,256]{2,1,0:T(8,128)S(1)}, u32[]{:S(2)}, u32[]{:S(2)}) collective-permute-start(f32[8,8,256]{2,1,0:T(8,128)S(1)} %get-tuple-element.217.own), channel_id=1, source_target_pairs={{0,248},{1,249},{2,250},{3,251},{4,252},{5,253},{6,254},{7,255},{8... | collective-permute-start | bytes 196616 | tf_op jit(solution)/shard_map/ppermute | solution.py:491
  26.8 1.5 %collective-permute-start.25 = (f32[15,8,256]{2,1,0:T(8,128)S(1)}, f32[15,8,256]{2,1,0:T(8,128)S(1)}, u32[]{:S(2)}, u32[]{:S(2)}) collective-permute-start(f32[15,8,256]{2,1,0:T(8,128)S(1)} %pad_maximum_fusion.11), channel_id=1, source_target_pairs={{0,4},{1,5},{2,6},{3,7},{4,0},{5,1},{6,2},{7,3},{8,12},{9,13},{10,... | collective-permute-start | bytes 368648 | tf_op jit(solution)/shard_map/ppermute | solution.py:491
  29.1 2.3 %collective-permute-start.27 = (f32[7,8,256]{2,1,0:T(8,128)S(1)}, f32[7,8,256]{2,1,0:T(8,128)S(1)}, u32[]{:S(2)}, u32[]{:S(2)}) collective-permute-start(f32[7,8,256]{2,1,0:T(8,128)S(1)} %slice_select_fusion.4), channel_id=1, source_target_pairs={{0,4},{1,5},{2,6},{3,7},{4,0},{5,1},{6,2},{7,3},{8,12},{9,13},{10,... | collective-permute-start | bytes 172040 | tf_op jit(solution)/shard_map/ppermute | solution.py:491
  32.3 2.7 %collective-permute-done.28.chip_b = f32[7,8,256]{2,1,0:T(8,128)S(1)} collective-permute-done((f32[7,8,256]{2,1,0:T(8,128)S(1)}, f32[7,8,256]{2,1,0:T(8,128)S(1)}, u32[]{:S(2)}, u32[]{:S(2)}) %collective-permute-start.28) | collective-permute-done | bytes 57376 | tf_op jit(solution)/shard_map/ppermute | solution.py:491
  35.0 2.4 %shard_map.88 = (f32[256,128]{1,0:T(8,128)S(1)}, f32[8,10,2,16,128]{4,3,2,1,0:T(8,128)S(1)}) custom-call(s32[4]{0:T(128)S(1)} %pad_add_fusion.info, f32[2]{0:T(128)S(1)} %add_convert_fusion.flags, f32[8,8,256]{2,1,0:T(8,128)S(1)} %get-tuple-element.217.own, f32[8,8,256]{2,1,0:T(8,128)S(1)} %collective-permute-done.23.inner, ...), custom_call_target="tpu_custom_call" | custom-call | flops 1000000 | bytes 1000000 | tf_op jit(solution)/shard_map/pallas_call | solution.py:452
  37.5 21.5 %all_to_all.22 = f32[256,1,128]{2,1,0:T(1,128)S(1)} all-to-all(f32[256,1,128]{2,1,0:T(1,128)S(1)} %bitcast.97), channel_id=1, replica_groups=mesh['gx'=64,'gy'=4] {'gx','gy'}, dimensions={0} | all-to-all | bytes 262144 | tf_op jit(solution)/shard_map/all_to_all | solution.py:552
  60.6 5.8 %collective-permute-done.29 = f32[3,4,8,256]{3,2,1,0:T(8,128)S(1)} collective-permute-done((f32[3,4,8,256]{3,2,1,0:T(8,128)S(1)}, f32[3,4,8,256]{3,2,1,0:T(8,128)S(1)}, u32[]{:S(2)}, u32[]{:S(2)}) %collective-permute-start.29) | collective-permute-done | bytes 98336 | tf_op jit(solution)/shard_map/ppermute | solution.py:491
  66.5 2.0 %collective-permute-start.31 = (f32[3,12,2,256]{3,2,1,0:T(2,128)S(1)}, f32[3,12,2,256]{3,2,1,0:T(2,128)S(1)}, u32[]{:S(2)}, u32[]{:S(2)}) collective-permute-start(f32[3,12,2,256]{3,2,1,0:T(2,128)S(1)} %bitcast.110), channel_id=1, source_target_pairs={{0,4},{1,5},{2,6},{3,7},{4,0},{5,1},{6,2},{7,3},{8,12},{9,13},{10,... | collective-permute-start | bytes 221192 | tf_op jit(solution)/shard_map/ppermute | solution.py:491
  69.3 3.2 %collective-permute-done.32.from_chip = f32[3,12,2,256]{3,2,1,0:T(2,128)S(1)} collective-permute-done((f32[3,12,2,256]{3,2,1,0:T(2,128)S(1)}, f32[3,12,2,256]{3,2,1,0:T(2,128)S(1)}, u32[]{:S(2)}, u32[]{:S(2)}) %collective-permute-start.32) | collective-permute-done | bytes 73760 | tf_op jit(solution)/shard_map/ppermute | solution.py:491
  72.5 1.4 %shard_map.90 = (f32[3,8,8,256]{3,2,1,0:T(8,128)S(1)}, f32[8,8,256]{2,1,0:T(8,128)S(1)}) custom-call(s32[4]{0:T(128)S(1)} %pad_add_fusion.info, f32[2]{0:T(128)S(1)} %add_convert_fusion.flags, f32[8,3]{1,0:T(8,128)S(1)} %copy.23.speed, f32[3,4,8,256]{3,2,1,0:T(8,128)S(1)} %broadcast_select_fusion.10.left, f32[3,8,8,256]{3,2,1,0:T(8,128)S(1)} %get-tuple-element.221.own, ...), custom_call_target="tpu_custom_call" | custom-call | flops 1000000 | bytes 1000000 | tf_op jit(solution)/shard_map/pallas_call | solution.py:452
  74.0 1.8 %collective-permute-start.34 = (f32[8,8,256]{2,1,0:T(8,128)S(1)}, f32[8,8,256]{2,1,0:T(8,128)S(1)}, u32[]{:S(2)}, u32[]{:S(2)}) collective-permute-start(f32[8,8,256]{2,1,0:T(8,128)S(1)} %get-tuple-element.222.own), channel_id=1, source_target_pairs={{0,248},{1,249},{2,250},{3,251},{4,252},{5,253},{6,254},{7,255},{8... | collective-permute-start | bytes 196616 | tf_op jit(solution)/shard_map/ppermute | solution.py:491
  77.1 2.3 %collective-permute-start.35 = (f32[15,8,256]{2,1,0:T(8,128)S(1)}, f32[15,8,256]{2,1,0:T(8,128)S(1)}, u32[]{:S(2)}, u32[]{:S(2)}) collective-permute-start(f32[15,8,256]{2,1,0:T(8,128)S(1)} %pad_maximum_fusion.12), channel_id=1, source_target_pairs={{0,4},{1,5},{2,6},{3,7},{4,0},{5,1},{6,2},{7,3},{8,12},{9,13},{10,... | collective-permute-start | bytes 368648 | tf_op jit(solution)/shard_map/ppermute | solution.py:491
  80.5 2.3 %collective-permute-start.37 = (f32[7,8,256]{2,1,0:T(8,128)S(1)}, f32[7,8,256]{2,1,0:T(8,128)S(1)}, u32[]{:S(2)}, u32[]{:S(2)}) collective-permute-start(f32[7,8,256]{2,1,0:T(8,128)S(1)} %slice_select_fusion.2), channel_id=1, source_target_pairs={{0,4},{1,5},{2,6},{3,7},{4,0},{5,1},{6,2},{7,3},{8,12},{9,13},{10,... | collective-permute-start | bytes 172040 | tf_op jit(solution)/shard_map/ppermute | solution.py:491
  83.7 2.7 %collective-permute-done.38.chip_b = f32[7,8,256]{2,1,0:T(8,128)S(1)} collective-permute-done((f32[7,8,256]{2,1,0:T(8,128)S(1)}, f32[7,8,256]{2,1,0:T(8,128)S(1)}, u32[]{:S(2)}, u32[]{:S(2)}) %collective-permute-start.38) | collective-permute-done | bytes 57376 | tf_op jit(solution)/shard_map/ppermute | solution.py:491
  86.4 3.1 %shard_map.91 = (f32[256,128]{1,0:T(8,128)}, f32[8,10,2,16,128]{4,3,2,1,0:T(8,128)S(1)}) custom-call(s32[4]{0:T(128)S(1)} %pad_add_fusion.info, f32[2]{0:T(128)S(1)} %add_convert_fusion.flags, f32[8,8,256]{2,1,0:T(8,128)S(1)} %get-tuple-element.222.own, f32[8,8,256]{2,1,0:T(8,128)S(1)} %collective-permute-done.33.inner, ...), custom_call_target="tpu_custom_call" | custom-call | flops 1000000 | bytes 1000000 | tf_op jit(solution)/shard_map/pallas_call | solution.py:452
  89.5 6.3 %all-to-all-start.1 = ((f32[256,1,128]{2,1,0:T(1,128)}), f32[256,1,128]{2,1,0:T(1,128)S(1)}, u32[]{:S(2)}, u32[]{:S(2)}) async-start(f32[256,1,128]{2,1,0:T(1,128)} %bitcast.40), calls=%async_computation.1 | async-start | bytes 262144 | tf_op jit(solution)/shard_map/all_to_all | solution.py:552
  95.8 12.8 %all-to-all-done.1 = f32[256,1,128]{2,1,0:T(1,128)S(1)} async-done(((f32[256,1,128]{2,1,0:T(1,128)}), f32[256,1,128]{2,1,0:T(1,128)S(1)}, u32[]{:S(2)}, u32[]{:S(2)}) %all-to-all-start.1) | async-done | bytes 131104 | tf_op jit(solution)/shard_map/all_to_all | solution.py:552
  108.6 1.5 %shard_map.92 = (s32[1]{0:T(128)}, f32[4,4,8,256]{3,2,1,0:T(8,128)S(1)}, f32[4,4,8,256]{3,2,1,0:T(8,128)S(1)}) custom-call(s32[4]{0:T(128)S(1)} %pad_add_fusion.info, f32[256,128]{1,0:T(8,128)S(1)} %bitcast.95, f32[16,128]{1,0:T(8,128)S(1)} %copy-done.3, f32[16,128]{1,0:T(8,128)S(1)} %copy-done.4, f32[8,16,128]{2,1,0:T(8,128)S(1)} %copy-done, ...), custom_call_target="tpu_custom_call" | custom-call | flops 1000000 | bytes 1000000 | tf_op jit(solution)/shard_map/pallas_call | solution.py:452
  110.8 3.1 %conditional.1 = ((f32[3,4,16,256]{3,2,1,0:T(8,128)}, f32[4,16,256]{2,1,0:T(8,128)})) conditional(s32[]{:T(128)} %bitcast.42, (pred[]{:T(512)}, f32[16,8,256]{2,1,0:T(8,128)S(1)}, f32[16,8,256]{2,1,0:T(8,128)S(1)}, s32[2]{0:T(128)S(1)}, f32[8,3]{0,1:T(4,128)S(1)}) %tuple.189, (f32[4,4,8,256]{3,2,1,0:T(8,128)S(1)}, s32[4]{0:T(128)S(1)}, ...), branch_computations={%region_0.9_spmd, %region_9.10_spmd} | conditional | flops 3892455 | bytes 14964919 | solution.py:576
  (79 shorter events, 17.5 us)
Async XLA Ops:
  2.4 11.5 %collective-permute-start.18 = (f32[13,8,256]{2,1,0:T(8,128)S(1)}, f32[13,8,256]{2,1,0:T(8,128)S(1)}, u32[]{:S(2)}, u32[]{:S(2)}) collective-permute-start(f32[13,8,256]{2,1,0:T(8,128)S(1)} %get-tuple-element.213), channel_id=1, source_target_pairs={{0,252},{1,253},{2,254},{3,255},{4,8},{5,9},{6,10},{7,11},{8,4},{9... | collective-permute-start | bytes 319496 | tf_op jit(solution)/shard_map/ppermute | solution.py:491
  5.1 9.2 %collective-permute-start.19 = (f32[13,8,256]{2,1,0:T(8,128)S(1)}, f32[13,8,256]{2,1,0:T(8,128)S(1)}, u32[]{:S(2)}, u32[]{:S(2)}) collective-permute-start(f32[13,8,256]{2,1,0:T(8,128)S(1)} %get-tuple-element.214), channel_id=1, source_target_pairs={{0,248},{1,249},{2,250},{3,251},{4,12},{5,13},{6,14},{7,15},{8,0},... | collective-permute-start | bytes 319496 | tf_op jit(solution)/shard_map/ppermute | solution.py:491
  6.3 8.1 %collective-permute-start.20 = (f32[16,8,256]{2,1,0:T(8,128)S(1)}, f32[16,8,256]{2,1,0:T(8,128)S(1)}, u32[]{:S(2)}, u32[]{:S(2)}) collective-permute-start(f32[16,8,256]{2,1,0:T(8,128)S(1)} %get-tuple-element.216), channel_id=1, source_target_pairs={{0,4},{1,5},{2,6},{3,7},{4,0},{5,1},{6,2},{7,3},{8,12},{9,13},{10,... | collective-permute-start | bytes 393224 | tf_op jit(solution)/shard_map/ppermute | solution.py:491
  14.7 44.2 %copy-start = (f32[8,16,128]{2,1,0:T(8,128)S(1)}, f32[8,16,128]{2,1,0:T(8,128)}, u32[]{:S(2)}) copy-start(f32[8,16,128]{2,1,0:T(8,128)} %constant.279.clone.coef) | copy-start | bytes 196612
  14.8 3.2 %collective-permute-start.21 = (f32[4,12,2,256]{3,2,1,0:T(2,128)S(1)}, f32[4,12,2,256]{3,2,1,0:T(2,128)S(1)}, u32[]{:S(2)}, u32[]{:S(2)}) collective-permute-start(f32[4,12,2,256]{3,2,1,0:T(2,128)S(1)} %bitcast.109), channel_id=1, source_target_pairs={{0,4},{1,5},{2,6},{3,7},{4,0},{5,1},{6,2},{7,3},{8,12},{9,13},{10,... | collective-permute-start | bytes 294920 | tf_op jit(solution)/shard_map/ppermute | solution.py:491
  16.7 4.3 %collective-permute-start.22 = (f32[4,12,2,256]{3,2,1,0:T(2,128)S(1)}, f32[4,12,2,256]{3,2,1,0:T(2,128)S(1)}, u32[]{:S(2)}, u32[]{:S(2)}) collective-permute-start(f32[4,12,2,256]{3,2,1,0:T(2,128)S(1)} %get-tuple-element.304), channel_id=1, source_target_pairs={{0,7},{1,4},{2,5},{3,6},{4,1},{5,2},{6,3},{7,0},{8,15},{9,12},{10,... | collective-permute-start | bytes 294920 | tf_op jit(solution)/shard_map/ppermute | solution.py:491
  22.4 4.4 %collective-permute-start.23 = (f32[8,8,256]{2,1,0:T(8,128)S(1)}, f32[8,8,256]{2,1,0:T(8,128)S(1)}, u32[]{:S(2)}, u32[]{:S(2)}) collective-permute-start(f32[8,8,256]{2,1,0:T(8,128)S(1)} %get-tuple-element.217.own), channel_id=1, source_target_pairs={{0,8},{1,9},{2,10},{3,11},{4,12},{5,13},{6,14},{7,15},{8,0},{9,1},... | collective-permute-start | bytes 196616 | tf_op jit(solution)/shard_map/ppermute | solution.py:491
  22.5 6.5 %collective-permute-start.24 = (f32[8,8,256]{2,1,0:T(8,128)S(1)}, f32[8,8,256]{2,1,0:T(8,128)S(1)}, u32[]{:S(2)}, u32[]{:S(2)}) collective-permute-start(f32[8,8,256]{2,1,0:T(8,128)S(1)} %get-tuple-element.217.own), channel_id=1, source_target_pairs={{0,248},{1,249},{2,250},{3,251},{4,252},{5,253},{6,254},{7,255},{8... | collective-permute-start | bytes 196616 | tf_op jit(solution)/shard_map/ppermute | solution.py:491
  26.8 8.2 %collective-permute-start.25 = (f32[15,8,256]{2,1,0:T(8,128)S(1)}, f32[15,8,256]{2,1,0:T(8,128)S(1)}, u32[]{:S(2)}, u32[]{:S(2)}) collective-permute-start(f32[15,8,256]{2,1,0:T(8,128)S(1)} %pad_maximum_fusion.11), channel_id=1, source_target_pairs={{0,4},{1,5},{2,6},{3,7},{4,0},{5,1},{6,2},{7,3},{8,12},{9,13},{10,... | collective-permute-start | bytes 368648 | tf_op jit(solution)/shard_map/ppermute | solution.py:491
  28.3 6.7 %collective-permute-start.26 = (f32[15,8,256]{2,1,0:T(8,128)S(1)}, f32[15,8,256]{2,1,0:T(8,128)S(1)}, u32[]{:S(2)}, u32[]{:S(2)}) collective-permute-start(f32[15,8,256]{2,1,0:T(8,128)S(1)} %pad_maximum_fusion.11), channel_id=1, source_target_pairs={{0,7},{1,4},{2,5},{3,6},{4,1},{5,2},{6,3},{7,0},{8,15},{9,12},{10,... | collective-permute-start | bytes 368648 | tf_op jit(solution)/shard_map/ppermute | solution.py:491
  29.1 3.2 %collective-permute-start.27 = (f32[7,8,256]{2,1,0:T(8,128)S(1)}, f32[7,8,256]{2,1,0:T(8,128)S(1)}, u32[]{:S(2)}, u32[]{:S(2)}) collective-permute-start(f32[7,8,256]{2,1,0:T(8,128)S(1)} %slice_select_fusion.4), channel_id=1, source_target_pairs={{0,4},{1,5},{2,6},{3,7},{4,0},{5,1},{6,2},{7,3},{8,12},{9,13},{10,... | collective-permute-start | bytes 172040 | tf_op jit(solution)/shard_map/ppermute | solution.py:491
  31.4 3.6 %collective-permute-start.28 = (f32[7,8,256]{2,1,0:T(8,128)S(1)}, f32[7,8,256]{2,1,0:T(8,128)S(1)}, u32[]{:S(2)}, u32[]{:S(2)}) collective-permute-start(f32[7,8,256]{2,1,0:T(8,128)S(1)} %slice_select_fusion.4), channel_id=1, source_target_pairs={{0,7},{1,4},{2,5},{3,6},{4,1},{5,2},{6,3},{7,0},{8,15},{9,12},{10,... | collective-permute-start | bytes 172040 | tf_op jit(solution)/shard_map/ppermute | solution.py:491
  59.5 6.9 %collective-permute-start.29 = (f32[3,4,8,256]{3,2,1,0:T(8,128)S(1)}, f32[3,4,8,256]{3,2,1,0:T(8,128)S(1)}, u32[]{:S(2)}, u32[]{:S(2)}) collective-permute-start(f32[3,4,8,256]{3,2,1,0:T(8,128)S(1)} %get-tuple-element.373), channel_id=1, source_target_pairs={{0,248},{1,249},{2,250},{3,251},{4,252},{5,253},{6,254},{7,255},{8... | collective-permute-start | bytes 294920 | tf_op jit(solution)/shard_map/ppermute | solution.py:491
  60.1 6.2 %collective-permute-start.30 = (f32[3,4,8,256]{3,2,1,0:T(8,128)S(1)}, f32[3,4,8,256]{3,2,1,0:T(8,128)S(1)}, u32[]{:S(2)}, u32[]{:S(2)}) collective-permute-start(f32[3,4,8,256]{3,2,1,0:T(8,128)S(1)} %get-tuple-element.372), channel_id=1, source_target_pairs={{0,8},{1,9},{2,10},{3,11},{4,12},{5,13},{6,14},{7,15},{8,0},{9,1},... | collective-permute-start | bytes 294920 | tf_op jit(solution)/shard_map/ppermute | solution.py:491
  66.5 2.9 %collective-permute-start.31 = (f32[3,12,2,256]{3,2,1,0:T(2,128)S(1)}, f32[3,12,2,256]{3,2,1,0:T(2,128)S(1)}, u32[]{:S(2)}, u32[]{:S(2)}) collective-permute-start(f32[3,12,2,256]{3,2,1,0:T(2,128)S(1)} %bitcast.110), channel_id=1, source_target_pairs={{0,4},{1,5},{2,6},{3,7},{4,0},{5,1},{6,2},{7,3},{8,12},{9,13},{10,... | collective-permute-start | bytes 221192 | tf_op jit(solution)/shard_map/ppermute | solution.py:491
  68.4 4.1 %collective-permute-start.32 = (f32[3,12,2,256]{3,2,1,0:T(2,128)S(1)}, f32[3,12,2,256]{3,2,1,0:T(2,128)S(1)}, u32[]{:S(2)}, u32[]{:S(2)}) collective-permute-start(f32[3,12,2,256]{3,2,1,0:T(2,128)S(1)} %get-tuple-element.301), channel_id=1, source_target_pairs={{0,7},{1,4},{2,5},{3,6},{4,1},{5,2},{6,3},{7,0},{8,15},{9,12},{10,... | collective-permute-start | bytes 221192 | tf_op jit(solution)/shard_map/ppermute | solution.py:491
  73.9 3.2 %collective-permute-start.33 = (f32[8,8,256]{2,1,0:T(8,128)S(1)}, f32[8,8,256]{2,1,0:T(8,128)S(1)}, u32[]{:S(2)}, u32[]{:S(2)}) collective-permute-start(f32[8,8,256]{2,1,0:T(8,128)S(1)} %get-tuple-element.222.own), channel_id=1, source_target_pairs={{0,8},{1,9},{2,10},{3,11},{4,12},{5,13},{6,14},{7,15},{8,0},{9,1},... | collective-permute-start | bytes 196616 | tf_op jit(solution)/shard_map/ppermute | solution.py:491
  74.0 6.5 %collective-permute-start.34 = (f32[8,8,256]{2,1,0:T(8,128)S(1)}, f32[8,8,256]{2,1,0:T(8,128)S(1)}, u32[]{:S(2)}, u32[]{:S(2)}) collective-permute-start(f32[8,8,256]{2,1,0:T(8,128)S(1)} %get-tuple-element.222.own), channel_id=1, source_target_pairs={{0,248},{1,249},{2,250},{3,251},{4,252},{5,253},{6,254},{7,255},{8... | collective-permute-start | bytes 196616 | tf_op jit(solution)/shard_map/ppermute | solution.py:491
  77.1 9.3 %collective-permute-start.35 = (f32[15,8,256]{2,1,0:T(8,128)S(1)}, f32[15,8,256]{2,1,0:T(8,128)S(1)}, u32[]{:S(2)}, u32[]{:S(2)}) collective-permute-start(f32[15,8,256]{2,1,0:T(8,128)S(1)} %pad_maximum_fusion.12), channel_id=1, source_target_pairs={{0,4},{1,5},{2,6},{3,7},{4,0},{5,1},{6,2},{7,3},{8,12},{9,13},{10,... | collective-permute-start | bytes 368648 | tf_op jit(solution)/shard_map/ppermute | solution.py:491
  79.4 7.0 %collective-permute-start.36 = (f32[15,8,256]{2,1,0:T(8,128)S(1)}, f32[15,8,256]{2,1,0:T(8,128)S(1)}, u32[]{:S(2)}, u32[]{:S(2)}) collective-permute-start(f32[15,8,256]{2,1,0:T(8,128)S(1)} %pad_maximum_fusion.12), channel_id=1, source_target_pairs={{0,7},{1,4},{2,5},{3,6},{4,1},{5,2},{6,3},{7,0},{8,15},{9,12},{10,... | collective-permute-start | bytes 368648 | tf_op jit(solution)/shard_map/ppermute | solution.py:491
  80.5 3.1 %collective-permute-start.37 = (f32[7,8,256]{2,1,0:T(8,128)S(1)}, f32[7,8,256]{2,1,0:T(8,128)S(1)}, u32[]{:S(2)}, u32[]{:S(2)}) collective-permute-start(f32[7,8,256]{2,1,0:T(8,128)S(1)} %slice_select_fusion.2), channel_id=1, source_target_pairs={{0,4},{1,5},{2,6},{3,7},{4,0},{5,1},{6,2},{7,3},{8,12},{9,13},{10,... | collective-permute-start | bytes 172040 | tf_op jit(solution)/shard_map/ppermute | solution.py:491
  82.8 3.6 %collective-permute-start.38 = (f32[7,8,256]{2,1,0:T(8,128)S(1)}, f32[7,8,256]{2,1,0:T(8,128)S(1)}, u32[]{:S(2)}, u32[]{:S(2)}) collective-permute-start(f32[7,8,256]{2,1,0:T(8,128)S(1)} %slice_select_fusion.2), channel_id=1, source_target_pairs={{0,7},{1,4},{2,5},{3,6},{4,1},{5,2},{6,3},{7,0},{8,15},{9,12},{10,... | collective-permute-start | bytes 172040 | tf_op jit(solution)/shard_map/ppermute | solution.py:491
  89.5 19.1 %all-to-all-start.1 = ((f32[256,1,128]{2,1,0:T(1,128)}), f32[256,1,128]{2,1,0:T(1,128)S(1)}, u32[]{:S(2)}, u32[]{:S(2)}) async-start(f32[256,1,128]{2,1,0:T(1,128)} %bitcast.40), calls=%async_computation.1 | async-start | bytes 262144 | tf_op jit(solution)/shard_map/all_to_all | solution.py:552
  110.8 1.8 %collective-permute-start = (f32[4,4,8,256]{3,2,1,0:T(8,128)S(1)}, f32[4,4,8,256]{3,2,1,0:T(8,128)S(1)}, u32[]{:S(2)}, u32[]{:S(2)}) collective-permute-start(f32[4,4,8,256]{3,2,1,0:T(8,128)S(1)} %get-tuple-element.193), channel_id=1, source_target_pairs={{0,4},{1,5},{2,6},{3,7},{4,0},{5,1},{6,2},{7,3},{8,12},{9,13},{10,... | collective-permute-start | bytes 393224 | tf_op jit(solution)/shard_map/cond/branch_1_fun/ppermute | solution.py:491
  (6 other events, 150.7 us)

commit v6 on v5

--- a/solution.py
+++ b/solution.py
@@ -197,7 +197,7 @@
 
 
 def source_kernel(
-    info, flags, speed, left, own, right, from_core, from_chip, cell, cell_core, cell_chip, bodied, source, pad, ids, body, *, step
+    info, flags, speed, left, own, right, core_a, chip_a, core_b, chip_b, cell, cell_core, cell_chip, bodied, source, pad, ids, body, *, step
 ):
     core = info[0]
     joined = 2 - info[1 + step]
@@ -215,7 +215,10 @@
         for i in range(2):
             put(c, i + 12, right[c, i])
         for i in range(1, 13):
-            a, b = from_core[c, i - 1], from_chip[c, i - 1]
+            if 4 <= i < 12:
+                a, b = core_a[c, i - 4], chip_a[c, i - 4]
+            else:
+                a, b = core_b[c, min(i - 1, 3)], chip_b[c, min(i - 1, 3)]
             up = jnp.where(core == 0, b, a) * up_flag
             down = jnp.where(core == 0, a, b) * down_flag
             for h in range(2):
@@ -522,17 +525,20 @@
         if step:
             left, right = beside(own[:, 0:4], own[:, 4:8], False)
             right = right[:, 0:2]
-        joined = jnp.concatenate([left, own, right], axis=1)
+        near_planes, far_planes = own, jnp.concatenate([left[:, 1:4], right[:, 0:1]], axis=1)
         if not step:
-            spare = jnp.concatenate([cell[0:1], cell, cell[0:3]], axis=0)
-            joined = jnp.concatenate([joined, spare[None]], axis=0)
-        top, bottom = joined[:, 1:13, 0:2], joined[:, 1:13, 6:8]
-        from_core, from_chip = send(pick(bottom, top), "core"), send(pick(top, bottom), "across")
+            near_planes = jnp.concatenate([own, jnp.concatenate([cell[3:10], cell[9:10]], axis=0)[None]], axis=0)
+            far_planes = jnp.concatenate([far_planes, jnp.concatenate([cell[0:3], cell[2:3]], axis=0)[None]], axis=0)
+        edges = []
+        for planes_out in (near_planes, far_planes):
+            top, bottom = planes_out[:, :, 0:2], planes_out[:, :, 6:8]
+            edges += [send(pick(bottom, top), "core"), send(pick(top, bottom), "across")]
         if not step:
-            cell_core, cell_chip = from_core[3, 0:10], from_chip[3, 0:10]
+            cell_core = jnp.concatenate([edges[2][3, 0:3], edges[0][3, 0:7]], axis=0)
+            cell_chip = jnp.concatenate([edges[3][3, 0:3], edges[1][3, 0:7]], axis=0)
         bodied, source = call(
             functools.partial(source_kernel, step=step),
-            (info, flags, swimmer_speed, left, own, right, from_core, from_chip, cell, cell_core, cell_chip),
+            (info, flags, swimmer_speed, left, own, right, *edges, cell, cell_core, cell_chip),
             3,
             [(3, 8, 8, NZ), (8, 8, NZ)],
             [(3, 14, 2, 24, HALF), (10, 2, 24, HALF), (3, 10, 2, 16, HALF)],

time: 114 us -> 116 us (1.018)
  blocking collectives: 21.5 us -> 0 us
  waiting for transfers between devices: 37.1 us -> 53 us
  starting transfers between devices: 38.3 us -> 44.4 us
    all_to_all x1 -> x0, blocking collectives: 21.5 us -> none  [body(): moments = lax.all_to_all(moments, AXES, 0, 0)]
    all_to_all x1 -> x2, waiting for transfers between devices: 12.8 us -> 25.5 us  [body(): moments = lax.all_to_all(moments, AXES, 0, 0)]
    all_to_all x1 -> x2, starting transfers between devices: 6.32 us -> 14.4 us  [body(): moments = lax.all_to_all(moments, AXES, 0, 0)]
    ppermute x22 -> x26, waiting for transfers between devices: 24.3 us -> 27.5 us  [body(): send = lambda value, name: lax.ppermute(value, AXES, route[name])]
    ppermute x22 -> x26, starting transfers between devices: 32 us -> 30 us  [body(): send = lambda value, name: lax.ppermute(value, AXES, route[name])]
    unnamed x16 -> x15, local copies, waits for them, and re-layouts: 2.55 us -> 2.54 us
  transfers between devices with their start and end apart: 23 -> 28, of which waited for: 14 -> 17; matrix products, arithmetic and copies ran while one was open for 1% -> 2% of each run, Pallas kernels for 0% -> 0%
where the time goes in v6:
time: 116 us; the launch traced here: 115 us
  waiting for transfers between devices  53 us (46%)
  starting transfers between devices  44.4 us (38%)
  Pallas kernels  12.2 us (11%)
  local copies, waits for them, and re-layouts  2.64 us (2%)
  between operations  1.7 us (1%)
  other arithmetic  1.16 us (1%)
    ppermute x26, starting transfers between devices, body(): send = lambda value, name: lax.ppermute(value, AXES, route[name])  30 us
    ppermute x26, waiting for transfers between devices, body(): send = lambda value, name: lax.ppermute(value, AXES, route[name])  27.5 us
    all_to_all x2, waiting for transfers between devices, body(): moments = lax.all_to_all(moments, AXES, 0, 0)  25.5 us
    all_to_all x2, starting transfers between devices, body(): moments = lax.all_to_all(moments, AXES, 0, 0)  14.4 us
    pallas_call x8, Pallas kernels, call(): pl.pallas_call(kernel, in_specs=[SMEM] * smem + [VMEM] * (len(args) - sme...  12.2 us
    unnamed x15, local copies, waits for them, and re-layouts  2.54 us
  transfers between devices with their start and end apart: 28, of which 17 were waited for; matrix products, arithmetic and copies ran while one was open for 2% of the time, Pallas kernels for 0%

profile of v6, /device:TPU:1, one launch (start us, length us, event | category | flops | bytes accessed | tf_op | source)
XLA Modules:
  0.0 115.3 jit_solution(3790085966936486256)
XLA Ops:
  2.4 3.3 %collective-permute-start.20 = (f32[16,8,256]{2,1,0:T(8,128)S(1)}, f32[16,8,256]{2,1,0:T(8,128)S(1)}, u32[]{:S(2)}, u32[]{:S(2)}) collective-permute-start(f32[16,8,256]{2,1,0:T(8,128)S(1)} %get-tuple-element.216), channel_id=1, source_target_pairs={{0,4},{1,5},{2,6},{3,7},{4,0},{5,1},{6,2},{7,3},{8,12},{9,13},{10,... | collective-permute-start | bytes 393224 | tf_op jit(solution)/shard_map/ppermute | solution.py:494
  8.0 1.9 %collective-permute-done.18 = f32[13,8,256]{2,1,0:T(8,128)S(1)} collective-permute-done((f32[13,8,256]{2,1,0:T(8,128)S(1)}, f32[13,8,256]{2,1,0:T(8,128)S(1)}, u32[]{:S(2)}, u32[]{:S(2)}) %collective-permute-start.18) | collective-permute-done | bytes 106528 | tf_op jit(solution)/shard_map/ppermute | solution.py:494
  9.9 5.1 %collective-permute-done.19 = f32[13,8,256]{2,1,0:T(8,128)S(1)} collective-permute-done((f32[13,8,256]{2,1,0:T(8,128)S(1)}, f32[13,8,256]{2,1,0:T(8,128)S(1)}, u32[]{:S(2)}, u32[]{:S(2)}) %collective-permute-start.19) | collective-permute-done | bytes 106528 | tf_op jit(solution)/shard_map/ppermute | solution.py:494
  15.3 3.1 %collective-permute-start.24 = (f32[4,4,2,256]{3,2,1,0:T(2,128)S(1)}, f32[4,4,2,256]{3,2,1,0:T(2,128)S(1)}, u32[]{:S(2)}, u32[]{:S(2)}) collective-permute-start(f32[4,4,2,256]{3,2,1,0:T(2,128)S(1)} %get-tuple-element.304), channel_id=1, source_target_pairs={{0,7},{1,4},{2,5},{3,6},{4,1},{5,2},{6,3},{7,0},{8,15},{9,12},{10,... | collective-permute-start | bytes 98312 | tf_op jit(solution)/shard_map/ppermute | solution.py:494
  18.7 1.8 %collective-permute-start.23 = (f32[4,4,2,256]{3,2,1,0:T(2,128)S(1)}, f32[4,4,2,256]{3,2,1,0:T(2,128)S(1)}, u32[]{:S(2)}, u32[]{:S(2)}) collective-permute-start(f32[4,4,2,256]{3,2,1,0:T(2,128)S(1)} %bitcast.121), channel_id=1, source_target_pairs={{0,4},{1,5},{2,6},{3,7},{4,0},{5,1},{6,2},{7,3},{8,12},{9,13},{10,... | collective-permute-start | bytes 98312 | tf_op jit(solution)/shard_map/ppermute | solution.py:494
  24.2 4.3 %collective-permute-start.26 = (f32[8,8,256]{2,1,0:T(8,128)S(1)}, f32[8,8,256]{2,1,0:T(8,128)S(1)}, u32[]{:S(2)}, u32[]{:S(2)}) collective-permute-start(f32[8,8,256]{2,1,0:T(8,128)S(1)} %get-tuple-element.217.own), channel_id=1, source_target_pairs={{0,248},{1,249},{2,250},{3,251},{4,252},{5,253},{6,254},{7,255},{8... | collective-permute-start | bytes 196616 | tf_op jit(solution)/shard_map/ppermute | solution.py:494
  28.5 1.4 %collective-permute-start.27 = (f32[15,8,256]{2,1,0:T(8,128)S(1)}, f32[15,8,256]{2,1,0:T(8,128)S(1)}, u32[]{:S(2)}, u32[]{:S(2)}) collective-permute-start(f32[15,8,256]{2,1,0:T(8,128)S(1)} %pad_maximum_fusion.11), channel_id=1, source_target_pairs={{0,4},{1,5},{2,6},{3,7},{4,0},{5,1},{6,2},{7,3},{8,12},{9,13},{10,... | collective-permute-start | bytes 368648 | tf_op jit(solution)/shard_map/ppermute | solution.py:494
  30.8 2.2 %collective-permute-start.29 = (f32[7,8,256]{2,1,0:T(8,128)S(1)}, f32[7,8,256]{2,1,0:T(8,128)S(1)}, u32[]{:S(2)}, u32[]{:S(2)}) collective-permute-start(f32[7,8,256]{2,1,0:T(8,128)S(1)} %slice_select_fusion.4), channel_id=1, source_target_pairs={{0,4},{1,5},{2,6},{3,7},{4,0},{5,1},{6,2},{7,3},{8,12},{9,13},{10,... | collective-permute-start | bytes 172040 | tf_op jit(solution)/shard_map/ppermute | solution.py:494
  33.9 2.7 %collective-permute-done.30.chip_b = f32[7,8,256]{2,1,0:T(8,128)S(1)} collective-permute-done((f32[7,8,256]{2,1,0:T(8,128)S(1)}, f32[7,8,256]{2,1,0:T(8,128)S(1)}, u32[]{:S(2)}, u32[]{:S(2)}) %collective-permute-start.30) | collective-permute-done | bytes 57376 | tf_op jit(solution)/shard_map/ppermute | solution.py:494
  36.6 3.1 %shard_map.88 = (f32[256,128]{1,0:T(8,128)}, f32[8,10,2,16,128]{4,3,2,1,0:T(8,128)S(1)}) custom-call(s32[4]{0:T(128)S(1)} %pad_add_fusion.info, f32[2]{0:T(128)S(1)} %add_convert_fusion.flags, f32[8,8,256]{2,1,0:T(8,128)S(1)} %get-tuple-element.217.own, f32[8,8,256]{2,1,0:T(8,128)S(1)} %collective-permute-done.25.inner, ...), custom_call_target="tpu_custom_call" | custom-call | flops 1000000 | bytes 1000000 | tf_op jit(solution)/shard_map/pallas_call | solution.py:455
  39.7 8.1 %all-to-all-start = ((f32[256,1,128]{2,1,0:T(1,128)}), f32[256,1,128]{2,1,0:T(1,128)S(1)}, u32[]{:S(2)}, u32[]{:S(2)}) async-start(f32[256,1,128]{2,1,0:T(1,128)} %bitcast.40), calls=%async_computation | async-start | bytes 262144 | tf_op jit(solution)/shard_map/all_to_all | solution.py:558
  47.8 12.7 %all-to-all-done = f32[256,1,128]{2,1,0:T(1,128)S(1)} async-done(((f32[256,1,128]{2,1,0:T(1,128)}), f32[256,1,128]{2,1,0:T(1,128)S(1)}, u32[]{:S(2)}, u32[]{:S(2)}) %all-to-all-start) | async-done | bytes 131104 | tf_op jit(solution)/shard_map/all_to_all | solution.py:558
  63.9 4.3 %collective-permute-done.31 = f32[3,4,8,256]{3,2,1,0:T(8,128)S(1)} collective-permute-done((f32[3,4,8,256]{3,2,1,0:T(8,128)S(1)}, f32[3,4,8,256]{3,2,1,0:T(8,128)S(1)}, u32[]{:S(2)}, u32[]{:S(2)}) %collective-permute-start.31) | collective-permute-done | bytes 98336 | tf_op jit(solution)/shard_map/ppermute | solution.py:494
  68.3 2.0 %collective-permute-start.35 = (f32[3,4,2,256]{3,2,1,0:T(2,128)S(1)}, f32[3,4,2,256]{3,2,1,0:T(2,128)S(1)}, u32[]{:S(2)}, u32[]{:S(2)}) collective-permute-start(f32[3,4,2,256]{3,2,1,0:T(2,128)S(1)} %bitcast.122), channel_id=1, source_target_pairs={{0,4},{1,5},{2,6},{3,7},{4,0},{5,1},{6,2},{7,3},{8,12},{9,13},{10,... | collective-permute-start | bytes 73736 | tf_op jit(solution)/shard_map/ppermute | solution.py:494
  71.1 2.4 %collective-permute-done.36.chip_b = f32[3,4,2,256]{3,2,1,0:T(2,128)S(1)} collective-permute-done((f32[3,4,2,256]{3,2,1,0:T(2,128)S(1)}, f32[3,4,2,256]{3,2,1,0:T(2,128)S(1)}, u32[]{:S(2)}, u32[]{:S(2)}) %collective-permute-start.36) | collective-permute-done | bytes 24608 | tf_op jit(solution)/shard_map/ppermute | solution.py:494
  75.0 1.8 %collective-permute-start.38 = (f32[8,8,256]{2,1,0:T(8,128)S(1)}, f32[8,8,256]{2,1,0:T(8,128)S(1)}, u32[]{:S(2)}, u32[]{:S(2)}) collective-permute-start(f32[8,8,256]{2,1,0:T(8,128)S(1)} %get-tuple-element.222.own), channel_id=1, source_target_pairs={{0,248},{1,249},{2,250},{3,251},{4,252},{5,253},{6,254},{7,255},{8... | collective-permute-start | bytes 196616 | tf_op jit(solution)/shard_map/ppermute | solution.py:494
  78.1 2.5 %collective-permute-start.39 = (f32[15,8,256]{2,1,0:T(8,128)S(1)}, f32[15,8,256]{2,1,0:T(8,128)S(1)}, u32[]{:S(2)}, u32[]{:S(2)}) collective-permute-start(f32[15,8,256]{2,1,0:T(8,128)S(1)} %pad_maximum_fusion.12), channel_id=1, source_target_pairs={{0,4},{1,5},{2,6},{3,7},{4,0},{5,1},{6,2},{7,3},{8,12},{9,13},{10,... | collective-permute-start | bytes 368648 | tf_op jit(solution)/shard_map/ppermute | solution.py:494
  81.5 2.5 %collective-permute-start.41 = (f32[7,8,256]{2,1,0:T(8,128)S(1)}, f32[7,8,256]{2,1,0:T(8,128)S(1)}, u32[]{:S(2)}, u32[]{:S(2)}) collective-permute-start(f32[7,8,256]{2,1,0:T(8,128)S(1)} %slice_select_fusion.2), channel_id=1, source_target_pairs={{0,4},{1,5},{2,6},{3,7},{4,0},{5,1},{6,2},{7,3},{8,12},{9,13},{10,... | collective-permute-start | bytes 172040 | tf_op jit(solution)/shard_map/ppermute | solution.py:494
  85.0 2.7 %collective-permute-done.42.chip_b = f32[7,8,256]{2,1,0:T(8,128)S(1)} collective-permute-done((f32[7,8,256]{2,1,0:T(8,128)S(1)}, f32[7,8,256]{2,1,0:T(8,128)S(1)}, u32[]{:S(2)}, u32[]{:S(2)}) %collective-permute-start.42) | collective-permute-done | bytes 57376 | tf_op jit(solution)/shard_map/ppermute | solution.py:494
  87.7 3.1 %shard_map.91 = (f32[256,128]{1,0:T(8,128)}, f32[8,10,2,16,128]{4,3,2,1,0:T(8,128)S(1)}) custom-call(s32[4]{0:T(128)S(1)} %pad_add_fusion.info, f32[2]{0:T(128)S(1)} %add_convert_fusion.flags, f32[8,8,256]{2,1,0:T(8,128)S(1)} %get-tuple-element.222.own, f32[8,8,256]{2,1,0:T(8,128)S(1)} %collective-permute-done.37.inner, ...), custom_call_target="tpu_custom_call" | custom-call | flops 1000000 | bytes 1000000 | tf_op jit(solution)/shard_map/pallas_call | solution.py:455
  90.8 6.3 %all-to-all-start.1 = ((f32[256,1,128]{2,1,0:T(1,128)}), f32[256,1,128]{2,1,0:T(1,128)S(1)}, u32[]{:S(2)}, u32[]{:S(2)}) async-start(f32[256,1,128]{2,1,0:T(1,128)} %bitcast.43), calls=%async_computation.1 | async-start | bytes 262144 | tf_op jit(solution)/shard_map/all_to_all | solution.py:558
  97.1 12.8 %all-to-all-done.1 = f32[256,1,128]{2,1,0:T(1,128)S(1)} async-done(((f32[256,1,128]{2,1,0:T(1,128)}), f32[256,1,128]{2,1,0:T(1,128)S(1)}, u32[]{:S(2)}, u32[]{:S(2)}) %all-to-all-start.1) | async-done | bytes 131104 | tf_op jit(solution)/shard_map/all_to_all | solution.py:558
  109.9 1.5 %shard_map.92 = (s32[1]{0:T(128)}, f32[4,4,8,256]{3,2,1,0:T(8,128)S(1)}, f32[4,4,8,256]{3,2,1,0:T(8,128)S(1)}) custom-call(s32[4]{0:T(128)S(1)} %pad_add_fusion.info, f32[256,128]{1,0:T(8,128)S(1)} %bitcast.105, f32[16,128]{1,0:T(8,128)S(1)} %copy-done.3, f32[16,128]{1,0:T(8,128)S(1)} %copy-done.4, f32[8,16,128]{2,1,0:T(8,128)S(1)} %copy-done, ...), custom_call_target="tpu_custom_call" | custom-call | flops 1000000 | bytes 1000000 | tf_op jit(solution)/shard_map/pallas_call | solution.py:455
  112.0 3.3 %conditional.1 = ((f32[3,4,16,256]{3,2,1,0:T(8,128)}, f32[4,16,256]{2,1,0:T(8,128)})) conditional(s32[]{:T(128)} %bitcast.45, (pred[]{:T(512)}, f32[16,8,256]{2,1,0:T(8,128)S(1)}, f32[16,8,256]{2,1,0:T(8,128)S(1)}, s32[2]{0:T(128)S(1)}, f32[8,3]{0,1:T(4,128)S(1)}) %tuple.189, (f32[4,4,8,256]{3,2,1,0:T(8,128)S(1)}, s32[4]{0:T(128)S(1)}, ...), branch_computations={%region_0.9_spmd, %region_9.10_spmd} | conditional | flops 3892455 | bytes 14964919 | solution.py:582
  (100 shorter events, 21.7 us)
Async XLA Ops:
  2.4 12.7 %collective-permute-start.20 = (f32[16,8,256]{2,1,0:T(8,128)S(1)}, f32[16,8,256]{2,1,0:T(8,128)S(1)}, u32[]{:S(2)}, u32[]{:S(2)}) collective-permute-start(f32[16,8,256]{2,1,0:T(8,128)S(1)} %get-tuple-element.216), channel_id=1, source_target_pairs={{0,4},{1,5},{2,6},{3,7},{4,0},{5,1},{6,2},{7,3},{8,12},{9,13},{10,... | collective-permute-start | bytes 393224 | tf_op jit(solution)/shard_map/ppermute | solution.py:494
  5.8 4.1 %collective-permute-start.18 = (f32[13,8,256]{2,1,0:T(8,128)S(1)}, f32[13,8,256]{2,1,0:T(8,128)S(1)}, u32[]{:S(2)}, u32[]{:S(2)}) collective-permute-start(f32[13,8,256]{2,1,0:T(8,128)S(1)} %get-tuple-element.213), channel_id=1, source_target_pairs={{0,252},{1,253},{2,254},{3,255},{4,8},{5,9},{6,10},{7,11},{8,4},{9... | collective-permute-start | bytes 319496 | tf_op jit(solution)/shard_map/ppermute | solution.py:494
  5.8 9.3 %collective-permute-start.19 = (f32[13,8,256]{2,1,0:T(8,128)S(1)}, f32[13,8,256]{2,1,0:T(8,128)S(1)}, u32[]{:S(2)}, u32[]{:S(2)}) collective-permute-start(f32[13,8,256]{2,1,0:T(8,128)S(1)} %get-tuple-element.214), channel_id=1, source_target_pairs={{0,248},{1,249},{2,250},{3,251},{4,12},{5,13},{6,14},{7,15},{8,0},... | collective-permute-start | bytes 319496 | tf_op jit(solution)/shard_map/ppermute | solution.py:494
  15.3 5.2 %collective-permute-start.24 = (f32[4,4,2,256]{3,2,1,0:T(2,128)S(1)}, f32[4,4,2,256]{3,2,1,0:T(2,128)S(1)}, u32[]{:S(2)}, u32[]{:S(2)}) collective-permute-start(f32[4,4,2,256]{3,2,1,0:T(2,128)S(1)} %get-tuple-element.304), channel_id=1, source_target_pairs={{0,7},{1,4},{2,5},{3,6},{4,1},{5,2},{6,3},{7,0},{8,15},{9,12},{10,... | collective-permute-start | bytes 98312 | tf_op jit(solution)/shard_map/ppermute | solution.py:494
  18.6 4.1 %collective-permute-start.22 = (f32[4,8,2,256]{3,2,1,0:T(2,128)S(1)}, f32[4,8,2,256]{3,2,1,0:T(2,128)S(1)}, u32[]{:S(2)}, u32[]{:S(2)}) collective-permute-start(f32[4,8,2,256]{3,2,1,0:T(2,128)S(1)} %get-tuple-element.307), channel_id=1, source_target_pairs={{0,7},{1,4},{2,5},{3,6},{4,1},{5,2},{6,3},{7,0},{8,15},{9,12},{10,... | collective-permute-start | bytes 196616 | tf_op jit(solution)/shard_map/ppermute | solution.py:494
  24.1 4.4 %collective-permute-start.25 = (f32[8,8,256]{2,1,0:T(8,128)S(1)}, f32[8,8,256]{2,1,0:T(8,128)S(1)}, u32[]{:S(2)}, u32[]{:S(2)}) collective-permute-start(f32[8,8,256]{2,1,0:T(8,128)S(1)} %get-tuple-element.217.own), channel_id=1, source_target_pairs={{0,8},{1,9},{2,10},{3,11},{4,12},{5,13},{6,14},{7,15},{8,0},{9,1},... | collective-permute-start | bytes 196616 | tf_op jit(solution)/shard_map/ppermute | solution.py:494
  24.2 6.5 %collective-permute-start.26 = (f32[8,8,256]{2,1,0:T(8,128)S(1)}, f32[8,8,256]{2,1,0:T(8,128)S(1)}, u32[]{:S(2)}, u32[]{:S(2)}) collective-permute-start(f32[8,8,256]{2,1,0:T(8,128)S(1)} %get-tuple-element.217.own), channel_id=1, source_target_pairs={{0,248},{1,249},{2,250},{3,251},{4,252},{5,253},{6,254},{7,255},{8... | collective-permute-start | bytes 196616 | tf_op jit(solution)/shard_map/ppermute | solution.py:494
  28.5 8.1 %collective-permute-start.27 = (f32[15,8,256]{2,1,0:T(8,128)S(1)}, f32[15,8,256]{2,1,0:T(8,128)S(1)}, u32[]{:S(2)}, u32[]{:S(2)}) collective-permute-start(f32[15,8,256]{2,1,0:T(8,128)S(1)} %pad_maximum_fusion.11), channel_id=1, source_target_pairs={{0,4},{1,5},{2,6},{3,7},{4,0},{5,1},{6,2},{7,3},{8,12},{9,13},{10,... | collective-permute-start | bytes 368648 | tf_op jit(solution)/shard_map/ppermute | solution.py:494
  29.9 6.7 %collective-permute-start.28 = (f32[15,8,256]{2,1,0:T(8,128)S(1)}, f32[15,8,256]{2,1,0:T(8,128)S(1)}, u32[]{:S(2)}, u32[]{:S(2)}) collective-permute-start(f32[15,8,256]{2,1,0:T(8,128)S(1)} %pad_maximum_fusion.11), channel_id=1, source_target_pairs={{0,7},{1,4},{2,5},{3,6},{4,1},{5,2},{6,3},{7,0},{8,15},{9,12},{10,... | collective-permute-start | bytes 368648 | tf_op jit(solution)/shard_map/ppermute | solution.py:494
  30.8 3.1 %collective-permute-start.29 = (f32[7,8,256]{2,1,0:T(8,128)S(1)}, f32[7,8,256]{2,1,0:T(8,128)S(1)}, u32[]{:S(2)}, u32[]{:S(2)}) collective-permute-start(f32[7,8,256]{2,1,0:T(8,128)S(1)} %slice_select_fusion.4), channel_id=1, source_target_pairs={{0,4},{1,5},{2,6},{3,7},{4,0},{5,1},{6,2},{7,3},{8,12},{9,13},{10,... | collective-permute-start | bytes 172040 | tf_op jit(solution)/shard_map/ppermute | solution.py:494
  33.0 3.6 %collective-permute-start.30 = (f32[7,8,256]{2,1,0:T(8,128)S(1)}, f32[7,8,256]{2,1,0:T(8,128)S(1)}, u32[]{:S(2)}, u32[]{:S(2)}) collective-permute-start(f32[7,8,256]{2,1,0:T(8,128)S(1)} %slice_select_fusion.4), channel_id=1, source_target_pairs={{0,7},{1,4},{2,5},{3,6},{4,1},{5,2},{6,3},{7,0},{8,15},{9,12},{10,... | collective-permute-start | bytes 172040 | tf_op jit(solution)/shard_map/ppermute | solution.py:494
  39.7 20.8 %all-to-all-start = ((f32[256,1,128]{2,1,0:T(1,128)}), f32[256,1,128]{2,1,0:T(1,128)S(1)}, u32[]{:S(2)}, u32[]{:S(2)}) async-start(f32[256,1,128]{2,1,0:T(1,128)} %bitcast.40), calls=%async_computation | async-start | bytes 262144 | tf_op jit(solution)/shard_map/all_to_all | solution.py:558
  61.0 7.2 %collective-permute-start.31 = (f32[3,4,8,256]{3,2,1,0:T(8,128)S(1)}, f32[3,4,8,256]{3,2,1,0:T(8,128)S(1)}, u32[]{:S(2)}, u32[]{:S(2)}) collective-permute-start(f32[3,4,8,256]{3,2,1,0:T(8,128)S(1)} %get-tuple-element.380), channel_id=1, source_target_pairs={{0,248},{1,249},{2,250},{3,251},{4,252},{5,253},{6,254},{7,255},{8... | collective-permute-start | bytes 294920 | tf_op jit(solution)/shard_map/ppermute | solution.py:494
  61.9 6.2 %collective-permute-start.32 = (f32[3,4,8,256]{3,2,1,0:T(8,128)S(1)}, f32[3,4,8,256]{3,2,1,0:T(8,128)S(1)}, u32[]{:S(2)}, u32[]{:S(2)}) collective-permute-start(f32[3,4,8,256]{3,2,1,0:T(8,128)S(1)} %get-tuple-element.379), channel_id=1, source_target_pairs={{0,8},{1,9},{2,10},{3,11},{4,12},{5,13},{6,14},{7,15},{8,0},{9,1},... | collective-permute-start | bytes 294920 | tf_op jit(solution)/shard_map/ppermute | solution.py:494
  62.4 8.0 %collective-permute-start.33 = (f32[3,8,2,256]{3,2,1,0:T(2,128)S(1)}, f32[3,8,2,256]{3,2,1,0:T(2,128)S(1)}, u32[]{:S(2)}, u32[]{:S(2)}) collective-permute-start(f32[3,8,2,256]{3,2,1,0:T(2,128)S(1)} %get-tuple-element.376), channel_id=1, source_target_pairs={{0,4},{1,5},{2,6},{3,7},{4,0},{5,1},{6,2},{7,3},{8,12},{9,13},{10,... | collective-permute-start | bytes 147464 | tf_op jit(solution)/shard_map/ppermute | solution.py:494
  63.5 6.9 %collective-permute-start.34 = (f32[3,8,2,256]{3,2,1,0:T(2,128)S(1)}, f32[3,8,2,256]{3,2,1,0:T(2,128)S(1)}, u32[]{:S(2)}, u32[]{:S(2)}) collective-permute-start(f32[3,8,2,256]{3,2,1,0:T(2,128)S(1)} %get-tuple-element.375), channel_id=1, source_target_pairs={{0,7},{1,4},{2,5},{3,6},{4,1},{5,2},{6,3},{7,0},{8,15},{9,12},{10,... | collective-permute-start | bytes 147464 | tf_op jit(solution)/shard_map/ppermute | solution.py:494
  70.2 3.3 %collective-permute-start.36 = (f32[3,4,2,256]{3,2,1,0:T(2,128)S(1)}, f32[3,4,2,256]{3,2,1,0:T(2,128)S(1)}, u32[]{:S(2)}, u32[]{:S(2)}) collective-permute-start(f32[3,4,2,256]{3,2,1,0:T(2,128)S(1)} %get-tuple-element.301), channel_id=1, source_target_pairs={{0,7},{1,4},{2,5},{3,6},{4,1},{5,2},{6,3},{7,0},{8,15},{9,12},{10,... | collective-permute-start | bytes 73736 | tf_op jit(solution)/shard_map/ppermute | solution.py:494
  74.9 3.2 %collective-permute-start.37 = (f32[8,8,256]{2,1,0:T(8,128)S(1)}, f32[8,8,256]{2,1,0:T(8,128)S(1)}, u32[]{:S(2)}, u32[]{:S(2)}) collective-permute-start(f32[8,8,256]{2,1,0:T(8,128)S(1)} %get-tuple-element.222.own), channel_id=1, source_target_pairs={{0,8},{1,9},{2,10},{3,11},{4,12},{5,13},{6,14},{7,15},{8,0},{9,1},... | collective-permute-start | bytes 196616 | tf_op jit(solution)/shard_map/ppermute | solution.py:494
  75.0 6.5 %collective-permute-start.38 = (f32[8,8,256]{2,1,0:T(8,128)S(1)}, f32[8,8,256]{2,1,0:T(8,128)S(1)}, u32[]{:S(2)}, u32[]{:S(2)}) collective-permute-start(f32[8,8,256]{2,1,0:T(8,128)S(1)} %get-tuple-element.222.own), channel_id=1, source_target_pairs={{0,248},{1,249},{2,250},{3,251},{4,252},{5,253},{6,254},{7,255},{8... | collective-permute-start | bytes 196616 | tf_op jit(solution)/shard_map/ppermute | solution.py:494
  78.1 9.6 %collective-permute-start.39 = (f32[15,8,256]{2,1,0:T(8,128)S(1)}, f32[15,8,256]{2,1,0:T(8,128)S(1)}, u32[]{:S(2)}, u32[]{:S(2)}) collective-permute-start(f32[15,8,256]{2,1,0:T(8,128)S(1)} %pad_maximum_fusion.12), channel_id=1, source_target_pairs={{0,4},{1,5},{2,6},{3,7},{4,0},{5,1},{6,2},{7,3},{8,12},{9,13},{10,... | collective-permute-start | bytes 368648 | tf_op jit(solution)/shard_map/ppermute | solution.py:494
  80.6 7.0 %collective-permute-start.40 = (f32[15,8,256]{2,1,0:T(8,128)S(1)}, f32[15,8,256]{2,1,0:T(8,128)S(1)}, u32[]{:S(2)}, u32[]{:S(2)}) collective-permute-start(f32[15,8,256]{2,1,0:T(8,128)S(1)} %pad_maximum_fusion.12), channel_id=1, source_target_pairs={{0,7},{1,4},{2,5},{3,6},{4,1},{5,2},{6,3},{7,0},{8,15},{9,12},{10,... | collective-permute-start | bytes 368648 | tf_op jit(solution)/shard_map/ppermute | solution.py:494
  81.5 3.4 %collective-permute-start.41 = (f32[7,8,256]{2,1,0:T(8,128)S(1)}, f32[7,8,256]{2,1,0:T(8,128)S(1)}, u32[]{:S(2)}, u32[]{:S(2)}) collective-permute-start(f32[7,8,256]{2,1,0:T(8,128)S(1)} %slice_select_fusion.2), channel_id=1, source_target_pairs={{0,4},{1,5},{2,6},{3,7},{4,0},{5,1},{6,2},{7,3},{8,12},{9,13},{10,... | collective-permute-start | bytes 172040 | tf_op jit(solution)/shard_map/ppermute | solution.py:494
  84.1 3.6 %collective-permute-start.42 = (f32[7,8,256]{2,1,0:T(8,128)S(1)}, f32[7,8,256]{2,1,0:T(8,128)S(1)}, u32[]{:S(2)}, u32[]{:S(2)}) collective-permute-start(f32[7,8,256]{2,1,0:T(8,128)S(1)} %slice_select_fusion.2), channel_id=1, source_target_pairs={{0,7},{1,4},{2,5},{3,6},{4,1},{5,2},{6,3},{7,0},{8,15},{9,12},{10,... | collective-permute-start | bytes 172040 | tf_op jit(solution)/shard_map/ppermute | solution.py:494
  90.8 19.1 %all-to-all-start.1 = ((f32[256,1,128]{2,1,0:T(1,128)}), f32[256,1,128]{2,1,0:T(1,128)S(1)}, u32[]{:S(2)}, u32[]{:S(2)}) async-start(f32[256,1,128]{2,1,0:T(1,128)} %bitcast.43), calls=%async_computation.1 | async-start | bytes 262144 | tf_op jit(solution)/shard_map/all_to_all | solution.py:558
  (11 other events, 198.0 us)
